TPU v7x, 32 devices: a whole 2x2x4 slice. The times are simulated.
32 devices in a mesh: row: 4 (over z), blk: 8 (over y, x, core).
Axes of the slice: x: 2, y: 2, z: 4, core: 2. Of those that a mesh axis runs over, the one named last changes fastest.
Arguments:
- tokens: bfloat16 [16, 1024, 768], P('row', 'blk'), may hold values from -6 to 6
- lengths: int32 [16, 8], P('row'), may hold values from 20 to 884, as said below
- norm_gain: bfloat16 [768], P('blk'), may hold values from 0.5 to 1.5
- qkv_weight: bfloat16 [768, 2304], P('blk', 'row'), may hold values from -0.21875 to 0.21875
- out_weight: bfloat16 [768, 768], P('blk', 'row'), may hold values from -6 to 6
- mlp_gain: bfloat16 [768], P('blk'), may hold values from 0.5 to 1.5
- in_weight: bfloat16 [768, 2304], P('blk', 'row'), may hold values from -0.21875 to 0.21875
- down_weight: bfloat16 [1152, 768], P('blk', 'row'), may hold values from -0.1875 to 0.1875
- cotangent: bfloat16 [16, 1024, 768], P('row', 'blk'), may hold values from -6 to 6
Outputs:
- output: bfloat16 [16, 1024, 768], P('row', 'blk')
- input_grad: bfloat16 [16, 1024, 768], P('row', 'blk')
- norm_gain_grad: float32 [768], P('blk')
- qkv_grad: float32 [768, 2304], P('blk', 'row')
- out_grad: float32 [768, 768], P('blk', 'row')
- mlp_gain_grad: float32 [768], P('blk')
- in_grad: float32 [768, 2304], P('blk', 'row')
- down_grad: float32 [1152, 768], P('blk', 'row')
Inputs may be any that keep to these rules, and one draw needn't show every extreme that they name: Each packed row holds 8 positive document lengths that sum to 1024.
All inputs are finite; a program needn't handle non-finite values.
Results may differ from a plain program's by a relative error of at most 0.03.
Values may be sent and summed in bfloat16 or wider, within the bound.
No kernel may reach another device: no remote copies, remote signals or barrier semaphores. Data moves between devices by JAX's collectives and lax.ppermute only.
A program may use at most 256 MiB of HBM per device.

v0:
```python
import functools
import math

import jax
import jax.numpy as jnp
import numpy as np
from jax import lax
from jax.experimental import pallas as pl
from jax.experimental.pallas import tpu as pltpu
from jax.sharding import PartitionSpec as P

D = 768
HEADS = 12
HD = 64
FF = 1152
NDOC = 8
PAIRS = HEADS // 2
EXT = 3 * D + 128

ROPE_BASE = 160000.0
NORM_EPSILON = 1e-05
MASKED = -1e30
F32 = jnp.float32
BF16 = jnp.bfloat16
NN = (((1,), (0,)), ((), ()))
NT = (((1,), (1,)), ((), ()))
TN = (((0,), (0,)), ((), ()))
VMEM_BYTES = 40 * 1024 * 1024
HALVES = 2
HALF_PAIRS = PAIRS // HALVES
HALF = D // HALVES
BACK_PARTS = ((0, 0, 1), (0, 1, 2), (1, 0, 3))
COSTS = {
    "prepare": 4,
    "place_rows": 2,
    "join_qkv": 2,
    "join_rest": 2,
    "project": 7,
    "attend": 9,
    "middle": 20,
    "attend_back": 12,
    "back_in": 7,
    "back_weight": 6,
    "cut_qkv": 2,
    "cut_rest": 2,
    "end_rest": 2,
    "end_qkv": 2,
}
SMEM = pl.BlockSpec(memory_space=pltpu.SMEM)
ANY = pl.BlockSpec(memory_space=pl.ANY)
VMEM = pl.BlockSpec(memory_space=pltpu.VMEM)


def dot(a, b, dims):
    return lax.dot_general(a, b, dims, preferred_element_type=F32)


def shape_of(dims, dtype):
    return jax.ShapeDtypeStruct(tuple(dims), dtype)


def params():
    return pltpu.CompilerParams(vmem_limit_bytes=VMEM_BYTES)


def cost(microseconds):
    return pl.CostEstimate(
        flops=int(microseconds * 1e6), bytes_accessed=1 << 10, transcendentals=0
    )


def tie(value, *others):
    return lax.optimization_barrier((value, *others))[0]


class Plan:
    def __init__(self, mesh, rows, tok):
        self.nrow = mesh.shape["row"]
        self.nblk = mesh.shape["blk"]
        self.rows = rows
        self.tok = tok
        self.local = rows * tok
        self.chips = self.nblk // 2
        self.bits = self.chips.bit_length() - 1
        self.groups = self.nblk // rows
        self.r = D // self.nblk
        self.rf = FF // self.nblk
        self.cw = D // self.nrow
        self.aligned = self.r % 16 == 0 and self.rf % 16 == 0
        self.packed = 4 * self.r + self.rf
        rows_, chips, nrow = self.rows, self.chips, self.nrow
        self.at_pick = 0
        self.at_base = self.at_pick + rows_
        self.at_own = self.at_base + self.groups * rows_
        self.at_other = self.at_own + chips
        self.at_z = self.at_other + chips
        self.at_lo = self.at_z + nrow
        self.size = self.at_lo + 1
        table = np.zeros((nrow, self.nblk, self.size), np.int32)
        for z in range(nrow):
            for blk in range(self.nblk):
                chip, core = blk // 2, blk % 2
                low = chip % rows_
                entry = table[z, blk]
                for j in range(rows_):
                    entry[self.at_pick + j] = low ^ j
                for e in range(self.groups):
                    other = blk ^ self.member(e)
                    for j in range(rows_):
                        entry[self.at_base + e * rows_ + j] = (2 * ((other // 2) ^ j) + other % 2) * tok
                for j in range(chips):
                    entry[self.at_own + j] = 2 * (chip ^ self.order(core, j)) + core
                    entry[self.at_other + j] = 2 * (chip ^ self.order(1 - core, j)) + 1 - core
                for other in range(nrow):
                    entry[self.at_z + other] = other ^ z
                entry[self.at_lo] = low
        self.table = table

    def member(self, e):
        return (e & 1) | ((e >> 1) * 2 * self.rows)

    def order(self, core, j):
        if core == 0:
            return j
        return int(format(j, "0%db" % self.bits)[::-1], 2) if self.bits else 0

    def step_pairs(self, step):
        def flip(blk):
            bit = step if blk % 2 == 0 else self.bits - 1 - step
            return 2 * ((blk // 2) ^ (1 << bit)) + blk % 2

        return [(blk, flip(blk)) for blk in range(self.nblk)]

    def xor_pairs(self, mask):
        return [(blk, blk ^ mask) for blk in range(self.nblk)]

    def z_pairs(self, mask):
        return [(z, z ^ mask) for z in range(self.nrow)]


def swap_cores(plan, value):
    return lax.ppermute(value, "blk", plan.xor_pairs(1))


def gather_z(plan, value, behind=None):
    pieces = [value]
    for j in range(1, plan.nrow):
        source = value if behind is None else tie(value, behind[j])
        pieces.append(lax.ppermute(source, "row", plan.z_pairs(j)))
    return pieces


def exchange_rows(plan, pieces):
    return [pieces[0]] + [
        lax.ppermute(pieces[j], "blk", plan.xor_pairs(2 * j)) for j in range(1, plan.rows)
    ]


def gather_start(plan, value, behind=()):
    pairs = [plan.step_pairs(step) for step in range(plan.bits)]
    first = lax.ppermute(value, "blk", pairs[0])
    second = [lax.ppermute(tie(value, *behind), "blk", pairs[1])] if plan.bits > 1 else []
    return [value, first] + second


def gather_more(plan, pieces):
    for step in range(1, plan.bits):
        have = 1 << step
        missing = pieces[len(pieces) - have :] if step > 1 else pieces[1:2]
        pieces = pieces + [lax.ppermute(piece, "blk", plan.step_pairs(step)) for piece in missing]
    return pieces


def add_low(a, b):
    return (a.astype(F32) + b.astype(F32)).astype(BF16)


def reduce_start(plan, grads):
    keep_low, keep_high, send_low, send_high = grads
    other_high = swap_cores(plan, send_high)
    return keep_low, keep_high, swap_cores(plan, send_low), other_high


def reduce_step(plan, step, low, high):
    moved = lax.ppermute(high, "blk", plan.step_pairs(step))
    half = low.shape[0] // 2
    if half == 0:
        return add_low(low, moved)[0], None
    high = add_low(low[half:], moved[half:])
    return add_low(low[:half], moved[:half]), high


def layer_norm(values):
    average = jnp.mean(values, axis=-1, keepdims=True)
    centred = values - average
    inv_std = lax.rsqrt(jnp.mean(centred * centred, axis=-1, keepdims=True) + NORM_EPSILON)
    return centred * inv_std, inv_std


def norm_backward(grad_out, normalized, inv_std, gain):
    scaled = grad_out * gain
    inner = jnp.mean(scaled * normalized, axis=-1, keepdims=True)
    outer = jnp.mean(scaled, axis=-1, keepdims=True)
    return inv_std * (scaled - outer - normalized * inner)


def swap_halves(values):
    lane = lax.broadcasted_iota(jnp.int32, values.shape, 1)
    width = values.shape[1]
    half = HD // 2
    return jnp.where(
        (lane & half) == 0, pltpu.roll(values, width - half, 1), pltpu.roll(values, half, 1)
    )


def rotate_pair(values, cosine, sine, direction):
    return values * cosine + swap_halves(values) * (direction * sine)


def rotate_all(values, cosine, sine, direction):
    return jnp.concatenate(
        [
            rotate_pair(values[:, 128 * p : 128 * (p + 1)], cosine, sine, direction)
            for p in range(values.shape[1] // 128)
        ],
        axis=1,
    )


def prepare_kernel(plan, meta, tokens, cotangent, w_out, w_in, w_down, *refs):
    rows = plan.rows
    for j in range(rows):
        row = meta[plan.at_pick + j]
        refs[j][0] = tokens[row]
        refs[j][1] = cotangent[row]
    if plan.aligned:
        refs[rows][...] = pack_rest(plan, w_out[...], w_in[...], w_down[...])


def prepare(plan, meta, tokens, cotangent, w_out, w_in, w_down):
    rows = plan.rows
    shapes = [shape_of((2, plan.tok, D), BF16)] * rows
    if plan.aligned:
        shapes.append(shape_of((3 * plan.r, 2 * plan.cw), BF16))
    results = pl.pallas_call(
        functools.partial(prepare_kernel, plan),
        in_specs=[SMEM] + [VMEM] * 5,
        out_specs=[VMEM] * len(shapes),
        out_shape=shapes,
        compiler_params=params(),
        cost_estimate=cost(COSTS["prepare"]),
        name="prepare",
    )(meta, tokens, cotangent, w_out, w_in, w_down)
    packed = results[rows] if plan.aligned else pack_rest(plan, w_out, w_in, w_down)
    return results[:rows], packed


def place_kernel(plan, meta, *refs):
    pieces, (out, grad) = refs[: plan.rows], refs[plan.rows :]
    for j in range(plan.rows):
        row = meta[plan.at_pick + j]
        out[row] = pieces[j][0]
        grad[row] = pieces[j][1]


def place(plan, meta, pieces):
    return pl.pallas_call(
        functools.partial(place_kernel, plan),
        in_specs=[SMEM] + [VMEM] * plan.rows,
        out_specs=[VMEM] * 2,
        out_shape=[shape_of((plan.rows, plan.tok, D), BF16)] * 2,
        compiler_params=params(),
        cost_estimate=cost(COSTS["place_rows"]),
        name="place_rows",
    )(meta, *pieces)


def ordered(plan, meta, pieces):
    stacked = jnp.stack(pieces)
    return [
        lax.dynamic_index_in_dim(stacked, meta[plan.at_z + z], 0, keepdims=False)
        for z in range(plan.nrow)
    ]


def join_qkv_kernel(plan, meta, gains, *refs):
    pieces, out, held = refs[: plan.nrow], refs[plan.nrow], refs[plan.nrow + 1]
    width = 3 * plan.cw
    for j in range(plan.nrow):
        held[j] = pieces[j][...]
    for z in range(plan.nrow):
        out[:, width * z : width * (z + 1)] = held[meta[plan.at_z + z]]
    out[:, 3 * D :] = gains[...]


def join_qkv(plan, meta, gains, pieces):
    if not plan.aligned:
        return jnp.concatenate(ordered(plan, meta, pieces) + [gains], axis=1)
    return pl.pallas_call(
        functools.partial(join_qkv_kernel, plan),
        in_specs=[SMEM] + [VMEM] * (1 + plan.nrow),
        out_specs=VMEM,
        out_shape=shape_of((plan.r, EXT), BF16),
        scratch_shapes=[pltpu.VMEM((plan.nrow, plan.r, 3 * plan.cw), BF16)],
        compiler_params=params(),
        cost_estimate=cost(COSTS["join_qkv"]),
        name="join_qkv",
    )(meta, gains, *pieces)


def pack_rest(plan, w_out, w_in, w_down, blank=None):
    cw = plan.cw
    left = jnp.concatenate([w_in[:, :cw], w_in[:, cw : 2 * cw], w_out], axis=0)
    if blank is None:
        blank = jnp.zeros((2 * plan.r - plan.rf, cw), BF16)
    right = jnp.concatenate([w_in[:, 2 * cw :], w_down, blank], axis=0)
    return jnp.concatenate([left, right], axis=1)


def unpack_rest(plan, piece):
    r, rf, cw = plan.r, plan.rf, plan.cw
    parts_in = [piece[:r, :cw], piece[r : 2 * r, :cw], piece[:r, cw:]]
    return parts_in, piece[2 * r : 3 * r, :cw], piece[r : r + rf, cw:]


def join_rest_kernel(plan, meta, *refs):
    pieces, out, held = refs[: plan.nrow], refs[plan.nrow], refs[plan.nrow + 1]
    r, cw = plan.r, plan.cw
    for j in range(plan.nrow):
        held[j] = pieces[j][...]
    for z in range(plan.nrow):
        parts_in, part_out, part_down = unpack_rest(plan, held[meta[plan.at_z + z]])
        out[:r, cw * z : cw * (z + 1)] = part_out
        for i in range(3):
            block, place_at = (3 * z + i) // plan.nrow, (3 * z + i) % plan.nrow
            out[r * (1 + block) : r * (2 + block), cw * place_at : cw * (place_at + 1)] = parts_in[i]
        out[4 * r :, cw * z : cw * (z + 1)] = part_down


def join_rest(plan, meta, pieces):
    if not plan.aligned:
        parts = [unpack_rest(plan, piece) for piece in ordered(plan, meta, pieces)]
        w_in = jnp.concatenate([part for item in parts for part in item[0]], axis=1)
        blocks = [jnp.concatenate([item[1] for item in parts], axis=1)]
        blocks += [w_in[:, D * t : D * (t + 1)] for t in range(3)]
        blocks += [jnp.concatenate([item[2] for item in parts], axis=1)]
        return jnp.concatenate(blocks, axis=0)
    return pl.pallas_call(
        functools.partial(join_rest_kernel, plan),
        in_specs=[SMEM] + [VMEM] * plan.nrow,
        out_specs=VMEM,
        out_shape=shape_of((plan.packed, D), BF16),
        scratch_shapes=[pltpu.VMEM((plan.nrow, 3 * plan.r, 2 * plan.cw), BF16)],
        compiler_params=params(),
        cost_estimate=cost(COSTS["join_rest"]),
        name="join_rest",
    )(meta, *pieces)


def by_block(plan, meta, own, other):
    stacked = jnp.stack(own + other)
    places = meta[plan.at_own : plan.at_other + plan.chips]
    return jnp.zeros_like(stacked).at[places].set(stacked)


def split_blocks(plan, meta, blocks):
    half = plan.chips // 2
    return [
        jnp.take(blocks, meta[plan.at_own + half * i : plan.at_own + half * (i + 1)], axis=0)
        for i in range(4)
    ]


def qkv_sources(plan, meta, own, other):
    if plan.aligned:
        return own + other
    return [by_block(plan, meta, own, other).reshape(D, EXT)]


def rest_sources(plan, meta, own, other):
    if plan.aligned:
        return own + other
    blocks = by_block(plan, meta, own, other)
    r = plan.r
    parts = [blocks[:, r * i : r * (i + 1)].reshape(D, D) for i in range(4)]
    parts.append(blocks[:, 4 * r :].reshape(FF, D))
    return [jnp.concatenate(parts, axis=0)]


def block_size(plan):
    return (plan.r, plan.rf) if plan.aligned else (D, FF)


def block_of(plan, meta, index):
    return meta[plan.at_own + index] if plan.aligned else 0


def rows_at(index, size):
    if isinstance(index, int):
        return pl.ds(index * size, size)
    return pl.ds(pl.multiple_of(index * size, size), size)


class Mover:
    def __init__(self, sems):
        self.sems = sems
        self.used = 0
        self.open = []

    def start(self, source, target):
        copy = pltpu.make_async_copy(source, target, self.sems.at[self.used])
        self.used += 1
        copy.start()
        return copy

    def send(self, source, target):
        self.open.append(self.start(source, target))

    def finish(self):
        for copy in self.open:
            copy.wait()


def wait_all(copies):
    for copy in copies:
        copy.wait()


def qkv_copies(plan, meta, sources, w_ref, sems):
    r, _ = block_size(plan)
    return [
        pltpu.make_async_copy(source, w_ref.at[rows_at(block_of(plan, meta, i), r)], sems.at[i])
        for i, source in enumerate(sources)
    ]


def grad_target(plan, grads, index):
    if not plan.aligned:
        return grads[0]
    half = plan.chips // 2
    return grads[index // half].at[index % half]


def grad_blocks(plan, height, width):
    return [shape_of((plan.chips // 2, height, width), BF16)] * 4


def source_count(plan):
    return 2 * plan.chips if plan.aligned else 1


def qkv_kernel(plan, meta, cos_ref, sin_ref, *refs):
    x_refs = refs[: plan.rows]
    count = source_count(plan)
    sources = refs[plan.rows : plan.rows + count]
    q_ref = refs[plan.rows + count]
    kv_refs = refs[plan.rows + count + 1 : plan.rows + count + 1 + HALVES]
    n_ref, gain_ref, w_ref, sems = refs[plan.rows + count + 1 + HALVES :]
    copies = qkv_copies(plan, meta, sources, w_ref, sems)
    for copy in copies:
        copy.start()
    units = [layer_norm(x_refs[j][0].astype(F32))[0] for j in range(plan.rows)]
    for copy in copies:
        copy.wait()
    gain_ref[...] = w_ref[:, 3 * D :].astype(F32).T[:8, :]
    for j in range(plan.rows):
        n_ref[plan.tok * j : plan.tok * (j + 1), :] = (units[j] * gain_ref[0:1, :]).astype(BF16)
    cosine, sine = cos_ref[...], sin_ref[...]
    normed = n_ref[...]
    queries = dot(normed, w_ref[:, :D], NN)
    q_ref[...] = rotate_all(queries, cosine, sine, 1.0).astype(BF16)
    keys = rotate_all(dot(normed, w_ref[:, D : 2 * D], NN), cosine, sine, 1.0).astype(BF16)
    values = dot(normed, w_ref[:, 2 * D : 3 * D], NN).astype(BF16)
    for h in range(HALVES):
        kv_refs[h][0] = keys[:, HALF * h : HALF * (h + 1)]
        kv_refs[h][1] = values[:, HALF * h : HALF * (h + 1)]


def project(plan, meta, cosine, sine, pieces, sources):
    local = plan.local
    count = len(sources)
    inputs = [meta, cosine, sine, *pieces, *sources]
    return pl.pallas_call(
        functools.partial(qkv_kernel, plan),
        in_specs=[SMEM, VMEM, VMEM] + [VMEM] * plan.rows + [ANY] * count,
        out_specs=[VMEM] * (3 + HALVES),
        out_shape=[shape_of((local, D), BF16)]
        + [shape_of((2, local, HALF), BF16)] * HALVES
        + [shape_of((local, D), BF16), shape_of((8, D), F32)],
        scratch_shapes=[pltpu.VMEM((D, EXT), BF16), pltpu.SemaphoreType.DMA((count,))],
        compiler_params=params(),
        cost_estimate=cost(COSTS["project"]),
        name="project",
    )(*inputs)


def fill_docs(plan, meta, lengths, kmask, qmask):
    low = meta[plan.at_lo]
    ends = []
    passed = jnp.int32(0)
    for n in range(NDOC):
        passed = passed + lengths[low, n]
        ends.append(passed)

    tok = plan.tok
    lane = lax.broadcasted_iota(jnp.int32, (tok, 128), 1) & (HD - 1)
    for i in range(plan.groups * plan.rows):
        places = meta[plan.at_base + i] + lax.broadcasted_iota(jnp.int32, (tok, 128), 0)
        docs = jnp.zeros((tok, 128), jnp.int32)
        for end in ends:
            docs = docs + (places >= end).astype(jnp.int32)
        part = slice(i * tok, (i + 1) * tok)
        same = docs == lane
        kmask[part, :] = jnp.where((lane < NDOC) & ~same, MASKED, 0.0).astype(BF16)
        if i < plan.rows:
            qmask[part, :] = jnp.where(same, 1.0, 0.0).astype(BF16)


def masks(plan, meta, lengths):
    keys = plan.groups * plan.local
    return pl.pallas_call(
        functools.partial(fill_docs, plan),
        in_specs=[SMEM, SMEM],
        out_specs=[VMEM, VMEM],
        out_shape=[shape_of((keys, 128), BF16), shape_of((plan.local, 128), BF16)],
        compiler_params=params(),
        cost_estimate=cost(1),
        name="masks",
    )(meta, lengths)


def head_part(pair, head, other=None):
    lane = lax.broadcasted_iota(jnp.int32, pair.shape, 1)
    keep = (lane < HD) if head == 0 else (lane >= HD)
    return jnp.where(keep, pair, jnp.zeros_like(pair) if other is None else other)


def attend_kernel(plan, width, order, kmask, qmask, q_ref, *refs):
    groups, local = plan.groups, plan.local
    kv = refs[:groups]
    o_ref, low_ref, lse_ref, s_ref, p_ref = refs[groups:]
    total_keys = groups * local
    chunk = 128
    values_t = []
    row = lax.broadcasted_iota(jnp.int32, (HD + 8, total_keys), 0)
    pair_t = jnp.concatenate([kv[e][1].T for e in range(groups)], axis=1)
    for h in range(2):
        head = pair_t[h * HD : (h + 1) * HD, :]
        values_t.append(jnp.concatenate([head, jnp.ones((8, total_keys), BF16)], axis=0))
    for first in range(0, local, width):
        rows = slice(first, first + width)
        queries = q_ref[rows, :] * jnp.asarray(1.0 / math.sqrt(HD), BF16)
        tops = []
        for h in range(2):
            head_queries = head_part(queries, h, qmask[rows, :])
            top = jnp.full((8, width), MASKED, F32)
            for e in range(groups):
                for c in range(0, local, 2 * chunk):
                    part = slice(e * local + c, e * local + c + 2 * chunk)
                    keys = head_part(kv[e][0, c : c + 2 * chunk, :], h, kmask[part, :])
                    scores = dot(keys, head_queries, NT)
                    s_ref[h, part, :] = scores
                    top = jnp.maximum(top, jnp.max(scores.reshape(-1, 8, width), axis=0))
            tops.append(jnp.max(top, axis=0, keepdims=True))
        parts = []
        for h in range(2):
            for c in range(0, total_keys, chunk):
                part = slice(c, c + chunk)
                p_ref[h, part, :] = jnp.exp(s_ref[h, part, :] - tops[h]).astype(BF16)
            weighted = dot(values_t[h], p_ref[h], NN)
            total = weighted[HD : HD + 1, :]
            parts.append(weighted[:HD, :] / total)
            lse_ref[0, h : h + 1, rows] = tops[h] + jnp.log(total)
        heads = jnp.concatenate(parts, axis=0).T
        o_ref[rows, :] = heads
        low_ref[rows, :] = heads.astype(BF16)


def attend(plan, part, meta, mask, queries, kv):
    local, groups = plan.local, plan.groups
    width = min(512, local)
    skip = part * HALF_PAIRS
    pair = pl.BlockSpec((local, 128), lambda p: (0, p))
    pair_q = pl.BlockSpec((local, 128), lambda p: (0, p + skip))
    pair_kv = pl.BlockSpec((2, local, 128), lambda p: (0, 0, p))
    whole_k = pl.BlockSpec((groups * local, 128), lambda p: (0, 0))
    whole_q = pl.BlockSpec((local, 128), lambda p: (0, 0))
    inputs = [meta, *mask, queries, *kv]
    return pl.pallas_call(
        functools.partial(attend_kernel, plan, width),
        grid=(HALF_PAIRS,),
        in_specs=[SMEM, whole_k, whole_q, pair_q] + [pair_kv] * groups,
        out_specs=[pair, pair, pl.BlockSpec((1, 2, local), lambda p: (p, 0, 0))],
        out_shape=[
            shape_of((local, HALF), F32),
            shape_of((local, HALF), BF16),
            shape_of((HALF_PAIRS, 2, local), F32),
        ],
        scratch_shapes=[
            pltpu.VMEM((2, groups * local, width), F32),
            pltpu.VMEM((2, groups * local, width), BF16),
        ],
        compiler_params=params(),
        cost_estimate=cost(COSTS["attend"]),
        name="attend",
    )(*inputs)


def attend_back_kernel(
    plan, width, order, kmask, qmask, q_ref, do_ref, o_ref, lse_ref, cos_ref, sin_ref, *refs
):
    groups, local = plan.groups, plan.local
    kv = refs[:groups]
    dq_ref = refs[groups]
    dkv = refs[groups + 1 : 2 * groups + 1]
    held, p_ref, ds_ref = refs[2 * groups + 1 :]
    keys_t = [kv[e][0].T for e in range(groups)]
    scale = 1.0 / math.sqrt(HD)
    chunk = 128
    for first in range(0, local, width):
        rows = slice(first, first + width)
        queries = q_ref[rows, :] * jnp.asarray(scale, BF16)
        dout = do_ref[rows, :]
        product = (dout.astype(F32) * o_ref[rows, :]).T
        parts = []
        for h in range(2):
            masked_queries = head_part(queries, h, qmask[rows, :])
            head_queries = head_part(queries, h)
            head_dout = head_part(dout, h)
            lse = lse_ref[0, h : h + 1, rows]
            delta = jnp.sum(product[h * HD : (h + 1) * HD, :], axis=0, keepdims=True)
            grad_queries = jnp.zeros((HD, width), F32)
            for e in range(groups):
                for c in range(0, local, chunk):
                    part = slice(c, c + chunk)
                    mask = kmask[e * local + c : e * local + c + chunk, :]
                    scores = dot(head_part(kv[e][0, part, :], h, mask), masked_queries, NT)
                    dprobs = dot(kv[e][1, part, :], head_dout, NT)
                    probs = jnp.exp(scores - lse)
                    p_ref[h, e, part, :] = probs.astype(BF16)
                    ds_ref[h, e, part, :] = (probs * (dprobs - delta)).astype(BF16)
                grad_values = dot(p_ref[h, e], head_dout, NN)
                grad_keys = dot(ds_ref[h, e], head_queries, NN)
                if first == 0 and h == 0:
                    held[e, 0] = grad_keys
                    held[e, 1] = grad_values
                else:
                    held[e, 0] += grad_keys
                    held[e, 1] += grad_values
                grad_queries = grad_queries + dot(
                    keys_t[e][h * HD : (h + 1) * HD, :], ds_ref[h, e], NN
                )
            parts.append(grad_queries)
        grad = jnp.concatenate(parts, axis=0).T * scale
        dq_ref[rows, :] = rotate_pair(grad, cos_ref[rows, :], sin_ref[rows, :], -1.0).astype(BF16)
    for e in range(groups):
        dkv[e][...] = held[e].astype(BF16)


def attend_back(plan, part, meta, mask, queries, dout, heads, lse, cosine, sine, kv):
    local, groups = plan.local, plan.groups
    width = min(512, local)
    half, first, count = part
    skip = half * HALF_PAIRS + first
    wide = 128 * count
    pair = pl.BlockSpec((local, 128), lambda p: (0, p))
    pair_h = pl.BlockSpec((local, 128), lambda p: (0, p + first))
    pair_q = pl.BlockSpec((local, 128), lambda p: (0, p + skip))
    whole_k = pl.BlockSpec((groups * local, 128), lambda p: (0, 0))
    inputs = [meta, *mask, queries, dout, heads, lse, cosine, sine, *kv]
    table = pl.BlockSpec((local, 128), lambda p: (0, 0))
    pair_kv = pl.BlockSpec((2, local, 128), lambda p: (0, 0, p))
    pair_kv_h = pl.BlockSpec((2, local, 128), lambda p: (0, 0, p + first))
    return pl.pallas_call(
        functools.partial(attend_back_kernel, plan, width),
        grid=(count,),
        in_specs=[
            SMEM,
            whole_k,
            table,
            pair_q,
            pair_q,
            pair_h,
            pl.BlockSpec((1, 2, local), lambda p: (p + first, 0, 0)),
            table,
            table,
        ]
        + [pair_kv_h] * groups,
        out_specs=[pair] + [pair_kv] * groups,
        out_shape=[shape_of((local, wide), BF16)] + [shape_of((2, local, wide), BF16)] * groups,
        scratch_shapes=[
            pltpu.VMEM((groups, 2, local, 128), F32),
            pltpu.VMEM((2, groups, local, width), BF16),
            pltpu.VMEM((2, groups, local, width), BF16),
        ],
        compiler_params=params(),
        cost_estimate=cost(4 * count),
        name="attend_back",
    )(*inputs)


def middle_kernel(plan, meta, gain_ref, *refs):
    rows, tok, local = plan.rows, plan.tok, plan.local
    count = source_count(plan)
    low_refs, refs = refs[:HALVES], refs[HALVES:]
    x_refs, refs = refs[:rows], refs[rows:]
    sources, refs = refs[:count], refs[count:]
    out_refs, refs = refs[:rows], refs[rows:]
    do_out, dh_out, refs = refs[0], refs[1], refs[2:]
    grads, refs = refs[: 4 if plan.aligned else 1], refs[4 if plan.aligned else 1 :]
    low_ref, x_ref, dy_ref, w_out, w_in, w_down, h_ref, unit_ref, n_ref, gu_ref = refs[:10]
    mid_ref, dgu_ref, out_ref, do_ref, dh_ref, da_ref, g_out, g_in, g_down, sems = refs[10:]
    mover = Mover(sems)
    r, rf = block_size(plan)
    blocks = [block_of(plan, meta, i) for i in range(count)]
    low_in = [
        mover.start(low_refs[h], low_ref.at[:, pl.ds(HALF * h, HALF)]) for h in range(HALVES)
    ]
    out_in = [
        mover.start(source.at[pl.ds(0, r)], w_out.at[rows_at(block, r)])
        for source, block in zip(sources, blocks)
    ]
    x_in = [mover.start(x_refs[j].at[0], x_ref.at[pl.ds(tok * j, tok)]) for j in range(rows)]

    def fetch_in(t):
        return [
            mover.start(source.at[pl.ds((1 + t) * r, r)], w_in.at[t, rows_at(block, r)])
            for source, block in zip(sources, blocks)
        ]

    wait_all(low_in)
    in_in = [fetch_in(0)]
    wait_all(out_in)
    wait_all(x_in)
    in_in.append(fetch_in(1))
    gain = gain_ref[1:2, :]
    inv_stds = []
    for j in range(rows):
        part = slice(tok * j, tok * (j + 1))
        hidden = x_ref[part, :].astype(F32) + dot(low_ref[part, :], w_out[...], NN)
        h_ref[part, :] = hidden
        unit, inv_std = layer_norm(hidden)
        inv_stds.append(inv_std)
        unit_ref[part, :] = unit
        n_ref[part, :] = (unit * gain).astype(BF16)
    for t in range(3):
        wait_all(in_in[t])
        if t == 0:
            in_in.append(fetch_in(2))
        if t == 1:
            dy_in = [
                mover.start(x_refs[j].at[1], dy_ref.at[pl.ds(tok * j, tok)]) for j in range(rows)
            ]
            down_in = [
                mover.start(source.at[pl.ds(4 * r, rf)], w_down.at[rows_at(block, rf)])
                for source, block in zip(sources, blocks)
            ]
        gu_ref[:, D * t : D * (t + 1)] = dot(n_ref[...], w_in[t], NN)
    wait_all(dy_in)
    wait_all(down_in)
    dy = dy_ref[...]
    size = FF // 3
    for f in range(3):
        cols = slice(size * f, size * (f + 1))
        up_cols = slice(FF + size * f, FF + size * (f + 1))
        gate = gu_ref[:, cols]
        up = gu_ref[:, up_cols]
        below = 0.5 + 0.5 * lax.erf(gate * math.sqrt(0.5))
        active = gate * below
        mid_ref[:, cols] = (active * up).astype(BF16)
        slope = below + gate * jnp.exp(-0.5 * gate * gate) * (1.0 / math.sqrt(2.0 * math.pi))
        dmid = dot(dy, w_down[cols, :], NT)
        dgu_ref[:, cols] = (dmid * up * slope).astype(BF16)
        dgu_ref[:, up_cols] = (dmid * active).astype(BF16)
    targets = [grad_target(plan, grads, i) for i in range(count)]
    g_down[...] = dot(mid_ref[...], dy, TN).astype(BF16)
    for target, block in zip(targets, blocks):
        mover.send(g_down.at[rows_at(block, rf)], target.at[pl.ds(4 * r, rf)])
    out_ref[...] = (h_ref[...] + dot(mid_ref[...], w_down[...], NN)).astype(BF16)
    for j in range(rows):
        mover.send(out_ref.at[pl.ds(tok * j, tok)], out_refs[j])
    grad_normed = dot(dgu_ref[:, :D], w_in[0], NT)
    for t in range(1, 3):
        grad_normed = grad_normed + dot(dgu_ref[:, D * t : D * (t + 1)], w_in[t], NT)
    dh_ref[...] = grad_normed

    def grad_in(t):
        g_in[t] = dot(n_ref[...], dgu_ref[:, D * t : D * (t + 1)], TN).astype(BF16)
        for target, block in zip(targets, blocks):
            mover.send(g_in.at[t, rows_at(block, r)], target.at[pl.ds((1 + t) * r, r)])

    for j in range(rows):
        part = slice(tok * j, tok * (j + 1))
        grad_hidden = dy[part, :].astype(F32) + norm_backward(
            dh_ref[part, :], unit_ref[part, :], inv_stds[j], gain
        )
        dh_ref[part, :] = grad_hidden
        da_ref[part, :] = grad_hidden.astype(BF16)
        if j < 3:
            grad_in(j)
    for t in range(rows, 3):
        grad_in(t)
    mover.send(dh_ref, dh_out)
    do_ref[...] = dot(da_ref[...], w_out[...], NT).astype(BF16)
    mover.send(do_ref, do_out)
    g_out[...] = dot(low_ref[...], da_ref[...], TN).astype(BF16)
    for target, block in zip(targets, blocks):
        mover.send(g_out.at[rows_at(block, r)], target.at[pl.ds(0, r)])
    mover.finish()


def middle(plan, meta, low, gains, pieces, sources):
    local, rows, tok = plan.local, plan.rows, plan.tok
    count = len(sources)
    total = 4 * D + FF
    if plan.aligned:
        grads = grad_blocks(plan, plan.packed, D)
    else:
        grads = [shape_of((total, D), BF16)]
    return pl.pallas_call(
        functools.partial(middle_kernel, plan),
        in_specs=[SMEM, VMEM] + [ANY] * (HALVES + rows + count),
        out_specs=[ANY] * (rows + 2 + len(grads)),
        out_shape=[shape_of((tok, D), BF16)] * rows
        + [shape_of((local, D), BF16), shape_of((local, D), F32)]
        + grads,
        scratch_shapes=[
            pltpu.VMEM((local, D), BF16),
            pltpu.VMEM((local, D), BF16),
            pltpu.VMEM((local, D), BF16),
            pltpu.VMEM((D, D), BF16),
            pltpu.VMEM((3, D, D), BF16),
            pltpu.VMEM((FF, D), BF16),
            pltpu.VMEM((local, D), F32),
            pltpu.VMEM((local, D), F32),
            pltpu.VMEM((local, D), BF16),
            pltpu.VMEM((local, 2 * FF), F32),
            pltpu.VMEM((local, FF), BF16),
            pltpu.VMEM((local, 2 * FF), BF16),
            pltpu.VMEM((local, D), BF16),
            pltpu.VMEM((local, D), BF16),
            pltpu.VMEM((local, D), F32),
            pltpu.VMEM((local, D), BF16),
            pltpu.VMEM((D, D), BF16),
            pltpu.VMEM((3, D, D), BF16),
            pltpu.VMEM((FF, D), BF16),
            pltpu.SemaphoreType.DMA((HALVES + 3 * rows + 2 + 10 * count,)),
        ],
        compiler_params=params(),
        cost_estimate=cost(COSTS["middle"]),
        name="middle",
    )(meta, gains, *low, *pieces, *sources)


def back_weight_kernel(plan, meta, *refs):
    groups, local = plan.groups, plan.local
    count = len(BACK_PARTS)
    cos_ref, sin_ref, n_in, refs = refs[0], refs[1], refs[2], refs[3:]
    dq_refs, refs = refs[:count], refs[count:]
    dkv, refs = refs[: count * groups], refs[count * groups :]
    dp_out, refs = refs[0], refs[1:]
    grads, refs = refs[: 4 if plan.aligned else 1], refs[4 if plan.aligned else 1 :]
    cos, sin, n_ref, dkv_ref, dp_ref, g_ref, sems = refs
    mover = Mover(sems)
    columns = []
    for half, first, pairs in BACK_PARTS:
        columns.append(pl.ds(HALF * half + 128 * first, 128 * pairs))
    first_in = [mover.start(n_in, n_ref)]
    for i in range(count):
        first_in.append(mover.start(dq_refs[i], dp_ref.at[0, :, columns[i]]))
    rest_in = [mover.start(cos_ref, cos), mover.start(sin_ref, sin)]
    for i in range(count):
        for e in range(groups):
            rest_in.append(
                mover.start(dkv[groups * i + e], dkv_ref.at[e, :, :, columns[i]])
            )
    r, _ = block_size(plan)

    def send_grad(t):
        cols = pl.ds(D * t, D)
        for i in range(source_count(plan)):
            at = rows_at(block_of(plan, meta, i), r)
            mover.send(g_ref.at[at, cols], grad_target(plan, grads, i).at[:, cols])

    wait_all(first_in)
    normed = n_ref[...]
    g_ref[:, :D] = dot(normed, dp_ref[0], TN).astype(BF16)
    send_grad(0)
    wait_all(rest_in)
    dp_ref[2] = sum_pieces([dkv_ref[e, 1] for e in range(groups)]).astype(BF16)
    g_ref[:, 2 * D : 3 * D] = dot(normed, dp_ref[2], TN).astype(BF16)
    send_grad(2)
    grad_keys = sum_pieces([dkv_ref[e, 0] for e in range(groups)])
    dp_ref[1] = rotate_all(grad_keys, cos[...], sin[...], -1.0).astype(BF16)
    mover.send(dp_ref, dp_out)
    g_ref[:, D : 2 * D] = dot(normed, dp_ref[1], TN).astype(BF16)
    send_grad(1)
    mover.finish()


def back_weight(plan, meta, cosine, sine, normed, dq, dkv):
    local, groups, count = plan.local, plan.groups, len(BACK_PARTS)
    if plan.aligned:
        grads = grad_blocks(plan, plan.r, 3 * D)
    else:
        grads = [shape_of((D, 3 * D), BF16)]
    results = pl.pallas_call(
        functools.partial(back_weight_kernel, plan),
        in_specs=[SMEM] + [ANY] * (3 + count * (1 + groups)),
        out_specs=[ANY] * (1 + len(grads)),
        out_shape=[shape_of((3, local, D), BF16)] + grads,
        scratch_shapes=[
            pltpu.VMEM((local, 128), F32),
            pltpu.VMEM((local, 128), F32),
            pltpu.VMEM((local, D), BF16),
            pltpu.VMEM((groups, 2, local, D), BF16),
            pltpu.VMEM((3, local, D), BF16),
            pltpu.VMEM((D, 3 * D), BF16),
            pltpu.SemaphoreType.DMA((4 + count * (1 + groups) + 3 * source_count(plan),)),
        ],
        compiler_params=params(),
        cost_estimate=cost(COSTS["back_weight"]),
        name="back_weight",
    )(meta, cosine, sine, normed, *dq, *dkv)
    return results[0], results[1:]


def back_in_kernel(plan, meta, dp_ref, dh_ref, gain_ref, *refs):
    rows, tok = plan.rows, plan.tok
    count = source_count(plan)
    x_refs, refs = refs[:rows], refs[rows:]
    out_refs, refs = refs[:rows], refs[rows:]
    sources, refs = refs[:count], refs[count:]
    both_refs = refs[:rows]
    w_ref, in_sems = refs[rows:]
    copies = qkv_copies(plan, meta, sources, w_ref, in_sems)
    for copy in copies:
        copy.start()
    for copy in copies:
        copy.wait()
    grad_normed = dot(dp_ref[0], w_ref[:, :D], NT)
    for t in range(1, 3):
        grad_normed = grad_normed + dot(dp_ref[t], w_ref[:, D * t : D * (t + 1)], NT)
    for j in range(rows):
        part = slice(tok * j, tok * (j + 1))
        unit, inv_std = layer_norm(x_refs[j][0].astype(F32))
        grad = grad_normed[part, :]
        back = norm_backward(grad, unit, inv_std, gain_ref[0:1, :])
        both_refs[j][0] = out_refs[j][...]
        both_refs[j][1] = (dh_ref[part, :] + back).astype(BF16)


def back_in(plan, meta, dprojected, dhidden, gains, pieces, outs, sources):
    rows, tok = plan.rows, plan.tok
    count = len(sources)
    return pl.pallas_call(
        functools.partial(back_in_kernel, plan),
        in_specs=[SMEM] + [VMEM] * (3 + 2 * rows) + [ANY] * count,
        out_specs=[VMEM] * rows,
        out_shape=[shape_of((2, tok, D), BF16)] * rows,
        scratch_shapes=[pltpu.VMEM((D, EXT), BF16), pltpu.SemaphoreType.DMA((count,))],
        compiler_params=params(),
        cost_estimate=cost(COSTS["back_in"]),
        name="back_in",
    )(meta, dprojected, dhidden, gains, *pieces, *outs, *sources)


def gain_columns(weight, grad):
    total = jnp.sum(weight.astype(F32) * grad.astype(F32), axis=1, keepdims=True)
    high = total.astype(BF16)
    return high, (total - high.astype(F32)).astype(BF16)


def pad_width(plan):
    return -(-(3 * plan.cw + 2) // 128) * 128


def gain_tail(plan, weight, grad):
    width = pad_width(plan) - 3 * plan.cw
    high, rest = gain_columns(weight, grad)
    lane = lax.broadcasted_iota(jnp.int32, (plan.r, width), 1)
    return jnp.where(lane == 0, high, jnp.where(lane == 1, rest, jnp.zeros_like(high)))


def cut_qkv_kernel(plan, meta, total, weight, *refs):
    outs, held = refs[: plan.nrow], refs[plan.nrow]
    width = 3 * plan.cw
    tail = gain_tail(plan, weight[:, : 3 * D], total[...])
    for z in range(plan.nrow):
        place_at = meta[plan.at_z + z]
        held[place_at, :, :width] = total[:, width * z : width * (z + 1)]
        held[place_at, :, width:] = tail
    for j in range(plan.nrow):
        outs[j][...] = held[j]


def cut_qkv(plan, meta, total, weight):
    width, wide = 3 * plan.cw, pad_width(plan)
    if not plan.aligned:
        tail = gain_tail(plan, weight[:, : 3 * D], total)
        parts = [
            jnp.concatenate([total[:, width * z : width * (z + 1)], tail], axis=1)
            for z in range(plan.nrow)
        ]
        return ordered(plan, meta, parts)
    return pl.pallas_call(
        functools.partial(cut_qkv_kernel, plan),
        in_specs=[SMEM, VMEM, VMEM],
        out_specs=[VMEM] * plan.nrow,
        out_shape=[shape_of((plan.r, wide), BF16)] * plan.nrow,
        scratch_shapes=[pltpu.VMEM((plan.nrow, plan.r, wide), BF16)],
        compiler_params=params(),
        cost_estimate=cost(COSTS["cut_qkv"]),
        name="cut_qkv",
    )(meta, total, weight)


def gain_blank(plan, weight, grad):
    r, blank = plan.r, 2 * plan.r - plan.rf
    cols = [weight[r * t : r * (t + 1)] for t in range(1, 4)]
    grads = [grad[r * t : r * (t + 1)] for t in range(1, 4)]
    high, rest = gain_columns(jnp.concatenate(cols, axis=1), jnp.concatenate(grads, axis=1))
    lane = lax.broadcasted_iota(jnp.int32, (blank, plan.cw), 1)
    found = jnp.zeros((blank, plan.cw), BF16)
    for i in range(r // blank):
        part = slice(blank * i, blank * (i + 1))
        found = jnp.where(lane == 2 * i, high[part], found)
        found = jnp.where(lane == 2 * i + 1, rest[part], found)
    return found


def cut_rest_kernel(plan, meta, total, weight, *refs):
    outs, held = refs[: plan.nrow], refs[plan.nrow]
    r, rf, cw = plan.r, plan.rf, plan.cw
    blank = gain_blank(plan, weight[...], total[...])
    for z in range(plan.nrow):
        place_at = meta[plan.at_z + z]
        cols = slice(cw * z, cw * (z + 1))
        parts = []
        for i in range(3):
            block, at = (3 * z + i) // plan.nrow, (3 * z + i) % plan.nrow
            parts.append(total[r * (1 + block) : r * (2 + block), cw * at : cw * (at + 1)])
        held[place_at, :r, :] = jnp.concatenate([parts[0], parts[2]], axis=1)
        held[place_at, r : 2 * r, :] = jnp.concatenate(
            [parts[1], total[4 * r : 5 * r, cols]], axis=1
        )
        rest = total[5 * r : 4 * r + rf, cols]
        held[place_at, 2 * r :, :] = jnp.concatenate(
            [total[:r, cols], jnp.concatenate([rest, blank], axis=0)], axis=1
        )
    for j in range(plan.nrow):
        outs[j][...] = held[j]


def cut_rest(plan, meta, total, weight):
    r, cw = plan.r, plan.cw
    if not plan.aligned:
        grad_in = jnp.concatenate([total[r * (1 + t) : r * (2 + t)] for t in range(3)], axis=1)
        blank = gain_blank(plan, weight, total)
        parts = [
            pack_rest(
                plan,
                total[:r, cw * z : cw * (z + 1)],
                grad_in[:, 3 * cw * z : 3 * cw * (z + 1)],
                total[4 * r :, cw * z : cw * (z + 1)],
                blank,
            )
            for z in range(plan.nrow)
        ]
        return ordered(plan, meta, parts)
    return pl.pallas_call(
        functools.partial(cut_rest_kernel, plan),
        in_specs=[SMEM, VMEM, VMEM],
        out_specs=[VMEM] * plan.nrow,
        out_shape=[shape_of((3 * r, 2 * cw), BF16)] * plan.nrow,
        scratch_shapes=[pltpu.VMEM((plan.nrow, 3 * r, 2 * cw), BF16)],
        compiler_params=params(),
        cost_estimate=cost(COSTS["cut_rest"]),
        name="cut_rest",
    )(meta, total, weight)


def reduce_z(plan, pieces):
    return [pieces[0]] + [
        lax.ppermute(pieces[j], "row", plan.z_pairs(j)) for j in range(1, plan.nrow)
    ]


def sum_pieces(pieces):
    total = pieces[0].astype(F32)
    for piece in pieces[1:]:
        total = total + piece.astype(F32)
    return total


def end_rest_kernel(plan, *refs):
    pieces, (g_out, g_in, g_down, g_gain) = refs[: plan.nrow], refs[plan.nrow :]
    total = sum_pieces([piece[...] for piece in pieces])
    parts_in, part_out, part_down = unpack_rest(plan, total)
    g_out[...] = part_out
    g_in[...] = jnp.concatenate(parts_in, axis=1)
    g_down[...] = part_down
    blank = 2 * plan.r - plan.rf
    g_gain[...] = total[3 * plan.r - blank :, plan.cw : plan.cw + 128].T[:8, :]


def end_rest(plan, pieces):
    r, blank = plan.r, 2 * plan.r - plan.rf
    if not plan.aligned:
        total = sum_pieces(pieces)
        parts_in, out_grad, down_grad = unpack_rest(plan, total)
        in_grad = jnp.concatenate(parts_in, axis=1)
        gain = total[3 * r - blank :, plan.cw : plan.cw + 8].T
    else:
        out_grad, in_grad, down_grad, gain = pl.pallas_call(
            functools.partial(end_rest_kernel, plan),
            in_specs=[VMEM] * plan.nrow,
            out_specs=[VMEM] * 4,
            out_shape=[
                shape_of((r, plan.cw), F32),
                shape_of((r, 3 * plan.cw), F32),
                shape_of((plan.rf, plan.cw), F32),
                shape_of((8, blank), F32),
            ],
            compiler_params=params(),
            cost_estimate=cost(COSTS["end_rest"]),
            name="end_rest",
        )(*pieces)
    gain = jnp.concatenate([gain[2 * i] + gain[2 * i + 1] for i in range(r // blank)])
    return out_grad, in_grad, down_grad, gain


def end_qkv_kernel(plan, gain_ref, *refs):
    pieces, (g_qkv, g_gain) = refs[: plan.nrow], refs[plan.nrow :]
    width, wide = 3 * plan.cw, pad_width(plan)
    total = sum_pieces([piece[...] for piece in pieces])
    g_qkv[...] = total[:, :width]
    tail = total[:, wide - 128 :].T
    at = width - (wide - 128)
    g_gain[...] = (tail[at : at + 1, :] + tail[at + 1 : at + 2, :]) / gain_ref[...]


def end_qkv(plan, gain, pieces):
    width, wide = 3 * plan.cw, pad_width(plan)
    if not plan.aligned:
        total = sum_pieces(pieces)
        return total[:, :width], (total[:, width] + total[:, width + 1]) / gain[0]
    grad, gain_grad = pl.pallas_call(
        functools.partial(end_qkv_kernel, plan),
        in_specs=[VMEM] * (1 + plan.nrow),
        out_specs=[VMEM] * 2,
        out_shape=[shape_of((plan.r, width), F32), shape_of((1, plan.r), F32)],
        compiler_params=params(),
        cost_estimate=cost(COSTS["end_qkv"]),
        name="end_qkv",
    )(gain, *pieces)
    return grad, gain_grad.reshape(plan.r)


def rotation_tables(plan, meta, lengths):
    ends = jnp.cumsum(lax.dynamic_index_in_dim(lengths, meta[plan.at_lo], 0, keepdims=False))
    starts = jnp.concatenate([jnp.zeros((1,), jnp.int32), ends[:-1]])
    bases = meta[plan.at_base : plan.at_base + plan.rows]
    places = (bases[:, None] + jnp.arange(plan.tok, dtype=jnp.int32)[None, :]).reshape(-1)
    passed = places[:, None] >= starts[None, :]
    positions = places - jnp.max(jnp.where(passed, starts[None, :], 0), axis=1)
    half = HD // 2
    inverse = ROPE_BASE ** (-(jnp.arange(half, dtype=F32) * (2.0 / HD)))
    angles = positions.astype(F32)[:, None] * inverse
    cosine, sine = jnp.cos(angles), jnp.sin(angles)
    return (
        jnp.concatenate([cosine] * 4, axis=1),
        jnp.concatenate([-sine, sine, -sine, sine], axis=1),
    )


def body(
    plan,
    tokens,
    lengths,
    norm_gain,
    qkv_weight,
    out_weight,
    mlp_gain,
    in_weight,
    down_weight,
    cotangent,
):
    blk, row = lax.axis_index("blk"), lax.axis_index("row")
    meta = lax.dynamic_slice(
        jnp.asarray(plan.table), (row, blk, 0), (1, 1, plan.size)
    ).reshape(plan.size)
    qkv_parts = gather_z(plan, qkv_weight)
    cut, packed = prepare(plan, meta, tokens, cotangent, out_weight, in_weight, down_weight)
    pieces = exchange_rows(plan, cut)
    rest_parts = gather_z(plan, packed, behind=qkv_parts)
    gains = jnp.pad(jnp.stack([norm_gain, mlp_gain], axis=1), ((0, 0), (0, 126)))
    cosine, sine = rotation_tables(plan, meta, lengths)
    mask = masks(plan, meta, lengths)
    qkv_joined = join_qkv(plan, meta, gains, qkv_parts)
    qkv_own = gather_start(plan, qkv_joined, pieces[1:])
    qkv_own[1] = tie(qkv_own[1], *rest_parts[2:], cosine, sine, *mask)
    qkv_own = gather_more(plan, qkv_own)
    qkv_own[-1] = tie(qkv_own[-1], rest_parts[1])
    qkv_other = [swap_cores(plan, piece) for piece in qkv_own]
    qkv_from = qkv_sources(plan, meta, qkv_own, qkv_other)
    rest_parts[0] = tie(rest_parts[0], qkv_joined, *qkv_other[:-1])
    joined = join_rest(plan, meta, rest_parts)
    results = project(plan, tie(meta, joined), cosine, sine, pieces, qkv_from)
    queries, kv, (normed, gains) = results[0], results[1 : 1 + HALVES], results[1 + HALVES :]
    kv = [
        [part]
        + [
            lax.ppermute(part, "blk", plan.xor_pairs(plan.member(e)))
            for e in range(1, plan.groups)
        ]
        for part in kv
    ]
    rest_own = gather_start(plan, joined)
    heads, low, lse = [None] * HALVES, [None] * HALVES, [None] * HALVES
    heads[0], low[0], lse[0] = attend(plan, 0, meta, mask, queries, kv[0])
    order = tie(meta, low[0], *rest_own[1:])
    rest_own[1:] = [tie(piece, low[0]) for piece in rest_own[1:]]
    rest_other = [swap_cores(plan, piece) for piece in rest_own]
    rest_more = gather_more(plan, rest_own)[len(rest_own) :]
    heads[1], low[1], lse[1] = attend(plan, 1, order, mask, queries, kv[1])
    rest_more = [tie(piece, low[1]) for piece in rest_more]
    rest_own = rest_own + rest_more
    rest_other = rest_other + [swap_cores(plan, piece) for piece in rest_more]
    rest_from = rest_sources(plan, meta, rest_own, rest_other)
    results = middle(plan, meta, low, gains, pieces, rest_from)
    outs, (dout, dhidden), rest_grads = (
        results[: plan.rows],
        results[plan.rows : plan.rows + 2],
        results[plan.rows + 2 :],
    )
    if not plan.aligned:
        r, rf, nblk = plan.r, plan.rf, plan.nblk
        whole = rest_grads[0]
        blocks = [whole[D * i : D * (i + 1)].reshape(nblk, r, D) for i in range(4)]
        blocks.append(whole[4 * D :].reshape(nblk, rf, D))
        rest_grads = split_blocks(plan, meta, jnp.concatenate(blocks, axis=1))
    keep_low, keep_high, other_low, other_high = reduce_start(plan, rest_grads)
    dq, dkv = [], []
    order = meta
    for i, part in enumerate(BACK_PARTS):
        half = part[0]
        results = attend_back(
            plan, part, order, mask, queries, dout, heads[half], lse[half], cosine, sine, kv[half]
        )
        dq.append(results[0])
        dkv.append(results[1])
        dkv += [
            lax.ppermute(results[1 + e], "blk", plan.xor_pairs(plan.member(e)))
            for e in range(1, plan.groups)
        ]
        if i == 0:
            rest_high = add_low(tie(keep_high, dq[0]), other_high)
            rest_low = add_low(tie(keep_low, dq[0]), other_low)
            order = tie(meta, dq[0], rest_high, rest_low)
        else:
            order = tie(meta, dq[i], *dkv[1 : plan.groups])
    rest_low, rest_high = reduce_step(plan, plan.bits - 1, tie(rest_low, dq[-1]), rest_high)
    order = tie(meta, rest_low) if rest_high is None else tie(meta, rest_low, rest_high)
    dprojected, qkv_grads = back_weight(plan, order, cosine, sine, normed, dq, dkv)
    if not plan.aligned:
        qkv_grads = split_blocks(plan, meta, qkv_grads[0].reshape(plan.nblk, plan.r, 3 * D))
    rest_low = tie(rest_low, dprojected)
    for step in reversed(range(plan.bits - 1)):
        rest_low, rest_high = reduce_step(plan, step, rest_low, rest_high)
    keep_low, keep_high, other_low, other_high = reduce_start(plan, qkv_grads)
    qkv_high = add_low(tie(keep_high, rest_low), other_high)
    qkv_low = add_low(keep_low, other_low)
    rest_cut = cut_rest(plan, meta, tie(rest_low, qkv_high), joined)
    order = tie(meta, qkv_high, qkv_low, *rest_cut)
    both = back_in(plan, order, dprojected, dhidden, gains, pieces, outs, qkv_from)
    rest_pieces = reduce_z(plan, rest_cut)
    qkv_low = tie(qkv_low, both[0], *rest_pieces[1:3])
    for step in reversed(range(plan.bits)):
        if step == 0:
            qkv_low = tie(qkv_low, *rest_pieces[3:])
        qkv_low, qkv_high = reduce_step(plan, step, qkv_low, qkv_high)
    both = exchange_rows(plan, [tie(piece, qkv_low) for piece in both])
    qkv_cut = cut_qkv(plan, meta, tie(qkv_low, *rest_pieces[1:]), qkv_joined)
    qkv_pieces = reduce_z(plan, qkv_cut)
    rest_pieces[0] = tie(rest_pieces[0], *qkv_cut)
    out_grad, in_grad, down_grad, mlp_gain_grad = end_rest(plan, rest_pieces)
    output, input_grad = place(plan, meta, [tie(both[0], *qkv_cut)] + both[1:])
    gain_row = norm_gain.astype(F32)[None]
    qkv_grad, norm_gain_grad = end_qkv(plan, tie(gain_row, output, input_grad, in_grad), qkv_pieces)
    mlp_gain_grad = mlp_gain_grad / mlp_gain.astype(F32)
    return (
        output,
        input_grad,
        norm_gain_grad,
        qkv_grad,
        out_grad,
        mlp_gain_grad,
        in_grad,
        down_grad,
    )


def solution(mesh):
    weights = P("blk", "row")
    acts = P("row", "blk", None)

    def run(*args):
        rows = args[0].shape[0] // mesh.shape["row"]
        tok = args[0].shape[1] // mesh.shape["blk"]
        plan = Plan(mesh, rows, tok)
        return jax.shard_map(
            functools.partial(body, plan),
            mesh=mesh,
            in_specs=(acts, P("row", None), P("blk"), weights, weights, P("blk"), weights, weights, acts),
            out_specs=(acts, acts, P("blk"), weights, weights, P("blk"), weights, weights),
            check_vma=False,
        )(*args)

    return run
```

profile of v0, /device:TPU:17, one launch (start us, length us, event | category | flops | bytes accessed | tf_op | source)
XLA Modules:
  0.0 209.1 jit_solution(1540020839848068641)
XLA Ops:
  0.7 2.5 %collective-permute-start.2 = (bf16[96,576]{1,0:T(8,128)(2,1)}, bf16[96,576]{1,0:T(8,128)(2,1)S(1)}, u32[]{:S(2)}, u32[]{:S(2)}) collective-permute-start(bf16[96,576]{1,0:T(8,128)(2,1)} %refs_0_.1), channel_id=1, source_target_pairs={{0,24},{8,16},{16,8},{24,0},{1,25},{9,17},{17,9},{25,1},{2,26},{10... | collective-permute-start | bytes 331784 | tf_op jit(solution)/shard_map/ppermute | solution.py:149
  3.2 1.1 collective-permute-start
  5.0 1.1 copy-done.4
  6.1 1.1 copy-done.5
  9.8 1.4 prepare.1
  11.3 2.2 %collective-permute-start.10 = (bf16[2,128,768]{2,1,0:T(8,128)(2,1)}, bf16[2,128,768]{2,1,0:T(8,128)(2,1)S(1)}, u32[]{:S(2)}, u32[]{:S(2)}) collective-permute-start(bf16[2,128,768]{2,1,0:T(8,128)(2,1)} %get-tuple-element.110), channel_id=1, source_target_pairs={{0,6},{1,7},{2,4},{3,5},{4,2},{5,3},{6,0},{7,1},{8,14},{9,15},{10,... | collective-permute-start | bytes 1179656 | tf_op jit(solution)/shard_map/ppermute | solution.py:155
  18.7 1.3 collective-permute-start.4
  20.1 1.4 collective-permute-done.10.refs_3_.refs_5_
  21.7 1.0 fusion.2
  22.7 7.3 %collective-permute-done.8.refs_1_.refs_3_ = bf16[2,128,768]{2,1,0:T(8,128)(2,1)S(1)} collective-permute-done((bf16[2,128,768]{2,1,0:T(8,128)(2,1)S(1)}, bf16[2,128,768]{2,1,0:T(8,128)(2,1)S(1)}, u32[]{:S(2)}, u32[]{:S(2)}) %collective-permute-start.8) | collective-permute-done | bytes 393248 | tf_op jit(solution)/shard_map/ppermute | solution.py:155
  30.0 1.2 collective-permute-done.9.refs_2_.refs_4_
  31.2 1.2 collective-permute-start.11
  32.9 1.1 masks.1
  34.0 6.8 %collective-permute-done.6.refs_3_ = bf16[288,384]{1,0:T(8,128)(2,1)S(1)} collective-permute-done((bf16[288,384]{1,0:T(8,128)(2,1)S(1)}, bf16[288,384]{1,0:T(8,128)(2,1)S(1)}, u32[]{:S(2)}, u32[]{:S(2)}) %collective-permute-start.6) | collective-permute-done | bytes 221216 | tf_op jit(solution)/shard_map/ppermute | solution.py:149
  40.8 1.2 collective-permute-start.14
  43.2 5.2 %collective-permute-done.13.refs_1_ = bf16[288,384]{1,0:T(8,128)(2,1)S(1)} collective-permute-done((bf16[288,384]{1,0:T(8,128)(2,1)S(1)}, bf16[288,384]{1,0:T(8,128)(2,1)S(1)}, u32[]{:S(2)}, u32[]{:S(2)}) %collective-permute-start.13) | collective-permute-done | bytes 221216 | tf_op jit(solution)/shard_map/ppermute | solution.py:149
  48.5 2.2 %collective-permute-start.15 = (bf16[96,2432]{1,0:T(8,128)(2,1)S(1)}, bf16[96,2432]{1,0:T(8,128)(2,1)S(1)}, u32[]{:S(2)}, u32[]{:S(2)}) collective-permute-start(bf16[96,2432]{1,0:T(8,128)(2,1)S(1)} %collective-permute-done.14.refs_7_.refs_11_), channel_id=1, source_target_pairs={{0,1},{1,0},{2,3},{3,2},{4,5},{5,4},{6,7},{7,6},{8,9},{9,8},{10,11... | collective-permute-start | bytes 1400840 | tf_op jit(solution)/shard_map/ppermute | solution.py:142
  52.2 6.2 %project.1 = (bf16[512,768]{1,0:T(8,128)(2,1)S(1)}, bf16[2,512,384]{2,1,0:T(8,128)(2,1)S(1)}, bf16[2,512,384]{2,1,0:T(8,128)(2,1)S(1)}, bf16[512,768]{1,0:T(8,128)(2,1)S(1)}, f32[8,768]{1,0:T(8,128)S(1)}) custom-call(s32[25]{0:T(128)S(1)} %fusion.3.meta.order, f32[512,128]{1,0:T(8,128)S(1)} %get-tuple-element.205.cos_ref.refs_0_, ...), custom_call_target="tpu_custom_call" | custom-call | flops 7000000 | bytes 1024 | tf_op jit(solution)/shard_map/project/pallas_call | solution.py:483
  58.4 1.1 collective-permute-start.16
  60.1 1.3 collective-permute-done.16.refs_1_
  61.4 6.4 %attend.2 = (f32[512,384]{1,0:T(8,128)S(1)}, bf16[512,384]{1,0:T(8,128)(2,1)S(1)}, f32[3,2,512]{2,1,0:T(2,128)S(1)}) custom-call(s32[25]{0:T(128)S(1)} %fusion.3.meta.order, bf16[1024,128]{1,0:T(8,128)(2,1)S(1)} %get-tuple-element.105.kmask, bf16[512,128]{1,0:T(8,128)(2,1)S(1)} %get-tuple-element.106.qmask, bf16[512,768]{1,0:T(8,128)(2,1)S(1)} %get-tuple-element.118.q_ref, ...), custom_call_target="tpu_custom_call" | custom-call | flops 9000000 | bytes 1024 | tf_op jit(solution)/shard_map/attend/pallas_call | solution.py:589
  70.0 2.3 %collective-permute-done.18.refs_8_ = bf16[528,768]{1,0:T(8,128)(2,1)S(1)} collective-permute-done((bf16[528,768]{1,0:T(8,128)(2,1)S(1)}, bf16[528,768]{1,0:T(8,128)(2,1)S(1)}, u32[]{:S(2)}, u32[]{:S(2)}) %collective-permute-start.18) | collective-permute-done | bytes 811040 | tf_op jit(solution)/shard_map/ppermute | solution.py:162
  72.3 6.4 %attend.3 = (f32[512,384]{1,0:T(8,128)S(1)}, bf16[512,384]{1,0:T(8,128)(2,1)S(1)}, f32[3,2,512]{2,1,0:T(2,128)S(1)}) custom-call(s32[25]{0:T(128)S(1)} %fusion.3.meta.order, bf16[1024,128]{1,0:T(8,128)(2,1)S(1)} %get-tuple-element.105.kmask, bf16[512,128]{1,0:T(8,128)(2,1)S(1)} %get-tuple-element.106.qmask, bf16[512,768]{1,0:T(8,128)(2,1)S(1)} %get-tuple-element.118.q_ref, ...), custom_call_target="tpu_custom_call" | custom-call | flops 9000000 | bytes 1024 | tf_op jit(solution)/shard_map/attend/pallas_call | solution.py:589
  79.6 1.2 collective-permute-done.20.refs_9_
  81.2 1.9 collective-permute-done.24.refs_13_
  83.2 1.1 copy-done.3
  84.3 1.0 copy-done.9
  85.3 33.9 %middle.1 = (bf16[128,768]{1,0:T(8,128)(2,1)S(1)}, bf16[128,768]{1,0:T(8,128)(2,1)S(1)}, bf16[128,768]{1,0:T(8,128)(2,1)S(1)}, bf16[128,768]{1,0:T(8,128)(2,1)S(...) custom-call(s32[25]{0:T(128)S(1)} %fusion.3.meta.order, ...), custom_call_target="tpu_custom_call" | custom-call | flops 20000000 | bytes 1024 | tf_op jit(solution)/shard_map/middle/pallas_call | solution.py:820
  119.8 3.5 %attend_back.3 = (bf16[512,128]{1,0:T(8,128)(2,1)S(1)}, bf16[2,512,128]{2,1,0:T(8,128)(2,1)S(1)}, bf16[2,512,128]{2,1,0:T(8,128)(2,1)S(1)}) custom-call(s32[25]{0:T(128)S(1)} %fusion.3.meta.order, bf16[1024,128]{1,0:T(8,128)(2,1)S(1)} %get-tuple-element.105.kmask, bf16[512,128]{1,0:T(8,128)(2,1)S(1)} %get-tuple-element.106.qmask, ...), custom_call_target="tpu_custom_call" | custom-call | flops 4000000 | bytes 1024 | tf_op jit(solution)/shard_map/attend_back/pallas_call | solution.py:674
  123.9 1.7 add_convert_fusion
  126.6 1.9 add_convert_fusion.1
  128.5 7.0 %attend_back.4 = (bf16[512,256]{1,0:T(8,128)(2,1)S(1)}, bf16[2,512,256]{2,1,0:T(8,128)(2,1)S(1)}, bf16[2,512,256]{2,1,0:T(8,128)(2,1)S(1)}) custom-call(s32[25]{0:T(128)S(1)} %fusion.3.meta.order, bf16[1024,128]{1,0:T(8,128)(2,1)S(1)} %get-tuple-element.105.kmask, bf16[512,128]{1,0:T(8,128)(2,1)S(1)} %get-tuple-element.106.qmask, ...), custom_call_target="tpu_custom_call" | custom-call | flops 8000000 | bytes 1024 | tf_op jit(solution)/shard_map/attend_back/pallas_call | solution.py:674
  135.6 10.3 %attend_back.5 = (bf16[512,384]{1,0:T(8,128)(2,1)S(1)}, bf16[2,512,384]{2,1,0:T(8,128)(2,1)S(1)}, bf16[2,512,384]{2,1,0:T(8,128)(2,1)S(1)}) custom-call(s32[25]{0:T(128)S(1)} %fusion.3.meta.order, bf16[1024,128]{1,0:T(8,128)(2,1)S(1)} %get-tuple-element.105.kmask, bf16[512,128]{1,0:T(8,128)(2,1)S(1)} %get-tuple-element.106.qmask, ...), custom_call_target="tpu_custom_call" | custom-call | flops 12000000 | bytes 1024 | tf_op jit(solution)/shard_map/attend_back/pallas_call | solution.py:674
  146.5 1.8 add_convert_fusion.5
  148.3 1.2 collective-permute-start.31
  149.4 6.1 %back_weight.1 = (bf16[3,512,768]{2,1,0:T(8,128)(2,1)S(1)}, bf16[2,96,2304]{2,1,0:T(8,128)(2,1)S(1)}, bf16[2,96,2304]{2,1,0:T(8,128)(2,1)S(1)}, bf16[2,96,2304]{2,1,0:T(8,128)(2,1)S(1)}, bf16[2,96,2304]{2,1,0:T(8,128)(2,1)S(1)}) custom-call(s32[25]{0:T(128)S(1)} %fusion.3.meta.order, f32[512,128]{1,0:T(8,128)S(1)} %get-tuple-element.205.cos_ref.refs_0_, ...), custom_call_target="tpu_custom_call" | custom-call | flops 6000000 | bytes 1024 | tf_op jit(solution)/shard_map/back_weight/pallas_call | solution.py:907
  156.1 3.6 %collective-permute-done.31 = bf16[1,528,768]{2,1,0:T(8,128)(2,1)S(1)} collective-permute-done((bf16[1,528,768]{2,1,0:T(8,128)(2,1)S(1)}, bf16[1,528,768]{2,1,0:T(8,128)(2,1)S(1)}, u32[]{:S(2)}, u32[]{:S(2)}) %collective-permute-start.31) | collective-permute-done | bytes 811040 | tf_op jit(solution)/shard_map/ppermute | solution.py:185
  160.2 1.0 collective-permute-start.36
  162.2 1.2 collective-permute-start.35
  163.7 5.6 %back_in.1 = (bf16[2,128,768]{2,1,0:T(8,128)(2,1)S(1)}, bf16[2,128,768]{2,1,0:T(8,128)(2,1)S(1)}, bf16[2,128,768]{2,1,0:T(8,128)(2,1)S(1)}, bf16[2,128,768]{2,1,0:T(8,128)(2,1)S(1)}) custom-call(s32[25]{0:T(128)S(1)} %fusion.3.meta.order, bf16[3,512,768]{2,1,0:T(8,128)(2,1)S(1)} %get-tuple-element.153.dp_ref, f32[512,768]{1,0:T(8,128)S(1)} %copy-done.1, ...), custom_call_target="tpu_custom_call" | custom-call | flops 7000000 | bytes 1024 | tf_op jit(solution)/shard_map/back_in/pallas_call | solution.py:956
  169.3 3.0 %collective-permute-done.35.refs_2_ = bf16[288,384]{1,0:T(8,128)(2,1)S(1)} collective-permute-done((bf16[288,384]{1,0:T(8,128)(2,1)S(1)}, bf16[288,384]{1,0:T(8,128)(2,1)S(1)}, u32[]{:S(2)}, u32[]{:S(2)}) %collective-permute-start.35) | collective-permute-done | bytes 221216 | tf_op jit(solution)/shard_map/ppermute | solution.py:1085
  172.7 1.2 collective-permute-start.38
  174.1 11.6 %collective-permute-done.37.refs_3_ = bf16[288,384]{1,0:T(8,128)(2,1)S(1)} collective-permute-done((bf16[288,384]{1,0:T(8,128)(2,1)S(1)}, bf16[288,384]{1,0:T(8,128)(2,1)S(1)}, u32[]{:S(2)}, u32[]{:S(2)}) %collective-permute-start.37) | collective-permute-done | bytes 221216 | tf_op jit(solution)/shard_map/ppermute | solution.py:1085
  185.8 1.1 collective-permute-start.41
  188.3 1.1 collective-permute-start.40
  190.9 6.1 %collective-permute-done.41.refs_3_ = bf16[2,128,768]{2,1,0:T(8,128)(2,1)S(1)} collective-permute-done((bf16[2,128,768]{2,1,0:T(8,128)(2,1)S(1)}, bf16[2,128,768]{2,1,0:T(8,128)(2,1)S(1)}, u32[]{:S(2)}, u32[]{:S(2)}) %collective-permute-start.41) | collective-permute-done | bytes 393248 | tf_op jit(solution)/shard_map/ppermute | solution.py:155
  197.6 8.7 %collective-permute-done.40.refs_2_ = bf16[2,128,768]{2,1,0:T(8,128)(2,1)S(1)} collective-permute-done((bf16[2,128,768]{2,1,0:T(8,128)(2,1)S(1)}, bf16[2,128,768]{2,1,0:T(8,128)(2,1)S(1)}, u32[]{:S(2)}, u32[]{:S(2)}) %collective-permute-start.40) | collective-permute-done | bytes 393248 | tf_op jit(solution)/shard_map/ppermute | solution.py:155
  206.3 1.8 place_rows.1
  (132 shorter events, 24.2 us)
Async XLA Ops:
  0.6 16.4 %copy-start.18 = (s32[4,8]{1,0:T(4,128)S(1)}, s32[4,8]{1,0:T(4,128)}, u32[]{:S(2)}) copy-start(s32[4,8]{1,0:T(4,128)} %lengths.1) | copy-start | bytes 388
  0.6 17.1 %copy-start.21 = (bf16[96]{0:T(256)(128)(2,1)S(1)}, bf16[96]{0:T(256)(128)(2,1)}, u32[]{:S(2)}) copy-start(bf16[96]{0:T(256)(128)(2,1)} %param.12) | copy-start | bytes 580
  0.7 17.1 %copy-start.20 = (bf16[96]{0:T(256)(128)(2,1)S(1)}, bf16[96]{0:T(256)(128)(2,1)}, u32[]{:S(2)}) copy-start(bf16[96]{0:T(256)(128)(2,1)} %param.15) | copy-start | bytes 580
  0.7 16.8 %collective-permute-start.1 = (bf16[96,576]{1,0:T(8,128)(2,1)}, bf16[96,576]{1,0:T(8,128)(2,1)S(1)}, u32[]{:S(2)}, u32[]{:S(2)}) collective-permute-start(bf16[96,576]{1,0:T(8,128)(2,1)} %refs_0_.1), channel_id=1, source_target_pairs={{0,16},{8,24},{16,0},{24,8},{1,17},{9,25},{17,1},{25,9},{2,18},{10... | collective-permute-start | bytes 331784 | tf_op jit(solution)/shard_map/ppermute | solution.py:149
  0.7 17.2 %collective-permute-start.2 = (bf16[96,576]{1,0:T(8,128)(2,1)}, bf16[96,576]{1,0:T(8,128)(2,1)S(1)}, u32[]{:S(2)}, u32[]{:S(2)}) collective-permute-start(bf16[96,576]{1,0:T(8,128)(2,1)} %refs_0_.1), channel_id=1, source_target_pairs={{0,24},{8,16},{16,8},{24,0},{1,25},{9,17},{17,9},{25,1},{2,26},{10... | collective-permute-start | bytes 331784 | tf_op jit(solution)/shard_map/ppermute | solution.py:149
  3.2 14.7 %collective-permute-start = (bf16[96,576]{1,0:T(8,128)(2,1)}, bf16[96,576]{1,0:T(8,128)(2,1)S(1)}, u32[]{:S(2)}, u32[]{:S(2)}) collective-permute-start(bf16[96,576]{1,0:T(8,128)(2,1)} %refs_0_.1), channel_id=1, source_target_pairs={{0,8},{8,0},{16,24},{24,16},{1,9},{9,1},{17,25},{25,17},{2,10},{10... | collective-permute-start | bytes 331784 | tf_op jit(solution)/shard_map/ppermute | solution.py:149
  11.3 10.2 %collective-permute-start.10 = (bf16[2,128,768]{2,1,0:T(8,128)(2,1)}, bf16[2,128,768]{2,1,0:T(8,128)(2,1)S(1)}, u32[]{:S(2)}, u32[]{:S(2)}) collective-permute-start(bf16[2,128,768]{2,1,0:T(8,128)(2,1)} %get-tuple-element.110), channel_id=1, source_target_pairs={{0,6},{1,7},{2,4},{3,5},{4,2},{5,3},{6,0},{7,1},{8,14},{9,15},{10,... | collective-permute-start | bytes 1179656 | tf_op jit(solution)/shard_map/ppermute | solution.py:155
  13.4 16.6 %collective-permute-start.8 = (bf16[2,128,768]{2,1,0:T(8,128)(2,1)S(1)}, bf16[2,128,768]{2,1,0:T(8,128)(2,1)S(1)}, u32[]{:S(2)}, u32[]{:S(2)}) collective-permute-start(bf16[2,128,768]{2,1,0:T(8,128)(2,1)S(1)} %get-tuple-element.108), channel_id=1, source_target_pairs={{0,2},{1,3},{2,0},{3,1},{4,6},{5,7},{6,4},{7,5},{8,10},{9,11},{10,... | collective-permute-start | bytes 1179656 | tf_op jit(solution)/shard_map/ppermute | solution.py:155
  17.5 13.7 %collective-permute-start.9 = (bf16[2,128,768]{2,1,0:T(8,128)(2,1)S(1)}, bf16[2,128,768]{2,1,0:T(8,128)(2,1)S(1)}, u32[]{:S(2)}, u32[]{:S(2)}) collective-permute-start(bf16[2,128,768]{2,1,0:T(8,128)(2,1)S(1)} %get-tuple-element.109), channel_id=1, source_target_pairs={{0,4},{1,5},{2,6},{3,7},{4,0},{5,1},{6,2},{7,3},{8,12},{9,13},{10,... | collective-permute-start | bytes 1179656 | tf_op jit(solution)/shard_map/ppermute | solution.py:155
  18.7 22.1 %collective-permute-start.4 = (bf16[96,2432]{1,0:T(8,128)(2,1)S(1)}, bf16[96,2432]{1,0:T(8,128)(2,1)S(1)}, u32[]{:S(2)}, u32[]{:S(2)}) collective-permute-start(bf16[96,2432]{1,0:T(8,128)(2,1)S(1)} %join_qkv.1.refs_4_.refs_8_.weight), channel_id=1, source_target_pairs={{0,2},{1,5},{2,0},{3,7},{4,6},{5,1},{6,4},{7,3},{8,10},{9,13},{10,... | collective-permute-start | bytes 1400840 | tf_op jit(solution)/shard_map/ppermute | solution.py:161
  20.0 14.0 %collective-permute-start.5 = (bf16[288,384]{1,0:T(8,128)(2,1)S(1)}, bf16[288,384]{1,0:T(8,128)(2,1)S(1)}, u32[]{:S(2)}, u32[]{:S(2)}) collective-permute-start(bf16[288,384]{1,0:T(8,128)(2,1)S(1)} %get-tuple-element.113.refs_0_), channel_id=1, source_target_pairs={{0,16},{8,24},{16,0},{24,8},{1,17},{9,25},{17,1},{25,9},{2,18},{10... | collective-permute-start | bytes 663560 | tf_op jit(solution)/shard_map/ppermute | solution.py:149
  21.5 19.3 %collective-permute-start.6 = (bf16[288,384]{1,0:T(8,128)(2,1)S(1)}, bf16[288,384]{1,0:T(8,128)(2,1)S(1)}, u32[]{:S(2)}, u32[]{:S(2)}) collective-permute-start(bf16[288,384]{1,0:T(8,128)(2,1)S(1)} %get-tuple-element.113.refs_0_), channel_id=1, source_target_pairs={{0,24},{8,16},{16,8},{24,0},{1,25},{9,17},{17,9},{25,1},{2,26},{10... | collective-permute-start | bytes 663560 | tf_op jit(solution)/shard_map/ppermute | solution.py:149
  31.2 11.5 %collective-permute-start.11 = (bf16[96,2432]{1,0:T(8,128)(2,1)S(1)}, bf16[96,2432]{1,0:T(8,128)(2,1)S(1)}, u32[]{:S(2)}, u32[]{:S(2)}) collective-permute-start(bf16[96,2432]{1,0:T(8,128)(2,1)S(1)} %join_qkv.1.refs_4_.refs_8_.weight), channel_id=1, source_target_pairs={{0,4},{1,3},{2,6},{3,1},{4,0},{5,7},{6,2},{7,5},{8,12},{9,11},{10,... | collective-permute-start | bytes 1400840 | tf_op jit(solution)/shard_map/ppermute | solution.py:162
  40.8 7.7 %collective-permute-start.14 = (bf16[96,2432]{1,0:T(8,128)(2,1)S(1)}, bf16[96,2432]{1,0:T(8,128)(2,1)S(1)}, u32[]{:S(2)}, u32[]{:S(2)}) collective-permute-start(bf16[96,2432]{1,0:T(8,128)(2,1)S(1)} %collective-permute-done.4.refs_5_.refs_9_), channel_id=1, source_target_pairs={{0,4},{1,3},{2,6},{3,1},{4,0},{5,7},{6,2},{7,5},{8,12},{9,11},{10,... | collective-permute-start | bytes 1400840 | tf_op jit(solution)/shard_map/ppermute | solution.py:170
  42.0 6.3 %collective-permute-start.13 = (bf16[288,384]{1,0:T(8,128)(2,1)S(1)}, bf16[288,384]{1,0:T(8,128)(2,1)S(1)}, u32[]{:S(2)}, u32[]{:S(2)}) collective-permute-start(bf16[288,384]{1,0:T(8,128)(2,1)S(1)} %get-tuple-element.113.refs_0_), channel_id=1, source_target_pairs={{0,8},{8,0},{16,24},{24,16},{1,9},{9,1},{17,25},{25,17},{2,10},{10... | collective-permute-start | bytes 663560 | tf_op jit(solution)/shard_map/ppermute | solution.py:149
  42.0 8.7 %collective-permute-start.3 = (bf16[96,2432]{1,0:T(8,128)(2,1)S(1)}, bf16[96,2432]{1,0:T(8,128)(2,1)S(1)}, u32[]{:S(2)}, u32[]{:S(2)}) collective-permute-start(bf16[96,2432]{1,0:T(8,128)(2,1)S(1)} %join_qkv.1.refs_4_.refs_8_.weight), channel_id=1, source_target_pairs={{0,1},{1,0},{2,3},{3,2},{4,5},{5,4},{6,7},{7,6},{8,9},{9,8},{10,11... | collective-permute-start | bytes 1400840 | tf_op jit(solution)/shard_map/ppermute | solution.py:142
  42.7 8.1 %collective-permute-start.7 = (bf16[96,2432]{1,0:T(8,128)(2,1)S(1)}, bf16[96,2432]{1,0:T(8,128)(2,1)S(1)}, u32[]{:S(2)}, u32[]{:S(2)}) collective-permute-start(bf16[96,2432]{1,0:T(8,128)(2,1)S(1)} %collective-permute-done.4.refs_5_.refs_9_), channel_id=1, source_target_pairs={{0,1},{1,0},{2,3},{3,2},{4,5},{5,4},{6,7},{7,6},{8,9},{9,8},{10,11... | collective-permute-start | bytes 1400840 | tf_op jit(solution)/shard_map/ppermute | solution.py:142
  42.7 8.1 %collective-permute-start.12 = (bf16[96,2432]{1,0:T(8,128)(2,1)S(1)}, bf16[96,2432]{1,0:T(8,128)(2,1)S(1)}, u32[]{:S(2)}, u32[]{:S(2)}) collective-permute-start(bf16[96,2432]{1,0:T(8,128)(2,1)S(1)} %collective-permute-done.11.refs_6_.refs_10_), channel_id=1, source_target_pairs={{0,1},{1,0},{2,3},{3,2},{4,5},{5,4},{6,7},{7,6},{8,9},{9,8},{10,11... | collective-permute-start | bytes 1400840 | tf_op jit(solution)/shard_map/ppermute | solution.py:142
  48.5 3.7 %collective-permute-start.15 = (bf16[96,2432]{1,0:T(8,128)(2,1)S(1)}, bf16[96,2432]{1,0:T(8,128)(2,1)S(1)}, u32[]{:S(2)}, u32[]{:S(2)}) collective-permute-start(bf16[96,2432]{1,0:T(8,128)(2,1)S(1)} %collective-permute-done.14.refs_7_.refs_11_), channel_id=1, source_target_pairs={{0,1},{1,0},{2,3},{3,2},{4,5},{5,4},{6,7},{7,6},{8,9},{9,8},{10,11... | collective-permute-start | bytes 1400840 | tf_op jit(solution)/shard_map/ppermute | solution.py:142
  51.6 17.0 %collective-permute-start.17 = (bf16[528,768]{1,0:T(8,128)(2,1)S(1)}, bf16[528,768]{1,0:T(8,128)(2,1)S(1)}, u32[]{:S(2)}, u32[]{:S(2)}) collective-permute-start(bf16[528,768]{1,0:T(8,128)(2,1)S(1)} %join_rest.1.refs_6_.weight), channel_id=1, source_target_pairs={{0,2},{1,5},{2,0},{3,7},{4,6},{5,1},{6,4},{7,3},{8,10},{9,13},{10,... | collective-permute-start | bytes 2433032 | tf_op jit(solution)/shard_map/ppermute | solution.py:161
  58.4 3.0 %collective-permute-start.16 = (bf16[2,512,384]{2,1,0:T(8,128)(2,1)S(1)}, bf16[2,512,384]{2,1,0:T(8,128)(2,1)S(1)}, u32[]{:S(2)}, u32[]{:S(2)}) collective-permute-start(bf16[2,512,384]{2,1,0:T(8,128)(2,1)S(1)} %get-tuple-element.119.refs_0_), channel_id=1, source_target_pairs={{0,1},{1,0},{2,3},{3,2},{4,5},{5,4},{6,7},{7,6},{8,9},{9,8},{10,11... | collective-permute-start | bytes 2359304 | tf_op jit(solution)/shard_map/ppermute | solution.py:1214
  59.5 12.7 %collective-permute-start.18 = (bf16[528,768]{1,0:T(8,128)(2,1)S(1)}, bf16[528,768]{1,0:T(8,128)(2,1)S(1)}, u32[]{:S(2)}, u32[]{:S(2)}) collective-permute-start(bf16[528,768]{1,0:T(8,128)(2,1)S(1)} %join_rest.1.refs_6_.weight), channel_id=1, source_target_pairs={{0,4},{1,3},{2,6},{3,1},{4,0},{5,7},{6,2},{7,5},{8,12},{9,11},{10,... | collective-permute-start | bytes 2433032 | tf_op jit(solution)/shard_map/ppermute | solution.py:162
  68.6 12.2 %collective-permute-start.20 = (bf16[528,768]{1,0:T(8,128)(2,1)S(1)}, bf16[528,768]{1,0:T(8,128)(2,1)S(1)}, u32[]{:S(2)}, u32[]{:S(2)}) collective-permute-start(bf16[528,768]{1,0:T(8,128)(2,1)S(1)} %collective-permute-done.17.refs_7_), channel_id=1, source_target_pairs={{0,4},{1,3},{2,6},{3,1},{4,0},{5,7},{6,2},{7,5},{8,12},{9,11},{10,... | collective-permute-start | bytes 2433032 | tf_op jit(solution)/shard_map/ppermute | solution.py:170
  69.2 3.1 %collective-permute-start.19 = (bf16[2,512,384]{2,1,0:T(8,128)(2,1)S(1)}, bf16[2,512,384]{2,1,0:T(8,128)(2,1)S(1)}, u32[]{:S(2)}, u32[]{:S(2)}) collective-permute-start(bf16[2,512,384]{2,1,0:T(8,128)(2,1)S(1)} %get-tuple-element.122.refs_0_), channel_id=1, source_target_pairs={{0,1},{1,0},{2,3},{3,2},{4,5},{5,4},{6,7},{7,6},{8,9},{9,8},{10,11... | collective-permute-start | bytes 2359304 | tf_op jit(solution)/shard_map/ppermute | solution.py:1214
  69.5 11.7 %collective-permute-start.21 = (bf16[528,768]{1,0:T(8,128)(2,1)S(1)}, bf16[528,768]{1,0:T(8,128)(2,1)S(1)}, u32[]{:S(2)}, u32[]{:S(2)}) collective-permute-start(bf16[528,768]{1,0:T(8,128)(2,1)S(1)} %join_rest.1.refs_6_.weight), channel_id=1, source_target_pairs={{0,1},{1,0},{2,3},{3,2},{4,5},{5,4},{6,7},{7,6},{8,9},{9,8},{10,11... | collective-permute-start | bytes 2433032 | tf_op jit(solution)/shard_map/ppermute | solution.py:142
  69.7 11.5 %collective-permute-start.22 = (bf16[528,768]{1,0:T(8,128)(2,1)S(1)}, bf16[528,768]{1,0:T(8,128)(2,1)S(1)}, u32[]{:S(2)}, u32[]{:S(2)}) collective-permute-start(bf16[528,768]{1,0:T(8,128)(2,1)S(1)} %collective-permute-done.17.refs_7_), channel_id=1, source_target_pairs={{0,1},{1,0},{2,3},{3,2},{4,5},{5,4},{6,7},{7,6},{8,9},{9,8},{10,11... | collective-permute-start | bytes 2433032 | tf_op jit(solution)/shard_map/ppermute | solution.py:142
  72.2 9.0 %collective-permute-start.23 = (bf16[528,768]{1,0:T(8,128)(2,1)S(1)}, bf16[528,768]{1,0:T(8,128)(2,1)S(1)}, u32[]{:S(2)}, u32[]{:S(2)}) collective-permute-start(bf16[528,768]{1,0:T(8,128)(2,1)S(1)} %collective-permute-done.18.refs_8_), channel_id=1, source_target_pairs={{0,1},{1,0},{2,3},{3,2},{4,5},{5,4},{6,7},{7,6},{8,9},{9,8},{10,11... | collective-permute-start | bytes 2433032 | tf_op jit(solution)/shard_map/ppermute | solution.py:142
  80.8 2.3 %collective-permute-start.24 = (bf16[528,768]{1,0:T(8,128)(2,1)S(1)}, bf16[528,768]{1,0:T(8,128)(2,1)S(1)}, u32[]{:S(2)}, u32[]{:S(2)}) collective-permute-start(bf16[528,768]{1,0:T(8,128)(2,1)S(1)} %collective-permute-done.20.refs_9_), channel_id=1, source_target_pairs={{0,1},{1,0},{2,3},{3,2},{4,5},{5,4},{6,7},{7,6},{8,9},{9,8},{10,11... | collective-permute-start | bytes 2433032 | tf_op jit(solution)/shard_map/ppermute | solution.py:142
  119.2 4.7 %collective-permute-start.26 = (bf16[2,528,768]{2,1,0:T(8,128)(2,1)}, bf16[2,528,768]{2,1,0:T(8,128)(2,1)S(1)}, u32[]{:S(2)}, u32[]{:S(2)}) collective-permute-start(bf16[2,528,768]{2,1,0:T(8,128)(2,1)} %get-tuple-element.136), channel_id=1, source_target_pairs={{0,1},{1,0},{2,3},{3,2},{4,5},{5,4},{6,7},{7,6},{8,9},{9,8},{10,11... | collective-permute-start | bytes 4866056 | tf_op jit(solution)/shard_map/ppermute | solution.py:142
  119.7 7.0 %collective-permute-start.25 = (bf16[2,528,768]{2,1,0:T(8,128)(2,1)}, bf16[2,528,768]{2,1,0:T(8,128)(2,1)}, u32[]{:S(2)}, u32[]{:S(2)}) collective-permute-start(bf16[2,528,768]{2,1,0:T(8,128)(2,1)} %get-tuple-element.133), channel_id=1, source_target_pairs={{0,1},{1,0},{2,3},{3,2},{4,5},{5,4},{6,7},{7,6},{8,9},{9,8},{10,11... | collective-permute-start | bytes 4866056 | tf_op jit(solution)/shard_map/ppermute | solution.py:142
  125.6 20.9 %collective-permute-start.28 = (bf16[2,528,768]{2,1,0:T(8,128)(2,1)}, bf16[2,528,768]{2,1,0:T(8,128)(2,1)}, u32[]{:S(2)}, u32[]{:S(2)}) collective-permute-start(bf16[2,528,768]{2,1,0:T(8,128)(2,1)} %add_convert_fusion), channel_id=1, source_target_pairs={{0,4},{1,3},{2,6},{3,1},{4,0},{5,7},{6,2},{7,5},{8,12},{9,11},{10,... | collective-permute-start | bytes 4866056 | tf_op jit(solution)/shard_map/ppermute | solution.py:185
  126.0 9.5 %collective-permute-start.27 = (bf16[2,512,128]{2,1,0:T(8,128)(2,1)S(1)}, bf16[2,512,128]{2,1,0:T(8,128)(2,1)S(1)}, u32[]{:S(2)}, u32[]{:S(2)}) collective-permute-start(bf16[2,512,128]{2,1,0:T(8,128)(2,1)S(1)} %get-tuple-element.139), channel_id=1, source_target_pairs={{0,1},{1,0},{2,3},{3,2},{4,5},{5,4},{6,7},{7,6},{8,9},{9,8},{10,11... | collective-permute-start | bytes 786440 | tf_op jit(solution)/shard_map/ppermute | solution.py:1254
  145.9 3.5 %collective-permute-start.30 = (bf16[2,512,384]{2,1,0:T(8,128)(2,1)S(1)}, bf16[2,512,384]{2,1,0:T(8,128)(2,1)S(1)}, u32[]{:S(2)}, u32[]{:S(2)}) collective-permute-start(bf16[2,512,384]{2,1,0:T(8,128)(2,1)S(1)} %get-tuple-element.151), channel_id=1, source_target_pairs={{0,1},{1,0},{2,3},{3,2},{4,5},{5,4},{6,7},{7,6},{8,9},{9,8},{10,11... | collective-permute-start | bytes 2359304 | tf_op jit(solution)/shard_map/ppermute | solution.py:1254
  146.0 3.4 %collective-permute-start.29 = (bf16[2,512,256]{2,1,0:T(8,128)(2,1)S(1)}, bf16[2,512,256]{2,1,0:T(8,128)(2,1)S(1)}, u32[]{:S(2)}, u32[]{:S(2)}) collective-permute-start(bf16[2,512,256]{2,1,0:T(8,128)(2,1)S(1)} %get-tuple-element.149), channel_id=1, source_target_pairs={{0,1},{1,0},{2,3},{3,2},{4,5},{5,4},{6,7},{7,6},{8,9},{9,8},{10,11... | collective-permute-start | bytes 1572872 | tf_op jit(solution)/shard_map/ppermute | solution.py:1254
  148.3 11.5 %collective-permute-start.31 = (bf16[1,528,768]{2,1,0:T(8,128)(2,1)S(1)}, bf16[1,528,768]{2,1,0:T(8,128)(2,1)S(1)}, u32[]{:S(2)}, u32[]{:S(2)}) collective-permute-start(bf16[1,528,768]{2,1,0:T(8,128)(2,1)S(1)} %get-tuple-element.196), channel_id=1, source_target_pairs={{0,2},{1,5},{2,0},{3,7},{4,6},{5,1},{6,4},{7,3},{8,10},{9,13},{10,... | collective-permute-start | bytes 2433032 | tf_op jit(solution)/shard_map/ppermute | solution.py:185
  155.5 4.4 %collective-permute-start.32 = (bf16[2,96,2304]{2,1,0:T(8,128)(2,1)S(1)}, bf16[2,96,2304]{2,1,0:T(8,128)(2,1)S(1)}, u32[]{:S(2)}, u32[]{:S(2)}) collective-permute-start(bf16[2,96,2304]{2,1,0:T(8,128)(2,1)S(1)} %get-tuple-element.156), channel_id=1, source_target_pairs={{0,1},{1,0},{2,3},{3,2},{4,5},{5,4},{6,7},{7,6},{8,9},{9,8},{10,11... | collective-permute-start | bytes 2654216 | tf_op jit(solution)/shard_map/ppermute | solution.py:142
  155.8 7.6 %collective-permute-start.33 = (bf16[2,96,2304]{2,1,0:T(8,128)(2,1)S(1)}, bf16[2,96,2304]{2,1,0:T(8,128)(2,1)S(1)}, u32[]{:S(2)}, u32[]{:S(2)}) collective-permute-start(bf16[2,96,2304]{2,1,0:T(8,128)(2,1)S(1)} %get-tuple-element.158), channel_id=1, source_target_pairs={{0,1},{1,0},{2,3},{3,2},{4,5},{5,4},{6,7},{7,6},{8,9},{9,8},{10,11... | collective-permute-start | bytes 2654216 | tf_op jit(solution)/shard_map/ppermute | solution.py:142
  160.2 12.3 %collective-permute-start.36 = (bf16[2,96,2304]{2,1,0:T(8,128)(2,1)S(1)}, bf16[2,96,2304]{2,1,0:T(8,128)(2,1)S(1)}, u32[]{:S(2)}, u32[]{:S(2)}) collective-permute-start(bf16[2,96,2304]{2,1,0:T(8,128)(2,1)S(1)} %add_convert_fusion.3), channel_id=1, source_target_pairs={{0,4},{1,3},{2,6},{3,1},{4,0},{5,7},{6,2},{7,5},{8,12},{9,11},{10,... | collective-permute-start | bytes 2654216 | tf_op jit(solution)/shard_map/ppermute | solution.py:185
  162.2 7.1 %collective-permute-start.34 = (bf16[288,384]{1,0:T(8,128)(2,1)S(1)}, bf16[288,384]{1,0:T(8,128)(2,1)S(1)}, u32[]{:S(2)}, u32[]{:S(2)}) collective-permute-start(bf16[288,384]{1,0:T(8,128)(2,1)S(1)} %get-tuple-element.161), channel_id=1, source_target_pairs={{0,8},{8,0},{16,24},{24,16},{1,9},{9,1},{17,25},{25,17},{2,10},{10... | collective-permute-start | bytes 663560 | tf_op jit(solution)/shard_map/ppermute | solution.py:1085
  162.2 10.1 %collective-permute-start.35 = (bf16[288,384]{1,0:T(8,128)(2,1)S(1)}, bf16[288,384]{1,0:T(8,128)(2,1)S(1)}, u32[]{:S(2)}, u32[]{:S(2)}) collective-permute-start(bf16[288,384]{1,0:T(8,128)(2,1)S(1)} %get-tuple-element.162), channel_id=1, source_target_pairs={{0,16},{8,24},{16,0},{24,8},{1,17},{9,25},{17,1},{25,9},{2,18},{10... | collective-permute-start | bytes 663560 | tf_op jit(solution)/shard_map/ppermute | solution.py:1085
  172.7 13.1 %collective-permute-start.38 = (bf16[1,96,2304]{2,1,0:T(8,128)(2,1)S(1)}, bf16[1,96,2304]{2,1,0:T(8,128)(2,1)S(1)}, u32[]{:S(2)}, u32[]{:S(2)}) collective-permute-start(bf16[1,96,2304]{2,1,0:T(8,128)(2,1)S(1)} %get-tuple-element.199), channel_id=1, source_target_pairs={{0,2},{1,5},{2,0},{3,7},{4,6},{5,1},{6,4},{7,3},{8,10},{9,13},{10,... | collective-permute-start | bytes 1327112 | tf_op jit(solution)/shard_map/ppermute | solution.py:185
  173.8 11.9 %collective-permute-start.37 = (bf16[288,384]{1,0:T(8,128)(2,1)S(1)}, bf16[288,384]{1,0:T(8,128)(2,1)S(1)}, u32[]{:S(2)}, u32[]{:S(2)}) collective-permute-start(bf16[288,384]{1,0:T(8,128)(2,1)S(1)} %get-tuple-element.163), channel_id=1, source_target_pairs={{0,24},{8,16},{16,8},{24,0},{1,25},{9,17},{17,9},{25,1},{2,26},{10... | collective-permute-start | bytes 663560 | tf_op jit(solution)/shard_map/ppermute | solution.py:1085
  185.8 11.1 %collective-permute-start.41 = (bf16[2,128,768]{2,1,0:T(8,128)(2,1)S(1)}, bf16[2,128,768]{2,1,0:T(8,128)(2,1)S(1)}, u32[]{:S(2)}, u32[]{:S(2)}) collective-permute-start(bf16[2,128,768]{2,1,0:T(8,128)(2,1)S(1)} %get-tuple-element.185), channel_id=1, source_target_pairs={{0,6},{1,7},{2,4},{3,5},{4,2},{5,3},{6,0},{7,1},{8,14},{9,15},{10,... | collective-permute-start | bytes 1179656 | tf_op jit(solution)/shard_map/ppermute | solution.py:155
  187.8 20.2 %collective-permute-start.42 = (bf16[96,640]{1,0:T(8,128)(2,1)S(1)}, bf16[96,640]{1,0:T(8,128)(2,1)S(1)}, u32[]{:S(2)}, u32[]{:S(2)}) collective-permute-start(bf16[96,640]{1,0:T(8,128)(2,1)S(1)} %get-tuple-element.176), channel_id=1, source_target_pairs={{0,8},{8,0},{16,24},{24,16},{1,9},{9,1},{17,25},{25,17},{2,10},{10... | collective-permute-start | bytes 368648 | tf_op jit(solution)/shard_map/ppermute | solution.py:1085
  187.9 20.2 %collective-permute-start.43 = (bf16[96,640]{1,0:T(8,128)(2,1)S(1)}, bf16[96,640]{1,0:T(8,128)(2,1)S(1)}, u32[]{:S(2)}, u32[]{:S(2)}) collective-permute-start(bf16[96,640]{1,0:T(8,128)(2,1)S(1)} %get-tuple-element.177), channel_id=1, source_target_pairs={{0,16},{8,24},{16,0},{24,8},{1,17},{9,25},{17,1},{25,9},{2,18},{10... | collective-permute-start | bytes 368648 | tf_op jit(solution)/shard_map/ppermute | solution.py:1085
  188.3 17.9 %collective-permute-start.40 = (bf16[2,128,768]{2,1,0:T(8,128)(2,1)S(1)}, bf16[2,128,768]{2,1,0:T(8,128)(2,1)S(1)}, u32[]{:S(2)}, u32[]{:S(2)}) collective-permute-start(bf16[2,128,768]{2,1,0:T(8,128)(2,1)S(1)} %get-tuple-element.183), channel_id=1, source_target_pairs={{0,4},{1,5},{2,6},{3,7},{4,0},{5,1},{6,2},{7,3},{8,12},{9,13},{10,... | collective-permute-start | bytes 1179656 | tf_op jit(solution)/shard_map/ppermute | solution.py:155
  189.4 16.8 %collective-permute-start.39 = (bf16[2,128,768]{2,1,0:T(8,128)(2,1)S(1)}, bf16[2,128,768]{2,1,0:T(8,128)(2,1)S(1)}, u32[]{:S(2)}, u32[]{:S(2)}) collective-permute-start(bf16[2,128,768]{2,1,0:T(8,128)(2,1)S(1)} %get-tuple-element.181), channel_id=1, source_target_pairs={{0,2},{1,3},{2,0},{3,1},{4,6},{5,7},{6,4},{7,5},{8,10},{9,11},{10,... | collective-permute-start | bytes 1179656 | tf_op jit(solution)/shard_map/ppermute | solution.py:155
  197.0 11.1 %collective-permute-start.44 = (bf16[96,640]{1,0:T(8,128)(2,1)S(1)}, bf16[96,640]{1,0:T(8,128)(2,1)S(1)}, u32[]{:S(2)}, u32[]{:S(2)}) collective-permute-start(bf16[96,640]{1,0:T(8,128)(2,1)S(1)} %get-tuple-element.178), channel_id=1, source_target_pairs={{0,24},{8,16},{16,8},{24,0},{1,25},{9,17},{17,9},{25,1},{2,26},{10... | collective-permute-start | bytes 368648 | tf_op jit(solution)/shard_map/ppermute | solution.py:1085
  (19 other events, 55.8 us)
where the time goes:
time: 213 us; the launch traced here: 209 us
  Pallas kernels  94.9 us (45%)
  waiting for transfers between devices  62.9 us (30%)
  starting transfers between devices  28.2 us (13%)
  local copies, waits for them, and re-layouts  10.8 us (5%)
  other arithmetic  8.89 us (4%)
  between operations  3.33 us (2%)
    pallas_call x1, Pallas kernels, middle(): pl.pallas_call(functools.partial(middle_kernel, plan), in_specs=[SMEM, VM...  33.9 us
    ppermute x6, waiting for transfers between devices, exchange_rows(): lax.ppermute(pieces[j], 'blk', plan.xor_pairs(2 * j))  24.7 us
    pallas_call x3, Pallas kernels, attend_back(): pl.pallas_call(functools.partial(attend_back_kernel, plan, width), grid=(...  20.9 us
    ppermute x6, waiting for transfers between devices, reduce_z(): lax.ppermute(pieces[j], 'row', plan.z_pairs(j))  14.7 us
    pallas_call x2, Pallas kernels, attend(): pl.pallas_call(functools.partial(attend_kernel, plan, width), grid=(HALF_...  12.9 us
    ppermute x6, waiting for transfers between devices, gather_z(): pieces.append(lax.ppermute(source, 'row', plan.z_pairs(j)))  12 us
    unnamed x44, local copies, waits for them, and re-layouts  8.66 us
    pallas_call x1, Pallas kernels, project(): pl.pallas_call(functools.partial(qkv_kernel, plan), in_specs=[SMEM, VMEM,...  6.24 us
  transfers between devices with their start and end apart: 45, of which 18 were waited for; matrix products, arithmetic and copies ran while one was open for 5% of the time, Pallas kernels for 29%

commit v1 on v0

--- a/solution.py
+++ b/solution.py
@@ -25,7 +25,23 @@
 NN = (((1,), (0,)), ((), ()))
 NT = (((1,), (1,)), ((), ()))
 TN = (((0,), (0,)), ((), ()))
-VMEM_BYTES = 40 * 1024 * 1024
+LIMITS = {
+    "prepare": 8,
+    "place_rows": 8,
+    "join_qkv": 4,
+    "join_rest": 6,
+    "project": 20,
+    "masks": 4,
+    "attend": 16,
+    "middle": 56,
+    "attend_back": 16,
+    "back_in": 20,
+    "back_weight": 16,
+    "cut_qkv": 4,
+    "cut_rest": 6,
+    "end_rest": 4,
+    "end_qkv": 4,
+}
 HALVES = 2
 HALF_PAIRS = PAIRS // HALVES
 HALF = D // HALVES
@@ -59,8 +75,9 @@
     return jax.ShapeDtypeStruct(tuple(dims), dtype)
 
 
-def params():
-    return pltpu.CompilerParams(vmem_limit_bytes=VMEM_BYTES)
+def params(plan, name):
+    size = max(1, plan.groups * plan.local // 1024)
+    return pltpu.CompilerParams(vmem_limit_bytes=min(56, LIMITS[name] * size) * 1024 * 1024)
 
 
 def cost(microseconds):
@@ -247,7 +264,7 @@
         in_specs=[SMEM] + [VMEM] * 5,
         out_specs=[VMEM] * len(shapes),
         out_shape=shapes,
-        compiler_params=params(),
+        compiler_params=params(plan, "prepare"),
         cost_estimate=cost(COSTS["prepare"]),
         name="prepare",
     )(meta, tokens, cotangent, w_out, w_in, w_down)
@@ -269,7 +286,7 @@
         in_specs=[SMEM] + [VMEM] * plan.rows,
         out_specs=[VMEM] * 2,
         out_shape=[shape_of((plan.rows, plan.tok, D), BF16)] * 2,
-        compiler_params=params(),
+        compiler_params=params(plan, "place_rows"),
         cost_estimate=cost(COSTS["place_rows"]),
         name="place_rows",
     )(meta, *pieces)
@@ -302,7 +319,7 @@
         out_specs=VMEM,
         out_shape=shape_of((plan.r, EXT), BF16),
         scratch_shapes=[pltpu.VMEM((plan.nrow, plan.r, 3 * plan.cw), BF16)],
-        compiler_params=params(),
+        compiler_params=params(plan, "join_qkv"),
         cost_estimate=cost(COSTS["join_qkv"]),
         name="join_qkv",
     )(meta, gains, *pieces)
@@ -351,7 +368,7 @@
         out_specs=VMEM,
         out_shape=shape_of((plan.packed, D), BF16),
         scratch_shapes=[pltpu.VMEM((plan.nrow, 3 * plan.r, 2 * plan.cw), BF16)],
-        compiler_params=params(),
+        compiler_params=params(plan, "join_rest"),
         cost_estimate=cost(COSTS["join_rest"]),
         name="join_rest",
     )(meta, *pieces)
@@ -488,7 +505,7 @@
         + [shape_of((2, local, HALF), BF16)] * HALVES
         + [shape_of((local, D), BF16), shape_of((8, D), F32)],
         scratch_shapes=[pltpu.VMEM((D, EXT), BF16), pltpu.SemaphoreType.DMA((count,))],
-        compiler_params=params(),
+        compiler_params=params(plan, "project"),
         cost_estimate=cost(COSTS["project"]),
         name="project",
     )(*inputs)
@@ -523,7 +540,7 @@
         in_specs=[SMEM, SMEM],
         out_specs=[VMEM, VMEM],
         out_shape=[shape_of((keys, 128), BF16), shape_of((plan.local, 128), BF16)],
-        compiler_params=params(),
+        compiler_params=params(plan, "masks"),
         cost_estimate=cost(1),
         name="masks",
     )(meta, lengths)
@@ -600,7 +617,7 @@
             pltpu.VMEM((2, groups * local, width), F32),
             pltpu.VMEM((2, groups * local, width), BF16),
         ],
-        compiler_params=params(),
+        compiler_params=params(plan, "attend"),
         cost_estimate=cost(COSTS["attend"]),
         name="attend",
     )(*inputs)
@@ -693,7 +710,7 @@
             pltpu.VMEM((2, groups, local, width), BF16),
             pltpu.VMEM((2, groups, local, width), BF16),
         ],
-        compiler_params=params(),
+        compiler_params=params(plan, "attend_back"),
         cost_estimate=cost(4 * count),
         name="attend_back",
     )(*inputs)
@@ -709,7 +726,7 @@
     do_out, dh_out, refs = refs[0], refs[1], refs[2:]
     grads, refs = refs[: 4 if plan.aligned else 1], refs[4 if plan.aligned else 1 :]
     low_ref, x_ref, dy_ref, w_out, w_in, w_down, h_ref, unit_ref, n_ref, gu_ref = refs[:10]
-    mid_ref, dgu_ref, out_ref, do_ref, dh_ref, da_ref, g_out, g_in, g_down, sems = refs[10:]
+    mid_ref, dgu_ref, out_ref, do_ref, dh_ref, da_ref, inv_ref, g_out, g_in, g_down, sems = refs[10:]
     mover = Mover(sems)
     r, rf = block_size(plan)
     blocks = [block_of(plan, meta, i) for i in range(count)]
@@ -728,82 +745,86 @@
             for source, block in zip(sources, blocks)
         ]
 
+    in_in = [fetch_in(t) for t in range(3)]
+    dy_in = [mover.start(x_refs[j].at[1], dy_ref.at[pl.ds(tok * j, tok)]) for j in range(rows)]
+    down_in = [
+        mover.start(source.at[pl.ds(4 * r, rf)], w_down.at[rows_at(block, rf)])
+        for source, block in zip(sources, blocks)
+    ]
     wait_all(low_in)
-    in_in = [fetch_in(0)]
     wait_all(out_in)
     wait_all(x_in)
-    in_in.append(fetch_in(1))
     gain = gain_ref[1:2, :]
-    inv_stds = []
-    for j in range(rows):
-        part = slice(tok * j, tok * (j + 1))
-        hidden = x_ref[part, :].astype(F32) + dot(low_ref[part, :], w_out[...], NN)
-        h_ref[part, :] = hidden
-        unit, inv_std = layer_norm(hidden)
-        inv_stds.append(inv_std)
-        unit_ref[part, :] = unit
-        n_ref[part, :] = (unit * gain).astype(BF16)
+
+    h_ref[...] = x_ref[...].astype(F32) + dot(low_ref[...], w_out[...], NN)
+    unit, inv_std = layer_norm(h_ref[...])
+    unit_ref[...] = unit
+    inv_ref[...] = jnp.broadcast_to(inv_std, (local, 128))
+    n_ref[...] = (unit * gain).astype(BF16)
+
     for t in range(3):
         wait_all(in_in[t])
-        if t == 0:
-            in_in.append(fetch_in(2))
-        if t == 1:
-            dy_in = [
-                mover.start(x_refs[j].at[1], dy_ref.at[pl.ds(tok * j, tok)]) for j in range(rows)
-            ]
-            down_in = [
-                mover.start(source.at[pl.ds(4 * r, rf)], w_down.at[rows_at(block, rf)])
-                for source, block in zip(sources, blocks)
-            ]
-        gu_ref[:, D * t : D * (t + 1)] = dot(n_ref[...], w_in[t], NN)
+
+    @pl.loop(0, 3)
+    def _(t):
+        gu_ref[:, pl.ds(pl.multiple_of(t * D, D), D)] = dot(n_ref[...], w_in[t], NN)
+
     wait_all(dy_in)
     wait_all(down_in)
-    dy = dy_ref[...]
     size = FF // 3
-    for f in range(3):
-        cols = slice(size * f, size * (f + 1))
-        up_cols = slice(FF + size * f, FF + size * (f + 1))
+
+    @pl.loop(0, 3)
+    def _(f):
+        cols = pl.ds(pl.multiple_of(f * size, size), size)
+        up_cols = pl.ds(pl.multiple_of(FF + f * size, size), size)
         gate = gu_ref[:, cols]
         up = gu_ref[:, up_cols]
         below = 0.5 + 0.5 * lax.erf(gate * math.sqrt(0.5))
         active = gate * below
         mid_ref[:, cols] = (active * up).astype(BF16)
         slope = below + gate * jnp.exp(-0.5 * gate * gate) * (1.0 / math.sqrt(2.0 * math.pi))
-        dmid = dot(dy, w_down[cols, :], NT)
+        dmid = dot(dy_ref[...], w_down[cols, :], NT)
         dgu_ref[:, cols] = (dmid * up * slope).astype(BF16)
         dgu_ref[:, up_cols] = (dmid * active).astype(BF16)
+        g_down[cols, :] = dot(mid_ref[:, cols], dy_ref[...], TN).astype(BF16)
+
     targets = [grad_target(plan, grads, i) for i in range(count)]
-    g_down[...] = dot(mid_ref[...], dy, TN).astype(BF16)
     for target, block in zip(targets, blocks):
         mover.send(g_down.at[rows_at(block, rf)], target.at[pl.ds(4 * r, rf)])
-    out_ref[...] = (h_ref[...] + dot(mid_ref[...], w_down[...], NN)).astype(BF16)
+    step = D // 3
+
+    @pl.loop(0, 3)
+    def _(n):
+        cols = pl.ds(pl.multiple_of(n * step, step), step)
+        mixed = dot(mid_ref[...], w_down[:, cols], NN)
+        out_ref[:, cols] = (h_ref[:, cols] + mixed).astype(BF16)
+        grad = dot(dgu_ref[:, :D], w_in[0, cols, :], NT)
+        for t in range(1, 3):
+            grad = grad + dot(dgu_ref[:, D * t : D * (t + 1)], w_in[t, cols, :], NT)
+        dh_ref[:, cols] = grad
     for j in range(rows):
         mover.send(out_ref.at[pl.ds(tok * j, tok)], out_refs[j])
-    grad_normed = dot(dgu_ref[:, :D], w_in[0], NT)
-    for t in range(1, 3):
-        grad_normed = grad_normed + dot(dgu_ref[:, D * t : D * (t + 1)], w_in[t], NT)
-    dh_ref[...] = grad_normed
-
-    def grad_in(t):
-        g_in[t] = dot(n_ref[...], dgu_ref[:, D * t : D * (t + 1)], TN).astype(BF16)
+
+    @pl.loop(0, 3)
+    def _(t):
+        g_in[t] = dot(
+            n_ref[...], dgu_ref[:, pl.ds(pl.multiple_of(t * D, D), D)], TN
+        ).astype(BF16)
+
+    for t in range(3):
         for target, block in zip(targets, blocks):
             mover.send(g_in.at[t, rows_at(block, r)], target.at[pl.ds((1 + t) * r, r)])
 
-    for j in range(rows):
-        part = slice(tok * j, tok * (j + 1))
-        grad_hidden = dy[part, :].astype(F32) + norm_backward(
-            dh_ref[part, :], unit_ref[part, :], inv_stds[j], gain
-        )
-        dh_ref[part, :] = grad_hidden
-        da_ref[part, :] = grad_hidden.astype(BF16)
-        if j < 3:
-            grad_in(j)
-    for t in range(rows, 3):
-        grad_in(t)
+    grad_hidden = dy_ref[...].astype(F32) + norm_backward(
+        dh_ref[...], unit_ref[...], inv_ref[:, 0:1], gain
+    )
+    dh_ref[...] = grad_hidden
+    da_ref[...] = grad_hidden.astype(BF16)
     mover.send(dh_ref, dh_out)
     do_ref[...] = dot(da_ref[...], w_out[...], NT).astype(BF16)
+    g_out[...] = dot(low_ref[...], da_ref[...], TN).astype(BF16)
+
     mover.send(do_ref, do_out)
-    g_out[...] = dot(low_ref[...], da_ref[...], TN).astype(BF16)
     for target, block in zip(targets, blocks):
         mover.send(g_out.at[rows_at(block, r)], target.at[pl.ds(0, r)])
     mover.finish()
@@ -841,12 +862,13 @@
             pltpu.VMEM((local, D), BF16),
             pltpu.VMEM((local, D), F32),
             pltpu.VMEM((local, D), BF16),
+            pltpu.VMEM((local, 128), F32),
             pltpu.VMEM((D, D), BF16),
             pltpu.VMEM((3, D, D), BF16),
             pltpu.VMEM((FF, D), BF16),
             pltpu.SemaphoreType.DMA((HALVES + 3 * rows + 2 + 10 * count,)),
         ],
-        compiler_params=params(),
+        compiler_params=params(plan, "middle"),
         cost_estimate=cost(COSTS["middle"]),
         name="middle",
     )(meta, gains, *low, *pieces, *sources)
@@ -918,7 +940,7 @@
             pltpu.VMEM((D, 3 * D), BF16),
             pltpu.SemaphoreType.DMA((4 + count * (1 + groups) + 3 * source_count(plan),)),
         ],
-        compiler_params=params(),
+        compiler_params=params(plan, "back_weight"),
         cost_estimate=cost(COSTS["back_weight"]),
         name="back_weight",
     )(meta, cosine, sine, normed, *dq, *dkv)
@@ -959,7 +981,7 @@
         out_specs=[VMEM] * rows,
         out_shape=[shape_of((2, tok, D), BF16)] * rows,
         scratch_shapes=[pltpu.VMEM((D, EXT), BF16), pltpu.SemaphoreType.DMA((count,))],
-        compiler_params=params(),
+        compiler_params=params(plan, "back_in"),
         cost_estimate=cost(COSTS["back_in"]),
         name="back_in",
     )(meta, dprojected, dhidden, gains, *pieces, *outs, *sources)
@@ -1009,7 +1031,7 @@
         out_specs=[VMEM] * plan.nrow,
         out_shape=[shape_of((plan.r, wide), BF16)] * plan.nrow,
         scratch_shapes=[pltpu.VMEM((plan.nrow, plan.r, wide), BF16)],
-        compiler_params=params(),
+        compiler_params=params(plan, "cut_qkv"),
         cost_estimate=cost(COSTS["cut_qkv"]),
         name="cut_qkv",
     )(meta, total, weight)
@@ -1074,7 +1096,7 @@
         out_specs=[VMEM] * plan.nrow,
         out_shape=[shape_of((3 * r, 2 * cw), BF16)] * plan.nrow,
         scratch_shapes=[pltpu.VMEM((plan.nrow, 3 * r, 2 * cw), BF16)],
-        compiler_params=params(),
+        compiler_params=params(plan, "cut_rest"),
         cost_estimate=cost(COSTS["cut_rest"]),
         name="cut_rest",
     )(meta, total, weight)
@@ -1122,7 +1144,7 @@
                 shape_of((plan.rf, plan.cw), F32),
                 shape_of((8, blank), F32),
             ],
-            compiler_params=params(),
+            compiler_params=params(plan, "end_rest"),
             cost_estimate=cost(COSTS["end_rest"]),
             name="end_rest",
         )(*pieces)
@@ -1150,7 +1172,7 @@
         in_specs=[VMEM] * (1 + plan.nrow),
         out_specs=[VMEM] * 2,
         out_shape=[shape_of((plan.r, width), F32), shape_of((1, plan.r), F32)],
-        compiler_params=params(),
+        compiler_params=params(plan, "end_qkv"),
         cost_estimate=cost(COSTS["end_qkv"]),
         name="end_qkv",
     )(gain, *pieces)

time: 213 us -> 195 us (0.915)
  the two profiles are of different devices: /device:TPU:17 before, /device:TPU:0 now
where the time goes in v1:
time: 195 us; the launch traced here: 191 us
  Pallas kernels  79.9 us (41%)
  starting transfers between devices  46.6 us (24%)
  waiting for transfers between devices  42.9 us (22%)
  local copies, waits for them, and re-layouts  13 us (7%)
  other arithmetic  4.78 us (2%)
  between operations  3.81 us (2%)
    pallas_call x3, Pallas kernels, attend_back(): pl.pallas_call(functools.partial(attend_back_kernel, plan, width), grid=(...  21 us
    pallas_call x1, Pallas kernels, middle(): pl.pallas_call(functools.partial(middle_kernel, plan), in_specs=[SMEM, VM...  19.4 us
    ppermute x6, starting transfers between devices, gather_z(): pieces.append(lax.ppermute(source, 'row', plan.z_pairs(j)))  15.2 us
    pallas_call x2, Pallas kernels, attend(): pl.pallas_call(functools.partial(attend_kernel, plan, width), grid=(HALF_...  12.9 us
    ppermute x6, waiting for transfers between devices, exchange_rows(): lax.ppermute(pieces[j], 'blk', plan.xor_pairs(2 * j))  11 us
    unnamed x110, local copies, waits for them, and re-layouts  10.8 us
    ppermute x6, starting transfers between devices, reduce_z(): lax.ppermute(pieces[j], 'row', plan.z_pairs(j))  10.8 us
    ppermute x6, waiting for transfers between devices, reduce_z(): lax.ppermute(pieces[j], 'row', plan.z_pairs(j))  9.34 us
  transfers between devices with their start and end apart: 45, of which 18 were waited for; matrix products, arithmetic and copies ran while one was open for 3% of the time, Pallas kernels for 31%

profile of v1, /device:TPU:0, one launch (start us, length us, event | category | flops | bytes accessed | tf_op | source)
XLA Modules:
  0.0 191.0 jit_solution(4098974573806890873)
XLA Ops:
  0.7 4.1 %collective-permute-start.1 = (bf16[96,576]{1,0:T(8,128)(2,1)}, bf16[96,576]{1,0:T(8,128)(2,1)S(1)}, u32[]{:S(2)}, u32[]{:S(2)}) collective-permute-start(bf16[96,576]{1,0:T(8,128)(2,1)} %refs_0_.1), channel_id=1, source_target_pairs={{0,16},{8,24},{16,0},{24,8},{1,17},{9,25},{17,1},{25,9},{2,18},{10... | collective-permute-start | bytes 331784 | tf_op jit(solution)/shard_map/ppermute | solution.py:166
  4.8 1.3 collective-permute-start.2
  7.0 1.1 copy-done.23
  8.2 1.1 copy-done.24
  11.9 1.5 prepare.1
  13.4 2.4 %collective-permute-start.10 = (bf16[2,128,768]{2,1,0:T(8,128)(2,1)}, bf16[2,128,768]{2,1,0:T(8,128)(2,1)S(1)}, u32[]{:S(2)}, u32[]{:S(2)}) collective-permute-start(bf16[2,128,768]{2,1,0:T(8,128)(2,1)} %get-tuple-element.110), channel_id=1, source_target_pairs={{0,6},{1,7},{2,4},{3,5},{4,2},{5,3},{6,0},{7,1},{8,14},{9,15},{10,... | collective-permute-start | bytes 1179656 | tf_op jit(solution)/shard_map/ppermute | solution.py:172
  21.7 1.6 collective-permute-start.4
  23.2 2.8 %collective-permute-start.5 = (bf16[288,384]{1,0:T(8,128)(2,1)S(1)}, bf16[288,384]{1,0:T(8,128)(2,1)S(1)}, u32[]{:S(2)}, u32[]{:S(2)}) collective-permute-start(bf16[288,384]{1,0:T(8,128)(2,1)S(1)} %get-tuple-element.113.refs_0_), channel_id=1, source_target_pairs={{0,16},{8,24},{16,0},{24,8},{1,17},{9,25},{17,1},{25,9},{2,18},{10... | collective-permute-start | bytes 663560 | tf_op jit(solution)/shard_map/ppermute | solution.py:166
  26.6 2.9 %collective-permute-start.6 = (bf16[288,384]{1,0:T(8,128)(2,1)S(1)}, bf16[288,384]{1,0:T(8,128)(2,1)S(1)}, u32[]{:S(2)}, u32[]{:S(2)}) collective-permute-start(bf16[288,384]{1,0:T(8,128)(2,1)S(1)} %get-tuple-element.113.refs_0_), channel_id=1, source_target_pairs={{0,24},{8,16},{16,8},{24,0},{1,25},{9,17},{17,9},{25,1},{2,26},{10... | collective-permute-start | bytes 663560 | tf_op jit(solution)/shard_map/ppermute | solution.py:166
  30.5 2.8 %collective-permute-done.8.refs_1_.refs_3_ = bf16[2,128,768]{2,1,0:T(8,128)(2,1)S(1)} collective-permute-done((bf16[2,128,768]{2,1,0:T(8,128)(2,1)}, bf16[2,128,768]{2,1,0:T(8,128)(2,1)S(1)}, u32[]{:S(2)}, u32[]{:S(2)}) %collective-permute-start.8) | collective-permute-done | bytes 393248 | tf_op jit(solution)/shard_map/ppermute | solution.py:172
  33.7 1.2 collective-permute-start.11
  35.4 1.1 masks.1
  36.4 3.9 %collective-permute-done.5.refs_2_ = bf16[288,384]{1,0:T(8,128)(2,1)S(1)} collective-permute-done((bf16[288,384]{1,0:T(8,128)(2,1)S(1)}, bf16[288,384]{1,0:T(8,128)(2,1)S(1)}, u32[]{:S(2)}, u32[]{:S(2)}) %collective-permute-start.5) | collective-permute-done | bytes 221216 | tf_op jit(solution)/shard_map/ppermute | solution.py:166
  41.1 3.8 %collective-permute-start.13 = (bf16[288,384]{1,0:T(8,128)(2,1)S(1)}, bf16[288,384]{1,0:T(8,128)(2,1)S(1)}, u32[]{:S(2)}, u32[]{:S(2)}) collective-permute-start(bf16[288,384]{1,0:T(8,128)(2,1)S(1)} %get-tuple-element.113.refs_0_), channel_id=1, source_target_pairs={{0,8},{8,0},{16,24},{24,16},{1,9},{9,1},{17,25},{25,17},{2,10},{10... | collective-permute-start | bytes 663560 | tf_op jit(solution)/shard_map/ppermute | solution.py:166
  45.5 4.7 %collective-permute-done.13.refs_1_ = bf16[288,384]{1,0:T(8,128)(2,1)S(1)} collective-permute-done((bf16[288,384]{1,0:T(8,128)(2,1)S(1)}, bf16[288,384]{1,0:T(8,128)(2,1)S(1)}, u32[]{:S(2)}, u32[]{:S(2)}) %collective-permute-start.13) | collective-permute-done | bytes 221216 | tf_op jit(solution)/shard_map/ppermute | solution.py:166
  51.2 1.0 collective-permute-start.17
  52.2 5.8 %project.1 = (bf16[512,768]{1,0:T(8,128)(2,1)S(1)}, bf16[2,512,384]{2,1,0:T(8,128)(2,1)S(1)}, bf16[2,512,384]{2,1,0:T(8,128)(2,1)S(1)}, bf16[512,768]{1,0:T(8,128)(2,1)S(1)}, f32[8,768]{1,0:T(8,128)S(1)}) custom-call(s32[25]{0:T(128)S(1)} %fusion.3.meta.order, f32[512,128]{1,0:T(8,128)S(1)} %get-tuple-element.205.cos_ref.refs_0_, ...), custom_call_target="tpu_custom_call" | custom-call | flops 7000000 | bytes 1024 | tf_op jit(solution)/shard_map/project/pallas_call | solution.py:500
  58.7 1.3 collective-permute-start.18
  60.0 1.0 collective-permute-done.16.refs_1_
  61.0 6.4 %attend.2 = (f32[512,384]{1,0:T(8,128)S(1)}, bf16[512,384]{1,0:T(8,128)(2,1)S(1)}, f32[3,2,512]{2,1,0:T(2,128)S(1)}) custom-call(s32[25]{0:T(128)S(1)} %fusion.3.meta.order, bf16[1024,128]{1,0:T(8,128)(2,1)S(1)} %get-tuple-element.105.kmask, bf16[512,128]{1,0:T(8,128)(2,1)S(1)} %get-tuple-element.106.qmask, bf16[512,768]{1,0:T(8,128)(2,1)S(1)} %get-tuple-element.118.q_ref, ...), custom_call_target="tpu_custom_call" | custom-call | flops 9000000 | bytes 1024 | tf_op jit(solution)/shard_map/attend/pallas_call | solution.py:606
  69.6 2.1 %collective-permute-done.18.refs_8_ = bf16[528,768]{1,0:T(8,128)(2,1)S(1)} collective-permute-done((bf16[528,768]{1,0:T(8,128)(2,1)S(1)}, bf16[528,768]{1,0:T(8,128)(2,1)S(1)}, u32[]{:S(2)}, u32[]{:S(2)}) %collective-permute-start.18) | collective-permute-done | bytes 811040 | tf_op jit(solution)/shard_map/ppermute | solution.py:179
  72.3 6.5 %attend.3 = (f32[512,384]{1,0:T(8,128)S(1)}, bf16[512,384]{1,0:T(8,128)(2,1)S(1)}, f32[3,2,512]{2,1,0:T(2,128)S(1)}) custom-call(s32[25]{0:T(128)S(1)} %fusion.3.meta.order, bf16[1024,128]{1,0:T(8,128)(2,1)S(1)} %get-tuple-element.105.kmask, bf16[512,128]{1,0:T(8,128)(2,1)S(1)} %get-tuple-element.106.qmask, bf16[512,768]{1,0:T(8,128)(2,1)S(1)} %get-tuple-element.118.q_ref, ...), custom_call_target="tpu_custom_call" | custom-call | flops 9000000 | bytes 1024 | tf_op jit(solution)/shard_map/attend/pallas_call | solution.py:606
  80.7 2.1 %collective-permute-done.24.refs_13_ = bf16[528,768]{1,0:T(8,128)(2,1)S(1)} collective-permute-done((bf16[528,768]{1,0:T(8,128)(2,1)S(1)}, bf16[528,768]{1,0:T(8,128)(2,1)S(1)}, u32[]{:S(2)}, u32[]{:S(2)}) %collective-permute-start.24) | collective-permute-done | bytes 811040 | tf_op jit(solution)/shard_map/ppermute | solution.py:159
  83.8 19.4 %middle.1 = (bf16[128,768]{1,0:T(8,128)(2,1)}, bf16[128,768]{1,0:T(8,128)(2,1)}, bf16[128,768]{1,0:T(8,128)(2,1)}, bf16[128,768]{1,0:T(8,128)(2,1)}, bf16[512,76...) custom-call(s32[25]{0:T(128)} %copy-done.35, ...), custom_call_target="tpu_custom_call" | custom-call | flops 20000000 | bytes 1024 | tf_op jit(solution)/shard_map/middle/pallas_call | solution.py:841
  103.7 1.1 copy-done.2
  104.9 3.5 %attend_back.3 = (bf16[512,128]{1,0:T(8,128)(2,1)S(1)}, bf16[2,512,128]{2,1,0:T(8,128)(2,1)S(1)}, bf16[2,512,128]{2,1,0:T(8,128)(2,1)S(1)}) custom-call(s32[25]{0:T(128)S(1)} %copy-done.36, bf16[1024,128]{1,0:T(8,128)(2,1)S(1)} %get-tuple-element.105.kmask, bf16[512,128]{1,0:T(8,128)(2,1)S(1)} %get-tuple-element.106.qmask, ...), custom_call_target="tpu_custom_call" | custom-call | flops 4000000 | bytes 1024 | tf_op jit(solution)/shard_map/attend_back/pallas_call | solution.py:691
  110.9 6.9 %attend_back.4 = (bf16[512,256]{1,0:T(8,128)(2,1)S(1)}, bf16[2,512,256]{2,1,0:T(8,128)(2,1)S(1)}, bf16[2,512,256]{2,1,0:T(8,128)(2,1)S(1)}) custom-call(s32[25]{0:T(128)S(1)} %copy-done.36, bf16[1024,128]{1,0:T(8,128)(2,1)S(1)} %get-tuple-element.105.kmask, bf16[512,128]{1,0:T(8,128)(2,1)S(1)} %get-tuple-element.106.qmask, ...), custom_call_target="tpu_custom_call" | custom-call | flops 8000000 | bytes 1024 | tf_op jit(solution)/shard_map/attend_back/pallas_call | solution.py:691
  117.9 10.5 %attend_back.5 = (bf16[512,384]{1,0:T(8,128)(2,1)S(1)}, bf16[2,512,384]{2,1,0:T(8,128)(2,1)S(1)}, bf16[2,512,384]{2,1,0:T(8,128)(2,1)S(1)}) custom-call(s32[25]{0:T(128)S(1)} %copy-done.36, bf16[1024,128]{1,0:T(8,128)(2,1)S(1)} %get-tuple-element.105.kmask, bf16[512,128]{1,0:T(8,128)(2,1)S(1)} %get-tuple-element.106.qmask, ...), custom_call_target="tpu_custom_call" | custom-call | flops 12000000 | bytes 1024 | tf_op jit(solution)/shard_map/attend_back/pallas_call | solution.py:691
  130.2 1.1 collective-permute-start.31
  131.5 5.9 %back_weight.1 = (bf16[3,512,768]{2,1,0:T(8,128)(2,1)S(1)}, bf16[2,96,2304]{2,1,0:T(8,128)(2,1)S(1)}, bf16[2,96,2304]{2,1,0:T(8,128)(2,1)S(1)}, bf16[2,96,2304]{2,1,0:T(8,128)(2,1)S(1)}, bf16[2,96,2304]{2,1,0:T(8,128)(2,1)S(1)}) custom-call(s32[25]{0:T(128)S(1)} %copy-done.36, f32[512,128]{1,0:T(8,128)S(1)} %get-tuple-element.205.cos_ref.refs_0_, ...), custom_call_target="tpu_custom_call" | custom-call | flops 6000000 | bytes 1024 | tf_op jit(solution)/shard_map/back_weight/pallas_call | solution.py:929
  137.9 4.6 %collective-permute-done.31 = bf16[1,528,768]{2,1,0:T(8,128)(2,1)S(1)} collective-permute-done((bf16[1,528,768]{2,1,0:T(8,128)(2,1)S(1)}, bf16[1,528,768]{2,1,0:T(8,128)(2,1)S(1)}, u32[]{:S(2)}, u32[]{:S(2)}) %collective-permute-start.31) | collective-permute-done | bytes 811040 | tf_op jit(solution)/shard_map/ppermute | solution.py:202
  145.1 3.2 %collective-permute-start.34 = (bf16[288,384]{1,0:T(8,128)(2,1)S(1)}, bf16[288,384]{1,0:T(8,128)(2,1)S(1)}, u32[]{:S(2)}, u32[]{:S(2)}) collective-permute-start(bf16[288,384]{1,0:T(8,128)(2,1)S(1)} %get-tuple-element.161), channel_id=1, source_target_pairs={{0,8},{8,0},{16,24},{24,16},{1,9},{9,1},{17,25},{25,17},{2,10},{10... | collective-permute-start | bytes 663560 | tf_op jit(solution)/shard_map/ppermute | solution.py:1107
  148.3 1.3 collective-permute-start.35
  150.0 5.6 %back_in.1 = (bf16[2,128,768]{2,1,0:T(8,128)(2,1)S(1)}, bf16[2,128,768]{2,1,0:T(8,128)(2,1)S(1)}, bf16[2,128,768]{2,1,0:T(8,128)(2,1)S(1)}, bf16[2,128,768]{2,1,0:T(8,128)(2,1)S(1)}) custom-call(s32[25]{0:T(128)S(1)} %copy-done.36, bf16[3,512,768]{2,1,0:T(8,128)(2,1)S(1)} %get-tuple-element.153.dp_ref, f32[512,768]{1,0:T(8,128)S(1)} %copy-done.22, ...), custom_call_target="tpu_custom_call" | custom-call | flops 7000000 | bytes 1024 | tf_op jit(solution)/shard_map/back_in/pallas_call | solution.py:978
  155.5 1.1 collective-permute-done.34.refs_1_
  156.7 2.9 %collective-permute-done.35.refs_2_ = bf16[288,384]{1,0:T(8,128)(2,1)S(1)} collective-permute-done((bf16[288,384]{1,0:T(8,128)(2,1)S(1)}, bf16[288,384]{1,0:T(8,128)(2,1)S(1)}, u32[]{:S(2)}, u32[]{:S(2)}) %collective-permute-start.35) | collective-permute-done | bytes 221216 | tf_op jit(solution)/shard_map/ppermute | solution.py:1107
  159.8 1.1 collective-permute-start.38
  160.9 2.5 %collective-permute-start.37 = (bf16[288,384]{1,0:T(8,128)(2,1)S(1)}, bf16[288,384]{1,0:T(8,128)(2,1)S(1)}, u32[]{:S(2)}, u32[]{:S(2)}) collective-permute-start(bf16[288,384]{1,0:T(8,128)(2,1)S(1)} %get-tuple-element.163), channel_id=1, source_target_pairs={{0,24},{8,16},{16,8},{24,0},{1,25},{9,17},{17,9},{25,1},{2,26},{10... | collective-permute-start | bytes 663560 | tf_op jit(solution)/shard_map/ppermute | solution.py:1107
  163.4 5.3 %collective-permute-done.37.refs_3_ = bf16[288,384]{1,0:T(8,128)(2,1)S(1)} collective-permute-done((bf16[288,384]{1,0:T(8,128)(2,1)S(1)}, bf16[288,384]{1,0:T(8,128)(2,1)S(1)}, u32[]{:S(2)}, u32[]{:S(2)}) %collective-permute-start.37) | collective-permute-done | bytes 221216 | tf_op jit(solution)/shard_map/ppermute | solution.py:1107
  168.7 2.2 %collective-permute-done.38 = bf16[1,96,2304]{2,1,0:T(8,128)(2,1)S(1)} collective-permute-done((bf16[1,96,2304]{2,1,0:T(8,128)(2,1)S(1)}, bf16[1,96,2304]{2,1,0:T(8,128)(2,1)S(1)}, u32[]{:S(2)}, u32[]{:S(2)}) %collective-permute-start.38) | collective-permute-done | bytes 442400 | tf_op jit(solution)/shard_map/ppermute | solution.py:202
  171.1 1.4 collective-permute-start.41
  173.4 2.1 %collective-permute-start.43 = (bf16[96,640]{1,0:T(8,128)(2,1)S(1)}, bf16[96,640]{1,0:T(8,128)(2,1)S(1)}, u32[]{:S(2)}, u32[]{:S(2)}) collective-permute-start(bf16[96,640]{1,0:T(8,128)(2,1)S(1)} %get-tuple-element.177), channel_id=1, source_target_pairs={{0,16},{8,24},{16,0},{24,8},{1,17},{9,25},{17,1},{25,9},{2,18},{10... | collective-permute-start | bytes 368648 | tf_op jit(solution)/shard_map/ppermute | solution.py:1107
  175.5 1.1 collective-permute-start.40
  176.6 1.0 collective-permute-start.39
  178.5 4.6 %collective-permute-done.41.refs_3_ = bf16[2,128,768]{2,1,0:T(8,128)(2,1)S(1)} collective-permute-done((bf16[2,128,768]{2,1,0:T(8,128)(2,1)S(1)}, bf16[2,128,768]{2,1,0:T(8,128)(2,1)S(1)}, u32[]{:S(2)}, u32[]{:S(2)}) %collective-permute-start.41) | collective-permute-done | bytes 393248 | tf_op jit(solution)/shard_map/ppermute | solution.py:172
  183.1 1.6 collective-permute-start.44
  185.3 2.7 %collective-permute-done.40.refs_2_ = bf16[2,128,768]{2,1,0:T(8,128)(2,1)S(1)} collective-permute-done((bf16[2,128,768]{2,1,0:T(8,128)(2,1)S(1)}, bf16[2,128,768]{2,1,0:T(8,128)(2,1)S(1)}, u32[]{:S(2)}, u32[]{:S(2)}) %collective-permute-start.40) | collective-permute-done | bytes 393248 | tf_op jit(solution)/shard_map/ppermute | solution.py:172
  188.0 1.8 place_rows.1
  (198 shorter events, 30.1 us)
Async XLA Ops:
  0.7 19.6 %collective-permute-start.1 = (bf16[96,576]{1,0:T(8,128)(2,1)}, bf16[96,576]{1,0:T(8,128)(2,1)S(1)}, u32[]{:S(2)}, u32[]{:S(2)}) collective-permute-start(bf16[96,576]{1,0:T(8,128)(2,1)} %refs_0_.1), channel_id=1, source_target_pairs={{0,16},{8,24},{16,0},{24,8},{1,17},{9,25},{17,1},{25,9},{2,18},{10... | collective-permute-start | bytes 331784 | tf_op jit(solution)/shard_map/ppermute | solution.py:166
  4.8 16.1 %collective-permute-start.2 = (bf16[96,576]{1,0:T(8,128)(2,1)}, bf16[96,576]{1,0:T(8,128)(2,1)S(1)}, u32[]{:S(2)}, u32[]{:S(2)}) collective-permute-start(bf16[96,576]{1,0:T(8,128)(2,1)} %refs_0_.1), channel_id=1, source_target_pairs={{0,24},{8,16},{16,8},{24,0},{1,25},{9,17},{17,9},{25,1},{2,26},{10... | collective-permute-start | bytes 331784 | tf_op jit(solution)/shard_map/ppermute | solution.py:166
  6.1 14.8 %collective-permute-start = (bf16[96,576]{1,0:T(8,128)(2,1)}, bf16[96,576]{1,0:T(8,128)(2,1)S(1)}, u32[]{:S(2)}, u32[]{:S(2)}) collective-permute-start(bf16[96,576]{1,0:T(8,128)(2,1)} %refs_0_.1), channel_id=1, source_target_pairs={{0,8},{8,0},{16,24},{24,16},{1,9},{9,1},{17,25},{25,17},{2,10},{10... | collective-permute-start | bytes 331784 | tf_op jit(solution)/shard_map/ppermute | solution.py:166
  11.9 60.4 %copy-start.35 = (s32[25]{0:T(128)}, s32[25]{0:T(128)S(1)}, u32[]{:S(2)}) copy-start(s32[25]{0:T(128)S(1)} %fusion.3.meta.order) | copy-start | bytes 304
  13.4 38.8 %copy-start.4 = (bf16[2,128,768]{2,1,0:T(8,128)(2,1)}, bf16[2,128,768]{2,1,0:T(8,128)(2,1)S(1)}, u32[]{:S(2)}) copy-start(bf16[2,128,768]{2,1,0:T(8,128)(2,1)S(1)} %get-tuple-element.115.refs_0_.refs_2_) | copy-start | bytes 1179652
  13.4 13.2 %collective-permute-start.10 = (bf16[2,128,768]{2,1,0:T(8,128)(2,1)}, bf16[2,128,768]{2,1,0:T(8,128)(2,1)S(1)}, u32[]{:S(2)}, u32[]{:S(2)}) collective-permute-start(bf16[2,128,768]{2,1,0:T(8,128)(2,1)} %get-tuple-element.110), channel_id=1, source_target_pairs={{0,6},{1,7},{2,4},{3,5},{4,2},{5,3},{6,0},{7,1},{8,14},{9,15},{10,... | collective-permute-start | bytes 1179656 | tf_op jit(solution)/shard_map/ppermute | solution.py:172
  15.9 17.5 %collective-permute-start.8 = (bf16[2,128,768]{2,1,0:T(8,128)(2,1)}, bf16[2,128,768]{2,1,0:T(8,128)(2,1)S(1)}, u32[]{:S(2)}, u32[]{:S(2)}) collective-permute-start(bf16[2,128,768]{2,1,0:T(8,128)(2,1)} %get-tuple-element.108), channel_id=1, source_target_pairs={{0,2},{1,3},{2,0},{3,1},{4,6},{5,7},{6,4},{7,5},{8,10},{9,11},{10,... | collective-permute-start | bytes 1179656 | tf_op jit(solution)/shard_map/ppermute | solution.py:172
  20.2 13.5 %collective-permute-start.9 = (bf16[2,128,768]{2,1,0:T(8,128)(2,1)S(1)}, bf16[2,128,768]{2,1,0:T(8,128)(2,1)S(1)}, u32[]{:S(2)}, u32[]{:S(2)}) collective-permute-start(bf16[2,128,768]{2,1,0:T(8,128)(2,1)S(1)} %get-tuple-element.109), channel_id=1, source_target_pairs={{0,4},{1,5},{2,6},{3,7},{4,0},{5,1},{6,2},{7,3},{8,12},{9,13},{10,... | collective-permute-start | bytes 1179656 | tf_op jit(solution)/shard_map/ppermute | solution.py:172
  21.7 19.5 %collective-permute-start.4 = (bf16[96,2432]{1,0:T(8,128)(2,1)S(1)}, bf16[96,2432]{1,0:T(8,128)(2,1)S(1)}, u32[]{:S(2)}, u32[]{:S(2)}) collective-permute-start(bf16[96,2432]{1,0:T(8,128)(2,1)S(1)} %join_qkv.1.refs_4_.refs_8_.weight), channel_id=1, source_target_pairs={{0,2},{1,5},{2,0},{3,7},{4,6},{5,1},{6,4},{7,3},{8,10},{9,13},{10,... | collective-permute-start | bytes 1400840 | tf_op jit(solution)/shard_map/ppermute | solution.py:178
  23.2 17.0 %collective-permute-start.5 = (bf16[288,384]{1,0:T(8,128)(2,1)S(1)}, bf16[288,384]{1,0:T(8,128)(2,1)S(1)}, u32[]{:S(2)}, u32[]{:S(2)}) collective-permute-start(bf16[288,384]{1,0:T(8,128)(2,1)S(1)} %get-tuple-element.113.refs_0_), channel_id=1, source_target_pairs={{0,16},{8,24},{16,0},{24,8},{1,17},{9,25},{17,1},{25,9},{2,18},{10... | collective-permute-start | bytes 663560 | tf_op jit(solution)/shard_map/ppermute | solution.py:166
  26.6 25.6 %copy-start.6 = (bf16[2,128,768]{2,1,0:T(8,128)(2,1)}, bf16[2,128,768]{2,1,0:T(8,128)(2,1)S(1)}, u32[]{:S(2)}) copy-start(bf16[2,128,768]{2,1,0:T(8,128)(2,1)S(1)} %collective-permute-done.10.refs_3_.refs_5_) | copy-start | bytes 1179652
  26.6 13.7 %collective-permute-start.6 = (bf16[288,384]{1,0:T(8,128)(2,1)S(1)}, bf16[288,384]{1,0:T(8,128)(2,1)S(1)}, u32[]{:S(2)}, u32[]{:S(2)}) collective-permute-start(bf16[288,384]{1,0:T(8,128)(2,1)S(1)} %get-tuple-element.113.refs_0_), channel_id=1, source_target_pairs={{0,24},{8,16},{16,8},{24,0},{1,25},{9,17},{17,9},{25,1},{2,26},{10... | collective-permute-start | bytes 663560 | tf_op jit(solution)/shard_map/ppermute | solution.py:166
  33.7 11.8 %collective-permute-start.11 = (bf16[96,2432]{1,0:T(8,128)(2,1)S(1)}, bf16[96,2432]{1,0:T(8,128)(2,1)S(1)}, u32[]{:S(2)}, u32[]{:S(2)}) collective-permute-start(bf16[96,2432]{1,0:T(8,128)(2,1)S(1)} %join_qkv.1.refs_4_.refs_8_.weight), channel_id=1, source_target_pairs={{0,4},{1,3},{2,6},{3,1},{4,0},{5,7},{6,2},{7,5},{8,12},{9,11},{10,... | collective-permute-start | bytes 1400840 | tf_op jit(solution)/shard_map/ppermute | solution.py:179
  41.1 9.1 %collective-permute-start.14 = (bf16[96,2432]{1,0:T(8,128)(2,1)S(1)}, bf16[96,2432]{1,0:T(8,128)(2,1)S(1)}, u32[]{:S(2)}, u32[]{:S(2)}) collective-permute-start(bf16[96,2432]{1,0:T(8,128)(2,1)S(1)} %collective-permute-done.4.refs_5_.refs_9_), channel_id=1, source_target_pairs={{0,4},{1,3},{2,6},{3,1},{4,0},{5,7},{6,2},{7,5},{8,12},{9,11},{10,... | collective-permute-start | bytes 1400840 | tf_op jit(solution)/shard_map/ppermute | solution.py:187
  41.1 9.1 %collective-permute-start.13 = (bf16[288,384]{1,0:T(8,128)(2,1)S(1)}, bf16[288,384]{1,0:T(8,128)(2,1)S(1)}, u32[]{:S(2)}, u32[]{:S(2)}) collective-permute-start(bf16[288,384]{1,0:T(8,128)(2,1)S(1)} %get-tuple-element.113.refs_0_), channel_id=1, source_target_pairs={{0,8},{8,0},{16,24},{24,16},{1,9},{9,1},{17,25},{25,17},{2,10},{10... | collective-permute-start | bytes 663560 | tf_op jit(solution)/shard_map/ppermute | solution.py:166
  44.9 5.3 %collective-permute-start.3 = (bf16[96,2432]{1,0:T(8,128)(2,1)S(1)}, bf16[96,2432]{1,0:T(8,128)(2,1)S(1)}, u32[]{:S(2)}, u32[]{:S(2)}) collective-permute-start(bf16[96,2432]{1,0:T(8,128)(2,1)S(1)} %join_qkv.1.refs_4_.refs_8_.weight), channel_id=1, source_target_pairs={{0,1},{1,0},{2,3},{3,2},{4,5},{5,4},{6,7},{7,6},{8,9},{9,8},{10,11... | collective-permute-start | bytes 1400840 | tf_op jit(solution)/shard_map/ppermute | solution.py:159
  45.0 5.3 %collective-permute-start.7 = (bf16[96,2432]{1,0:T(8,128)(2,1)S(1)}, bf16[96,2432]{1,0:T(8,128)(2,1)S(1)}, u32[]{:S(2)}, u32[]{:S(2)}) collective-permute-start(bf16[96,2432]{1,0:T(8,128)(2,1)S(1)} %collective-permute-done.4.refs_5_.refs_9_), channel_id=1, source_target_pairs={{0,1},{1,0},{2,3},{3,2},{4,5},{5,4},{6,7},{7,6},{8,9},{9,8},{10,11... | collective-permute-start | bytes 1400840 | tf_op jit(solution)/shard_map/ppermute | solution.py:159
  45.5 4.8 %collective-permute-start.12 = (bf16[96,2432]{1,0:T(8,128)(2,1)S(1)}, bf16[96,2432]{1,0:T(8,128)(2,1)S(1)}, u32[]{:S(2)}, u32[]{:S(2)}) collective-permute-start(bf16[96,2432]{1,0:T(8,128)(2,1)S(1)} %collective-permute-done.11.refs_6_.refs_10_), channel_id=1, source_target_pairs={{0,1},{1,0},{2,3},{3,2},{4,5},{5,4},{6,7},{7,6},{8,9},{9,8},{10,11... | collective-permute-start | bytes 1400840 | tf_op jit(solution)/shard_map/ppermute | solution.py:159
  50.2 2.0 %collective-permute-start.15 = (bf16[96,2432]{1,0:T(8,128)(2,1)S(1)}, bf16[96,2432]{1,0:T(8,128)(2,1)S(1)}, u32[]{:S(2)}, u32[]{:S(2)}) collective-permute-start(bf16[96,2432]{1,0:T(8,128)(2,1)S(1)} %collective-permute-done.14.refs_7_.refs_11_), channel_id=1, source_target_pairs={{0,1},{1,0},{2,3},{3,2},{4,5},{5,4},{6,7},{7,6},{8,9},{9,8},{10,11... | collective-permute-start | bytes 1400840 | tf_op jit(solution)/shard_map/ppermute | solution.py:159
  51.2 17.0 %collective-permute-start.17 = (bf16[528,768]{1,0:T(8,128)(2,1)S(1)}, bf16[528,768]{1,0:T(8,128)(2,1)S(1)}, u32[]{:S(2)}, u32[]{:S(2)}) collective-permute-start(bf16[528,768]{1,0:T(8,128)(2,1)S(1)} %join_rest.1.refs_6_.weight), channel_id=1, source_target_pairs={{0,2},{1,5},{2,0},{3,7},{4,6},{5,1},{6,4},{7,3},{8,10},{9,13},{10,... | collective-permute-start | bytes 2433032 | tf_op jit(solution)/shard_map/ppermute | solution.py:178
  58.7 2.3 %collective-permute-start.16 = (bf16[2,512,384]{2,1,0:T(8,128)(2,1)S(1)}, bf16[2,512,384]{2,1,0:T(8,128)(2,1)S(1)}, u32[]{:S(2)}, u32[]{:S(2)}) collective-permute-start(bf16[2,512,384]{2,1,0:T(8,128)(2,1)S(1)} %get-tuple-element.119.refs_0_), channel_id=1, source_target_pairs={{0,1},{1,0},{2,3},{3,2},{4,5},{5,4},{6,7},{7,6},{8,9},{9,8},{10,11... | collective-permute-start | bytes 2359304 | tf_op jit(solution)/shard_map/ppermute | solution.py:1236
  58.7 13.0 %collective-permute-start.18 = (bf16[528,768]{1,0:T(8,128)(2,1)S(1)}, bf16[528,768]{1,0:T(8,128)(2,1)S(1)}, u32[]{:S(2)}, u32[]{:S(2)}) collective-permute-start(bf16[528,768]{1,0:T(8,128)(2,1)S(1)} %join_rest.1.refs_6_.weight), channel_id=1, source_target_pairs={{0,4},{1,3},{2,6},{3,1},{4,0},{5,7},{6,2},{7,5},{8,12},{9,11},{10,... | collective-permute-start | bytes 2433032 | tf_op jit(solution)/shard_map/ppermute | solution.py:179
  68.2 12.3 %collective-permute-start.20 = (bf16[528,768]{1,0:T(8,128)(2,1)S(1)}, bf16[528,768]{1,0:T(8,128)(2,1)S(1)}, u32[]{:S(2)}, u32[]{:S(2)}) collective-permute-start(bf16[528,768]{1,0:T(8,128)(2,1)S(1)} %collective-permute-done.17.refs_7_), channel_id=1, source_target_pairs={{0,4},{1,3},{2,6},{3,1},{4,0},{5,7},{6,2},{7,5},{8,12},{9,11},{10,... | collective-permute-start | bytes 2433032 | tf_op jit(solution)/shard_map/ppermute | solution.py:187
  69.1 3.2 %collective-permute-start.19 = (bf16[2,512,384]{2,1,0:T(8,128)(2,1)S(1)}, bf16[2,512,384]{2,1,0:T(8,128)(2,1)S(1)}, u32[]{:S(2)}, u32[]{:S(2)}) collective-permute-start(bf16[2,512,384]{2,1,0:T(8,128)(2,1)S(1)} %get-tuple-element.122.refs_0_), channel_id=1, source_target_pairs={{0,1},{1,0},{2,3},{3,2},{4,5},{5,4},{6,7},{7,6},{8,9},{9,8},{10,11... | collective-permute-start | bytes 2359304 | tf_op jit(solution)/shard_map/ppermute | solution.py:1236
  69.1 11.6 %collective-permute-start.21 = (bf16[528,768]{1,0:T(8,128)(2,1)S(1)}, bf16[528,768]{1,0:T(8,128)(2,1)S(1)}, u32[]{:S(2)}, u32[]{:S(2)}) collective-permute-start(bf16[528,768]{1,0:T(8,128)(2,1)S(1)} %join_rest.1.refs_6_.weight), channel_id=1, source_target_pairs={{0,1},{1,0},{2,3},{3,2},{4,5},{5,4},{6,7},{7,6},{8,9},{9,8},{10,11... | collective-permute-start | bytes 2433032 | tf_op jit(solution)/shard_map/ppermute | solution.py:159
  69.6 11.1 %collective-permute-start.22 = (bf16[528,768]{1,0:T(8,128)(2,1)S(1)}, bf16[528,768]{1,0:T(8,128)(2,1)S(1)}, u32[]{:S(2)}, u32[]{:S(2)}) collective-permute-start(bf16[528,768]{1,0:T(8,128)(2,1)S(1)} %collective-permute-done.17.refs_7_), channel_id=1, source_target_pairs={{0,1},{1,0},{2,3},{3,2},{4,5},{5,4},{6,7},{7,6},{8,9},{9,8},{10,11... | collective-permute-start | bytes 2433032 | tf_op jit(solution)/shard_map/ppermute | solution.py:159
  71.7 9.0 %collective-permute-start.23 = (bf16[528,768]{1,0:T(8,128)(2,1)S(1)}, bf16[528,768]{1,0:T(8,128)(2,1)S(1)}, u32[]{:S(2)}, u32[]{:S(2)}) collective-permute-start(bf16[528,768]{1,0:T(8,128)(2,1)S(1)} %collective-permute-done.18.refs_8_), channel_id=1, source_target_pairs={{0,1},{1,0},{2,3},{3,2},{4,5},{5,4},{6,7},{7,6},{8,9},{9,8},{10,11... | collective-permute-start | bytes 2433032 | tf_op jit(solution)/shard_map/ppermute | solution.py:159
  80.5 2.3 %collective-permute-start.24 = (bf16[528,768]{1,0:T(8,128)(2,1)S(1)}, bf16[528,768]{1,0:T(8,128)(2,1)S(1)}, u32[]{:S(2)}, u32[]{:S(2)}) collective-permute-start(bf16[528,768]{1,0:T(8,128)(2,1)S(1)} %collective-permute-done.20.refs_9_), channel_id=1, source_target_pairs={{0,1},{1,0},{2,3},{3,2},{4,5},{5,4},{6,7},{7,6},{8,9},{9,8},{10,11... | collective-permute-start | bytes 2433032 | tf_op jit(solution)/shard_map/ppermute | solution.py:159
  103.1 5.2 %collective-permute-start.26 = (bf16[2,528,768]{2,1,0:T(8,128)(2,1)}, bf16[2,528,768]{2,1,0:T(8,128)(2,1)S(1)}, u32[]{:S(2)}, u32[]{:S(2)}) collective-permute-start(bf16[2,528,768]{2,1,0:T(8,128)(2,1)} %get-tuple-element.136), channel_id=1, source_target_pairs={{0,1},{1,0},{2,3},{3,2},{4,5},{5,4},{6,7},{7,6},{8,9},{9,8},{10,11... | collective-permute-start | bytes 4866056 | tf_op jit(solution)/shard_map/ppermute | solution.py:159
  103.4 6.4 %collective-permute-start.25 = (bf16[2,528,768]{2,1,0:T(8,128)(2,1)}, bf16[2,528,768]{2,1,0:T(8,128)(2,1)S(1)}, u32[]{:S(2)}, u32[]{:S(2)}) collective-permute-start(bf16[2,528,768]{2,1,0:T(8,128)(2,1)} %get-tuple-element.133), channel_id=1, source_target_pairs={{0,1},{1,0},{2,3},{3,2},{4,5},{5,4},{6,7},{7,6},{8,9},{9,8},{10,11... | collective-permute-start | bytes 4866056 | tf_op jit(solution)/shard_map/ppermute | solution.py:159
  108.8 21.0 %collective-permute-start.28 = (bf16[2,528,768]{2,1,0:T(8,128)(2,1)S(1)}, bf16[2,528,768]{2,1,0:T(8,128)(2,1)S(1)}, u32[]{:S(2)}, u32[]{:S(2)}) collective-permute-start(bf16[2,528,768]{2,1,0:T(8,128)(2,1)S(1)} %add_convert_fusion), channel_id=1, source_target_pairs={{0,4},{1,3},{2,6},{3,1},{4,0},{5,7},{6,2},{7,5},{8,12},{9,11},{10,... | collective-permute-start | bytes 4866056 | tf_op jit(solution)/shard_map/ppermute | solution.py:202
  109.8 8.1 %collective-permute-start.27 = (bf16[2,512,128]{2,1,0:T(8,128)(2,1)S(1)}, bf16[2,512,128]{2,1,0:T(8,128)(2,1)S(1)}, u32[]{:S(2)}, u32[]{:S(2)}) collective-permute-start(bf16[2,512,128]{2,1,0:T(8,128)(2,1)S(1)} %get-tuple-element.139), channel_id=1, source_target_pairs={{0,1},{1,0},{2,3},{3,2},{4,5},{5,4},{6,7},{7,6},{8,9},{9,8},{10,11... | collective-permute-start | bytes 786440 | tf_op jit(solution)/shard_map/ppermute | solution.py:1276
  128.4 3.1 %collective-permute-start.30 = (bf16[2,512,384]{2,1,0:T(8,128)(2,1)S(1)}, bf16[2,512,384]{2,1,0:T(8,128)(2,1)S(1)}, u32[]{:S(2)}, u32[]{:S(2)}) collective-permute-start(bf16[2,512,384]{2,1,0:T(8,128)(2,1)S(1)} %get-tuple-element.151), channel_id=1, source_target_pairs={{0,1},{1,0},{2,3},{3,2},{4,5},{5,4},{6,7},{7,6},{8,9},{9,8},{10,11... | collective-permute-start | bytes 2359304 | tf_op jit(solution)/shard_map/ppermute | solution.py:1276
  128.5 3.0 %collective-permute-start.29 = (bf16[2,512,256]{2,1,0:T(8,128)(2,1)S(1)}, bf16[2,512,256]{2,1,0:T(8,128)(2,1)S(1)}, u32[]{:S(2)}, u32[]{:S(2)}) collective-permute-start(bf16[2,512,256]{2,1,0:T(8,128)(2,1)S(1)} %get-tuple-element.149), channel_id=1, source_target_pairs={{0,1},{1,0},{2,3},{3,2},{4,5},{5,4},{6,7},{7,6},{8,9},{9,8},{10,11... | collective-permute-start | bytes 1572872 | tf_op jit(solution)/shard_map/ppermute | solution.py:1276
  130.2 12.3 %collective-permute-start.31 = (bf16[1,528,768]{2,1,0:T(8,128)(2,1)S(1)}, bf16[1,528,768]{2,1,0:T(8,128)(2,1)S(1)}, u32[]{:S(2)}, u32[]{:S(2)}) collective-permute-start(bf16[1,528,768]{2,1,0:T(8,128)(2,1)S(1)} %get-tuple-element.196), channel_id=1, source_target_pairs={{0,2},{1,5},{2,0},{3,7},{4,6},{5,1},{6,4},{7,3},{8,10},{9,13},{10,... | collective-permute-start | bytes 2433032 | tf_op jit(solution)/shard_map/ppermute | solution.py:202
  137.4 5.4 %collective-permute-start.32 = (bf16[2,96,2304]{2,1,0:T(8,128)(2,1)S(1)}, bf16[2,96,2304]{2,1,0:T(8,128)(2,1)S(1)}, u32[]{:S(2)}, u32[]{:S(2)}) collective-permute-start(bf16[2,96,2304]{2,1,0:T(8,128)(2,1)S(1)} %get-tuple-element.156), channel_id=1, source_target_pairs={{0,1},{1,0},{2,3},{3,2},{4,5},{5,4},{6,7},{7,6},{8,9},{9,8},{10,11... | collective-permute-start | bytes 2654216 | tf_op jit(solution)/shard_map/ppermute | solution.py:159
  137.6 12.0 %collective-permute-start.33 = (bf16[2,96,2304]{2,1,0:T(8,128)(2,1)S(1)}, bf16[2,96,2304]{2,1,0:T(8,128)(2,1)S(1)}, u32[]{:S(2)}, u32[]{:S(2)}) collective-permute-start(bf16[2,96,2304]{2,1,0:T(8,128)(2,1)S(1)} %get-tuple-element.158), channel_id=1, source_target_pairs={{0,1},{1,0},{2,3},{3,2},{4,5},{5,4},{6,7},{7,6},{8,9},{9,8},{10,11... | collective-permute-start | bytes 2654216 | tf_op jit(solution)/shard_map/ppermute | solution.py:159
  143.1 16.5 %collective-permute-start.36 = (bf16[2,96,2304]{2,1,0:T(8,128)(2,1)S(1)}, bf16[2,96,2304]{2,1,0:T(8,128)(2,1)S(1)}, u32[]{:S(2)}, u32[]{:S(2)}) collective-permute-start(bf16[2,96,2304]{2,1,0:T(8,128)(2,1)S(1)} %add_convert_fusion.3), channel_id=1, source_target_pairs={{0,4},{1,3},{2,6},{3,1},{4,0},{5,7},{6,2},{7,5},{8,12},{9,11},{10,... | collective-permute-start | bytes 2654216 | tf_op jit(solution)/shard_map/ppermute | solution.py:202
  145.1 11.6 %collective-permute-start.34 = (bf16[288,384]{1,0:T(8,128)(2,1)S(1)}, bf16[288,384]{1,0:T(8,128)(2,1)S(1)}, u32[]{:S(2)}, u32[]{:S(2)}) collective-permute-start(bf16[288,384]{1,0:T(8,128)(2,1)S(1)} %get-tuple-element.161), channel_id=1, source_target_pairs={{0,8},{8,0},{16,24},{24,16},{1,9},{9,1},{17,25},{25,17},{2,10},{10... | collective-permute-start | bytes 663560 | tf_op jit(solution)/shard_map/ppermute | solution.py:1107
  148.3 11.2 %collective-permute-start.35 = (bf16[288,384]{1,0:T(8,128)(2,1)S(1)}, bf16[288,384]{1,0:T(8,128)(2,1)S(1)}, u32[]{:S(2)}, u32[]{:S(2)}) collective-permute-start(bf16[288,384]{1,0:T(8,128)(2,1)S(1)} %get-tuple-element.162), channel_id=1, source_target_pairs={{0,16},{8,24},{16,0},{24,8},{1,17},{9,25},{17,1},{25,9},{2,18},{10... | collective-permute-start | bytes 663560 | tf_op jit(solution)/shard_map/ppermute | solution.py:1107
  159.8 11.2 %collective-permute-start.38 = (bf16[1,96,2304]{2,1,0:T(8,128)(2,1)S(1)}, bf16[1,96,2304]{2,1,0:T(8,128)(2,1)S(1)}, u32[]{:S(2)}, u32[]{:S(2)}) collective-permute-start(bf16[1,96,2304]{2,1,0:T(8,128)(2,1)S(1)} %get-tuple-element.199), channel_id=1, source_target_pairs={{0,2},{1,5},{2,0},{3,7},{4,6},{5,1},{6,4},{7,3},{8,10},{9,13},{10,... | collective-permute-start | bytes 1327112 | tf_op jit(solution)/shard_map/ppermute | solution.py:202
  160.9 7.8 %collective-permute-start.37 = (bf16[288,384]{1,0:T(8,128)(2,1)S(1)}, bf16[288,384]{1,0:T(8,128)(2,1)S(1)}, u32[]{:S(2)}, u32[]{:S(2)}) collective-permute-start(bf16[288,384]{1,0:T(8,128)(2,1)S(1)} %get-tuple-element.163), channel_id=1, source_target_pairs={{0,24},{8,16},{16,8},{24,0},{1,25},{9,17},{17,9},{25,1},{2,26},{10... | collective-permute-start | bytes 663560 | tf_op jit(solution)/shard_map/ppermute | solution.py:1107
  171.1 12.0 %collective-permute-start.41 = (bf16[2,128,768]{2,1,0:T(8,128)(2,1)S(1)}, bf16[2,128,768]{2,1,0:T(8,128)(2,1)S(1)}, u32[]{:S(2)}, u32[]{:S(2)}) collective-permute-start(bf16[2,128,768]{2,1,0:T(8,128)(2,1)S(1)} %get-tuple-element.185), channel_id=1, source_target_pairs={{0,6},{1,7},{2,4},{3,5},{4,2},{5,3},{6,0},{7,1},{8,14},{9,15},{10,... | collective-permute-start | bytes 1179656 | tf_op jit(solution)/shard_map/ppermute | solution.py:172
  173.4 16.4 %collective-permute-start.42 = (bf16[96,640]{1,0:T(8,128)(2,1)S(1)}, bf16[96,640]{1,0:T(8,128)(2,1)S(1)}, u32[]{:S(2)}, u32[]{:S(2)}) collective-permute-start(bf16[96,640]{1,0:T(8,128)(2,1)S(1)} %get-tuple-element.176), channel_id=1, source_target_pairs={{0,8},{8,0},{16,24},{24,16},{1,9},{9,1},{17,25},{25,17},{2,10},{10... | collective-permute-start | bytes 368648 | tf_op jit(solution)/shard_map/ppermute | solution.py:1107
  173.4 16.4 %collective-permute-start.43 = (bf16[96,640]{1,0:T(8,128)(2,1)S(1)}, bf16[96,640]{1,0:T(8,128)(2,1)S(1)}, u32[]{:S(2)}, u32[]{:S(2)}) collective-permute-start(bf16[96,640]{1,0:T(8,128)(2,1)S(1)} %get-tuple-element.177), channel_id=1, source_target_pairs={{0,16},{8,24},{16,0},{24,8},{1,17},{9,25},{17,1},{25,9},{2,18},{10... | collective-permute-start | bytes 368648 | tf_op jit(solution)/shard_map/ppermute | solution.py:1107
  175.5 12.5 %collective-permute-start.40 = (bf16[2,128,768]{2,1,0:T(8,128)(2,1)S(1)}, bf16[2,128,768]{2,1,0:T(8,128)(2,1)S(1)}, u32[]{:S(2)}, u32[]{:S(2)}) collective-permute-start(bf16[2,128,768]{2,1,0:T(8,128)(2,1)S(1)} %get-tuple-element.183), channel_id=1, source_target_pairs={{0,4},{1,5},{2,6},{3,7},{4,0},{5,1},{6,2},{7,3},{8,12},{9,13},{10,... | collective-permute-start | bytes 1179656 | tf_op jit(solution)/shard_map/ppermute | solution.py:172
  176.6 11.4 %collective-permute-start.39 = (bf16[2,128,768]{2,1,0:T(8,128)(2,1)S(1)}, bf16[2,128,768]{2,1,0:T(8,128)(2,1)S(1)}, u32[]{:S(2)}, u32[]{:S(2)}) collective-permute-start(bf16[2,128,768]{2,1,0:T(8,128)(2,1)S(1)} %get-tuple-element.181), channel_id=1, source_target_pairs={{0,2},{1,3},{2,0},{3,1},{4,6},{5,7},{6,4},{7,5},{8,10},{9,11},{10,... | collective-permute-start | bytes 1179656 | tf_op jit(solution)/shard_map/ppermute | solution.py:172
  183.1 6.7 %collective-permute-start.44 = (bf16[96,640]{1,0:T(8,128)(2,1)S(1)}, bf16[96,640]{1,0:T(8,128)(2,1)S(1)}, u32[]{:S(2)}, u32[]{:S(2)}) collective-permute-start(bf16[96,640]{1,0:T(8,128)(2,1)S(1)} %get-tuple-element.178), channel_id=1, source_target_pairs={{0,24},{8,16},{16,8},{24,0},{1,25},{9,17},{17,9},{25,1},{2,26},{10... | collective-permute-start | bytes 368648 | tf_op jit(solution)/shard_map/ppermute | solution.py:1107
  (52 other events, 359.6 us)

commit v2 on v1

--- a/solution.py
+++ b/solution.py
@@ -26,7 +26,7 @@
 NT = (((1,), (1,)), ((), ()))
 TN = (((0,), (0,)), ((), ()))
 LIMITS = {
-    "prepare": 8,
+    "prepare": 60,
     "place_rows": 8,
     "join_qkv": 4,
     "join_rest": 6,
@@ -77,7 +77,7 @@
 
 def params(plan, name):
     size = max(1, plan.groups * plan.local // 1024)
-    return pltpu.CompilerParams(vmem_limit_bytes=min(56, LIMITS[name] * size) * 1024 * 1024)
+    return pltpu.CompilerParams(vmem_limit_bytes=min(60, LIMITS[name] * size) * 1024 * 1024)
 
 
 def cost(microseconds):
@@ -547,8 +547,7 @@
 
 
 def head_part(pair, head, other=None):
-    lane = lax.broadcasted_iota(jnp.int32, pair.shape, 1)
-    keep = (lane < HD) if head == 0 else (lane >= HD)
+    keep = (lax.broadcasted_iota(jnp.int32, pair.shape, 1) // HD) == head
     return jnp.where(keep, pair, jnp.zeros_like(pair) if other is None else other)
 
 
@@ -630,22 +629,25 @@
     kv = refs[:groups]
     dq_ref = refs[groups]
     dkv = refs[groups + 1 : 2 * groups + 1]
-    held, p_ref, ds_ref = refs[2 * groups + 1 :]
-    keys_t = [kv[e][0].T for e in range(groups)]
+    held, p_ref, ds_ref, keys_t, product, grad_t = refs[2 * groups + 1 :]
+    for e in range(groups):
+        keys_t[e] = kv[e][0].T
+    held[...] = jnp.zeros_like(held)
     scale = 1.0 / math.sqrt(HD)
     chunk = 128
     for first in range(0, local, width):
         rows = slice(first, first + width)
-        queries = q_ref[rows, :] * jnp.asarray(scale, BF16)
-        dout = do_ref[rows, :]
-        product = (dout.astype(F32) * o_ref[rows, :]).T
-        parts = []
-        for h in range(2):
+        product[...] = (do_ref[rows, :].astype(F32) * o_ref[rows, :]).T
+
+        @pl.loop(0, 2)
+        def _(h):
+            head = pl.ds(pl.multiple_of(h * HD, HD), HD)
+            queries = q_ref[rows, :] * jnp.asarray(scale, BF16)
             masked_queries = head_part(queries, h, qmask[rows, :])
             head_queries = head_part(queries, h)
-            head_dout = head_part(dout, h)
-            lse = lse_ref[0, h : h + 1, rows]
-            delta = jnp.sum(product[h * HD : (h + 1) * HD, :], axis=0, keepdims=True)
+            head_dout = head_part(do_ref[rows, :], h)
+            lse = lse_ref[0, pl.ds(h, 1), rows]
+            delta = jnp.sum(product[head, :], axis=0, keepdims=True)
             grad_queries = jnp.zeros((HD, width), F32)
             for e in range(groups):
                 for c in range(0, local, chunk):
@@ -654,21 +656,14 @@
                     scores = dot(head_part(kv[e][0, part, :], h, mask), masked_queries, NT)
                     dprobs = dot(kv[e][1, part, :], head_dout, NT)
                     probs = jnp.exp(scores - lse)
-                    p_ref[h, e, part, :] = probs.astype(BF16)
-                    ds_ref[h, e, part, :] = (probs * (dprobs - delta)).astype(BF16)
-                grad_values = dot(p_ref[h, e], head_dout, NN)
-                grad_keys = dot(ds_ref[h, e], head_queries, NN)
-                if first == 0 and h == 0:
-                    held[e, 0] = grad_keys
-                    held[e, 1] = grad_values
-                else:
-                    held[e, 0] += grad_keys
-                    held[e, 1] += grad_values
-                grad_queries = grad_queries + dot(
-                    keys_t[e][h * HD : (h + 1) * HD, :], ds_ref[h, e], NN
-                )
-            parts.append(grad_queries)
-        grad = jnp.concatenate(parts, axis=0).T * scale
+                    p_ref[e, part, :] = probs.astype(BF16)
+                    ds_ref[e, part, :] = (probs * (dprobs - delta)).astype(BF16)
+                held[e, 0] += dot(ds_ref[e], head_queries, NN)
+                held[e, 1] += dot(p_ref[e], head_dout, NN)
+                grad_queries = grad_queries + dot(keys_t[e, head, :], ds_ref[e], NN)
+            grad_t[head, :] = grad_queries
+
+        grad = grad_t[...].T * scale
         dq_ref[rows, :] = rotate_pair(grad, cos_ref[rows, :], sin_ref[rows, :], -1.0).astype(BF16)
     for e in range(groups):
         dkv[e][...] = held[e].astype(BF16)
@@ -707,8 +702,11 @@
         out_shape=[shape_of((local, wide), BF16)] + [shape_of((2, local, wide), BF16)] * groups,
         scratch_shapes=[
             pltpu.VMEM((groups, 2, local, 128), F32),
-            pltpu.VMEM((2, groups, local, width), BF16),
-            pltpu.VMEM((2, groups, local, width), BF16),
+            pltpu.VMEM((groups, local, width), BF16),
+            pltpu.VMEM((groups, local, width), BF16),
+            pltpu.VMEM((groups, 128, local), BF16),
+            pltpu.VMEM((128, width), F32),
+            pltpu.VMEM((128, width), F32),
         ],
         compiler_params=params(plan, "attend_back"),
         cost_estimate=cost(4 * count),

time: 195 us -> 192 us (0.985); the launches traced: 191 us -> 192 us
  Pallas kernels: 79.9 us -> 83.9 us
  local copies, waits for them, and re-layouts: 13 us -> 9.8 us
    unnamed x110 -> x106, local copies, waits for them, and re-layouts: 10.8 us -> 7.1 us
    ppermute x6, starting transfers between devices: 7 us -> 10.3 us  [exchange_rows(): lax.ppermute(pieces[j], 'blk', plan.xor_pairs(2 * j))]
    pallas_call x3, Pallas kernels: 21 us -> 23.4 us  [attend_back(): pl.pallas_call(functools.partial(attend_back_kernel, plan, width), grid=(...]
    ppermute x4, waiting for transfers between devices: 7.69 us -> 5.45 us  [reduce_step(): moved = lax.ppermute(high, 'blk', plan.step_pairs(step))]
    ppermute x6, starting transfers between devices: 10.8 us -> 8.72 us  [reduce_z(): lax.ppermute(pieces[j], 'row', plan.z_pairs(j))]
  transfers between devices with their start and end apart: 45 -> 45, of which waited for: 18 -> 22; matrix products, arithmetic and copies ran while one was open for 3% -> 4% of each run, Pallas kernels for 31% -> 33%
where the time goes in v2:
time: 192 us
  Pallas kernels  83.9 us (44%)
  starting transfers between devices  47.7 us (25%)
  waiting for transfers between devices  42.4 us (22%)
  local copies, waits for them, and re-layouts  9.8 us (5%)
  other arithmetic  4.72 us (2%)
  between operations  3.39 us (2%)
    pallas_call x3, Pallas kernels, attend_back(): pl.pallas_call(functools.partial(attend_back_kernel, plan, width), grid=(...  23.4 us
    pallas_call x1, Pallas kernels, middle(): pl.pallas_call(functools.partial(middle_kernel, plan), in_specs=[SMEM, VM...  19.4 us
    ppermute x6, starting transfers between devices, gather_z(): pieces.append(lax.ppermute(source, 'row', plan.z_pairs(j)))  15.4 us
    pallas_call x2, Pallas kernels, attend(): pl.pallas_call(functools.partial(attend_kernel, plan, width), grid=(HALF_...  12.9 us
    ppermute x6, waiting for transfers between devices, exchange_rows(): lax.ppermute(pieces[j], 'blk', plan.xor_pairs(2 * j))  11.2 us
    ppermute x6, starting transfers between devices, exchange_rows(): lax.ppermute(pieces[j], 'blk', plan.xor_pairs(2 * j))  10.3 us
    ppermute x6, waiting for transfers between devices, reduce_z(): lax.ppermute(pieces[j], 'row', plan.z_pairs(j))  10.1 us
    ppermute x6, waiting for transfers between devices, gather_z(): pieces.append(lax.ppermute(source, 'row', plan.z_pairs(j)))  8.91 us
  transfers between devices with their start and end apart: 45, of which 22 were waited for; matrix products, arithmetic and copies ran while one was open for 4% of the time, Pallas kernels for 33%

profile of v2, /device:TPU:0, one launch (start us, length us, event | category | flops | bytes accessed | tf_op | source)
XLA Modules:
  0.0 191.9 jit_solution(16352336180978688175)
XLA Ops:
  0.7 4.1 %collective-permute-start.1 = (bf16[96,576]{1,0:T(8,128)(2,1)}, bf16[96,576]{1,0:T(8,128)(2,1)S(1)}, u32[]{:S(2)}, u32[]{:S(2)}) collective-permute-start(bf16[96,576]{1,0:T(8,128)(2,1)} %refs_0_.1), channel_id=1, source_target_pairs={{0,16},{8,24},{16,0},{24,8},{1,17},{9,25},{17,1},{25,9},{2,18},{10... | collective-permute-start | bytes 331784 | tf_op jit(solution)/shard_map/ppermute | solution.py:166
  4.8 1.3 collective-permute-start.2
  6.4 1.2 fusion.3.meta.order
  7.6 2.7 %prepare.1 = (bf16[2,128,768]{2,1,0:T(8,128)(2,1)}, bf16[2,128,768]{2,1,0:T(8,128)(2,1)}, bf16[2,128,768]{2,1,0:T(8,128)(2,1)}, bf16[2,128,768]{2,1,0:T(8,128)(2,1)}, bf16[288,384]{1,0:T(8,128)(2,1)}) custom-call(s32[25]{0:T(128)} %fusion.3.meta.order, bf16[4,128,768]{2,1,0:T(8,128)(2,1)} %tokens.1, bf16[4,128,768]{2,1,0:T(8,128)(2,1)} %cotangent.1, ...), custom_call_target="tpu_custom_call" | custom-call | flops 4000000 | bytes 1024 | tf_op jit(solution)/shard_map/prepare/pallas_call | solution.py:262
  10.2 2.4 %collective-permute-start.10 = (bf16[2,128,768]{2,1,0:T(8,128)(2,1)}, bf16[2,128,768]{2,1,0:T(8,128)(2,1)S(1)}, u32[]{:S(2)}, u32[]{:S(2)}) collective-permute-start(bf16[2,128,768]{2,1,0:T(8,128)(2,1)} %get-tuple-element.110), channel_id=1, source_target_pairs={{0,6},{1,7},{2,4},{3,5},{4,2},{5,3},{6,0},{7,1},{8,14},{9,15},{10,... | collective-permute-start | bytes 1179656 | tf_op jit(solution)/shard_map/ppermute | solution.py:172
  18.5 1.6 collective-permute-start.4
  20.1 2.8 %collective-permute-start.5 = (bf16[288,384]{1,0:T(8,128)(2,1)}, bf16[288,384]{1,0:T(8,128)(2,1)S(1)}, u32[]{:S(2)}, u32[]{:S(2)}) collective-permute-start(bf16[288,384]{1,0:T(8,128)(2,1)} %get-tuple-element.113.refs_0_), channel_id=1, source_target_pairs={{0,16},{8,24},{16,0},{24,8},{1,17},{9,25},{17,1},{25,9},{2,18},{10... | collective-permute-start | bytes 663560 | tf_op jit(solution)/shard_map/ppermute | solution.py:166
  23.4 2.9 %collective-permute-start.6 = (bf16[288,384]{1,0:T(8,128)(2,1)}, bf16[288,384]{1,0:T(8,128)(2,1)S(1)}, u32[]{:S(2)}, u32[]{:S(2)}) collective-permute-start(bf16[288,384]{1,0:T(8,128)(2,1)} %get-tuple-element.113.refs_0_), channel_id=1, source_target_pairs={{0,24},{8,16},{16,8},{24,0},{1,25},{9,17},{17,9},{25,1},{2,26},{10... | collective-permute-start | bytes 663560 | tf_op jit(solution)/shard_map/ppermute | solution.py:166
  26.3 1.0 fusion.2
  27.3 2.8 %collective-permute-done.8.refs_1_.refs_3_ = bf16[2,128,768]{2,1,0:T(8,128)(2,1)S(1)} collective-permute-done((bf16[2,128,768]{2,1,0:T(8,128)(2,1)}, bf16[2,128,768]{2,1,0:T(8,128)(2,1)S(1)}, u32[]{:S(2)}, u32[]{:S(2)}) %collective-permute-start.8) | collective-permute-done | bytes 393248 | tf_op jit(solution)/shard_map/ppermute | solution.py:172
  30.6 1.1 collective-permute-start.11
  32.2 1.1 masks.1
  33.2 4.1 %collective-permute-done.5.refs_2_ = bf16[288,384]{1,0:T(8,128)(2,1)S(1)} collective-permute-done((bf16[288,384]{1,0:T(8,128)(2,1)}, bf16[288,384]{1,0:T(8,128)(2,1)S(1)}, u32[]{:S(2)}, u32[]{:S(2)}) %collective-permute-start.5) | collective-permute-done | bytes 221216 | tf_op jit(solution)/shard_map/ppermute | solution.py:166
  38.1 4.0 %collective-permute-start.13 = (bf16[288,384]{1,0:T(8,128)(2,1)S(1)}, bf16[288,384]{1,0:T(8,128)(2,1)S(1)}, u32[]{:S(2)}, u32[]{:S(2)}) collective-permute-start(bf16[288,384]{1,0:T(8,128)(2,1)S(1)} %copy-done.27), channel_id=1, source_target_pairs={{0,8},{8,0},{16,24},{24,16},{1,9},{9,1},{17,25},{25,17},{2,10},{10... | collective-permute-start | bytes 663560 | tf_op jit(solution)/shard_map/ppermute | solution.py:166
  42.6 4.8 %collective-permute-done.13.refs_1_ = bf16[288,384]{1,0:T(8,128)(2,1)S(1)} collective-permute-done((bf16[288,384]{1,0:T(8,128)(2,1)S(1)}, bf16[288,384]{1,0:T(8,128)(2,1)S(1)}, u32[]{:S(2)}, u32[]{:S(2)}) %collective-permute-start.13) | collective-permute-done | bytes 221216 | tf_op jit(solution)/shard_map/ppermute | solution.py:166
  49.3 5.9 %project.1 = (bf16[512,768]{1,0:T(8,128)(2,1)S(1)}, bf16[2,512,384]{2,1,0:T(8,128)(2,1)S(1)}, bf16[2,512,384]{2,1,0:T(8,128)(2,1)S(1)}, bf16[512,768]{1,0:T(8,128)(2,1)S(1)}, f32[8,768]{1,0:T(8,128)S(1)}) custom-call(s32[25]{0:T(128)S(1)} %copy-done.32, f32[512,128]{1,0:T(8,128)S(1)} %get-tuple-element.205.cos_ref.refs_0_, ...), custom_call_target="tpu_custom_call" | custom-call | flops 7000000 | bytes 1024 | tf_op jit(solution)/shard_map/project/pallas_call | solution.py:500
  56.0 1.3 collective-permute-start.18
  58.1 6.4 %attend.2 = (f32[512,384]{1,0:T(8,128)S(1)}, bf16[512,384]{1,0:T(8,128)(2,1)S(1)}, f32[3,2,512]{2,1,0:T(2,128)S(1)}) custom-call(s32[25]{0:T(128)S(1)} %copy-done.32, bf16[1024,128]{1,0:T(8,128)(2,1)S(1)} %get-tuple-element.105.kmask, bf16[512,128]{1,0:T(8,128)(2,1)S(1)} %get-tuple-element.106.qmask, bf16[512,768]{1,0:T(8,128)(2,1)S(1)} %get-tuple-element.118.q_ref, ...), custom_call_target="tpu_custom_call" | custom-call | flops 9000000 | bytes 1024 | tf_op jit(solution)/shard_map/attend/pallas_call | solution.py:605
  65.9 1.0 collective-permute-start.20
  67.5 1.4 collective-permute-done.18.refs_8_
  69.3 6.4 %attend.3 = (f32[512,384]{1,0:T(8,128)S(1)}, bf16[512,384]{1,0:T(8,128)(2,1)S(1)}, f32[3,2,512]{2,1,0:T(2,128)S(1)}) custom-call(s32[25]{0:T(128)S(1)} %copy-done.32, bf16[1024,128]{1,0:T(8,128)(2,1)S(1)} %get-tuple-element.105.kmask, bf16[512,128]{1,0:T(8,128)(2,1)S(1)} %get-tuple-element.106.qmask, bf16[512,768]{1,0:T(8,128)(2,1)S(1)} %get-tuple-element.118.q_ref, ...), custom_call_target="tpu_custom_call" | custom-call | flops 9000000 | bytes 1024 | tf_op jit(solution)/shard_map/attend/pallas_call | solution.py:605
  78.2 2.3 %collective-permute-done.24.refs_13_ = bf16[528,768]{1,0:T(8,128)(2,1)S(1)} collective-permute-done((bf16[528,768]{1,0:T(8,128)(2,1)S(1)}, bf16[528,768]{1,0:T(8,128)(2,1)S(1)}, u32[]{:S(2)}, u32[]{:S(2)}) %collective-permute-start.24) | collective-permute-done | bytes 811040 | tf_op jit(solution)/shard_map/ppermute | solution.py:159
  81.4 19.4 %middle.1 = (bf16[128,768]{1,0:T(8,128)(2,1)}, bf16[128,768]{1,0:T(8,128)(2,1)}, bf16[128,768]{1,0:T(8,128)(2,1)}, bf16[128,768]{1,0:T(8,128)(2,1)}, bf16[512,76...) custom-call(s32[25]{0:T(128)} %fusion.3.meta.order, ...), custom_call_target="tpu_custom_call" | custom-call | flops 20000000 | bytes 1024 | tf_op jit(solution)/shard_map/middle/pallas_call | solution.py:839
  101.4 1.1 copy-done.2
  102.6 4.0 %attend_back.3 = (bf16[512,128]{1,0:T(8,128)(2,1)S(1)}, bf16[2,512,128]{2,1,0:T(8,128)(2,1)S(1)}, bf16[2,512,128]{2,1,0:T(8,128)(2,1)S(1)}) custom-call(s32[25]{0:T(128)S(1)} %copy-done.33, bf16[1024,128]{1,0:T(8,128)(2,1)S(1)} %get-tuple-element.105.kmask, bf16[512,128]{1,0:T(8,128)(2,1)S(1)} %get-tuple-element.106.qmask, ...), custom_call_target="tpu_custom_call" | custom-call | flops 4000000 | bytes 1024 | tf_op jit(solution)/shard_map/attend_back/pallas_call | solution.py:686
  107.0 1.1 collective-permute-start.28
  109.2 7.8 %attend_back.4 = (bf16[512,256]{1,0:T(8,128)(2,1)S(1)}, bf16[2,512,256]{2,1,0:T(8,128)(2,1)S(1)}, bf16[2,512,256]{2,1,0:T(8,128)(2,1)S(1)}) custom-call(s32[25]{0:T(128)S(1)} %copy-done.33, bf16[1024,128]{1,0:T(8,128)(2,1)S(1)} %get-tuple-element.105.kmask, bf16[512,128]{1,0:T(8,128)(2,1)S(1)} %get-tuple-element.106.qmask, ...), custom_call_target="tpu_custom_call" | custom-call | flops 8000000 | bytes 1024 | tf_op jit(solution)/shard_map/attend_back/pallas_call | solution.py:686
  117.1 11.6 %attend_back.5 = (bf16[512,384]{1,0:T(8,128)(2,1)S(1)}, bf16[2,512,384]{2,1,0:T(8,128)(2,1)S(1)}, bf16[2,512,384]{2,1,0:T(8,128)(2,1)S(1)}) custom-call(s32[25]{0:T(128)S(1)} %copy-done.33, bf16[1024,128]{1,0:T(8,128)(2,1)S(1)} %get-tuple-element.105.kmask, bf16[512,128]{1,0:T(8,128)(2,1)S(1)} %get-tuple-element.106.qmask, ...), custom_call_target="tpu_custom_call" | custom-call | flops 12000000 | bytes 1024 | tf_op jit(solution)/shard_map/attend_back/pallas_call | solution.py:686
  129.6 1.0 collective-permute-start.31
  130.7 1.1 collective-permute-done.29.refs_9_
  131.8 6.1 %back_weight.1 = (bf16[3,512,768]{2,1,0:T(8,128)(2,1)S(1)}, bf16[2,96,2304]{2,1,0:T(8,128)(2,1)S(1)}, bf16[2,96,2304]{2,1,0:T(8,128)(2,1)S(1)}, bf16[2,96,2304]{2,1,0:T(8,128)(2,1)S(1)}, bf16[2,96,2304]{2,1,0:T(8,128)(2,1)S(1)}) custom-call(s32[25]{0:T(128)S(1)} %copy-done.33, f32[512,128]{1,0:T(8,128)S(1)} %get-tuple-element.205.cos_ref.refs_0_, ...), custom_call_target="tpu_custom_call" | custom-call | flops 6000000 | bytes 1024 | tf_op jit(solution)/shard_map/back_weight/pallas_call | solution.py:927
  138.5 3.5 %collective-permute-done.31 = bf16[1,528,768]{2,1,0:T(8,128)(2,1)S(1)} collective-permute-done((bf16[1,528,768]{2,1,0:T(8,128)(2,1)S(1)}, bf16[1,528,768]{2,1,0:T(8,128)(2,1)S(1)}, u32[]{:S(2)}, u32[]{:S(2)}) %collective-permute-start.31) | collective-permute-done | bytes 811040 | tf_op jit(solution)/shard_map/ppermute | solution.py:202
  142.4 1.0 collective-permute-start.36
  144.5 3.4 %collective-permute-start.34 = (bf16[288,384]{1,0:T(8,128)(2,1)S(1)}, bf16[288,384]{1,0:T(8,128)(2,1)S(1)}, u32[]{:S(2)}, u32[]{:S(2)}) collective-permute-start(bf16[288,384]{1,0:T(8,128)(2,1)S(1)} %get-tuple-element.161), channel_id=1, source_target_pairs={{0,8},{8,0},{16,24},{24,16},{1,9},{9,1},{17,25},{25,17},{2,10},{10... | collective-permute-start | bytes 663560 | tf_op jit(solution)/shard_map/ppermute | solution.py:1105
  148.0 1.2 collective-permute-start.35
  149.5 5.6 %back_in.1 = (bf16[2,128,768]{2,1,0:T(8,128)(2,1)S(1)}, bf16[2,128,768]{2,1,0:T(8,128)(2,1)S(1)}, bf16[2,128,768]{2,1,0:T(8,128)(2,1)S(1)}, bf16[2,128,768]{2,1,0:T(8,128)(2,1)S(1)}) custom-call(s32[25]{0:T(128)S(1)} %copy-done.33, bf16[3,512,768]{2,1,0:T(8,128)(2,1)S(1)} %get-tuple-element.153.dp_ref, f32[512,768]{1,0:T(8,128)S(1)} %copy-done.20, ...), custom_call_target="tpu_custom_call" | custom-call | flops 7000000 | bytes 1024 | tf_op jit(solution)/shard_map/back_in/pallas_call | solution.py:976
  155.2 1.9 collective-permute-done.34.refs_1_
  157.1 2.5 %collective-permute-done.35.refs_2_ = bf16[288,384]{1,0:T(8,128)(2,1)S(1)} collective-permute-done((bf16[288,384]{1,0:T(8,128)(2,1)S(1)}, bf16[288,384]{1,0:T(8,128)(2,1)S(1)}, u32[]{:S(2)}, u32[]{:S(2)}) %collective-permute-start.35) | collective-permute-done | bytes 221216 | tf_op jit(solution)/shard_map/ppermute | solution.py:1105
  159.7 1.1 collective-permute-start.38
  160.9 2.6 %collective-permute-start.37 = (bf16[288,384]{1,0:T(8,128)(2,1)S(1)}, bf16[288,384]{1,0:T(8,128)(2,1)S(1)}, u32[]{:S(2)}, u32[]{:S(2)}) collective-permute-start(bf16[288,384]{1,0:T(8,128)(2,1)S(1)} %get-tuple-element.163), channel_id=1, source_target_pairs={{0,24},{8,16},{16,8},{24,0},{1,25},{9,17},{17,9},{25,1},{2,26},{10... | collective-permute-start | bytes 663560 | tf_op jit(solution)/shard_map/ppermute | solution.py:1105
  163.4 5.3 %collective-permute-done.37.refs_3_ = bf16[288,384]{1,0:T(8,128)(2,1)S(1)} collective-permute-done((bf16[288,384]{1,0:T(8,128)(2,1)S(1)}, bf16[288,384]{1,0:T(8,128)(2,1)S(1)}, u32[]{:S(2)}, u32[]{:S(2)}) %collective-permute-start.37) | collective-permute-done | bytes 221216 | tf_op jit(solution)/shard_map/ppermute | solution.py:1105
  168.7 1.9 %collective-permute-done.38 = bf16[1,96,2304]{2,1,0:T(8,128)(2,1)S(1)} collective-permute-done((bf16[1,96,2304]{2,1,0:T(8,128)(2,1)S(1)}, bf16[1,96,2304]{2,1,0:T(8,128)(2,1)S(1)}, u32[]{:S(2)}, u32[]{:S(2)}) %collective-permute-start.38) | collective-permute-done | bytes 442400 | tf_op jit(solution)/shard_map/ppermute | solution.py:202
  170.8 4.6 %collective-permute-start.41 = (bf16[2,128,768]{2,1,0:T(8,128)(2,1)S(1)}, bf16[2,128,768]{2,1,0:T(8,128)(2,1)S(1)}, u32[]{:S(2)}, u32[]{:S(2)}) collective-permute-start(bf16[2,128,768]{2,1,0:T(8,128)(2,1)S(1)} %get-tuple-element.185), channel_id=1, source_target_pairs={{0,6},{1,7},{2,4},{3,5},{4,2},{5,3},{6,0},{7,1},{8,14},{9,15},{10,... | collective-permute-start | bytes 1179656 | tf_op jit(solution)/shard_map/ppermute | solution.py:172
  177.3 1.3 collective-permute-start.39
  179.5 4.9 %collective-permute-done.41.refs_3_ = bf16[2,128,768]{2,1,0:T(8,128)(2,1)S(1)} collective-permute-done((bf16[2,128,768]{2,1,0:T(8,128)(2,1)S(1)}, bf16[2,128,768]{2,1,0:T(8,128)(2,1)S(1)}, u32[]{:S(2)}, u32[]{:S(2)}) %collective-permute-start.41) | collective-permute-done | bytes 393248 | tf_op jit(solution)/shard_map/ppermute | solution.py:172
  184.4 1.4 collective-permute-start.44
  187.3 1.5 collective-permute-done.39.refs_1_
  188.8 1.8 place_rows.1
  (194 shorter events, 27.0 us)
Async XLA Ops:
  0.7 16.4 %collective-permute-start.1 = (bf16[96,576]{1,0:T(8,128)(2,1)}, bf16[96,576]{1,0:T(8,128)(2,1)S(1)}, u32[]{:S(2)}, u32[]{:S(2)}) collective-permute-start(bf16[96,576]{1,0:T(8,128)(2,1)} %refs_0_.1), channel_id=1, source_target_pairs={{0,16},{8,24},{16,0},{24,8},{1,17},{9,25},{17,1},{25,9},{2,18},{10... | collective-permute-start | bytes 331784 | tf_op jit(solution)/shard_map/ppermute | solution.py:166
  4.8 12.9 %collective-permute-start.2 = (bf16[96,576]{1,0:T(8,128)(2,1)}, bf16[96,576]{1,0:T(8,128)(2,1)S(1)}, u32[]{:S(2)}, u32[]{:S(2)}) collective-permute-start(bf16[96,576]{1,0:T(8,128)(2,1)} %refs_0_.1), channel_id=1, source_target_pairs={{0,24},{8,16},{16,8},{24,0},{1,25},{9,17},{17,9},{25,1},{2,26},{10... | collective-permute-start | bytes 331784 | tf_op jit(solution)/shard_map/ppermute | solution.py:166
  6.1 11.6 %collective-permute-start = (bf16[96,576]{1,0:T(8,128)(2,1)}, bf16[96,576]{1,0:T(8,128)(2,1)S(1)}, u32[]{:S(2)}, u32[]{:S(2)}) collective-permute-start(bf16[96,576]{1,0:T(8,128)(2,1)} %refs_0_.1), channel_id=1, source_target_pairs={{0,8},{8,0},{16,24},{24,16},{1,9},{9,1},{17,25},{25,17},{2,10},{10... | collective-permute-start | bytes 331784 | tf_op jit(solution)/shard_map/ppermute | solution.py:166
  10.2 27.8 %copy-start.27 = (bf16[288,384]{1,0:T(8,128)(2,1)S(1)}, bf16[288,384]{1,0:T(8,128)(2,1)}, u32[]{:S(2)}) copy-start(bf16[288,384]{1,0:T(8,128)(2,1)} %get-tuple-element.113.refs_0_) | copy-start | bytes 663556
  10.2 13.2 %collective-permute-start.10 = (bf16[2,128,768]{2,1,0:T(8,128)(2,1)}, bf16[2,128,768]{2,1,0:T(8,128)(2,1)S(1)}, u32[]{:S(2)}, u32[]{:S(2)}) collective-permute-start(bf16[2,128,768]{2,1,0:T(8,128)(2,1)} %get-tuple-element.110), channel_id=1, source_target_pairs={{0,6},{1,7},{2,4},{3,5},{4,2},{5,3},{6,0},{7,1},{8,14},{9,15},{10,... | collective-permute-start | bytes 1179656 | tf_op jit(solution)/shard_map/ppermute | solution.py:172
  12.7 17.5 %collective-permute-start.8 = (bf16[2,128,768]{2,1,0:T(8,128)(2,1)}, bf16[2,128,768]{2,1,0:T(8,128)(2,1)S(1)}, u32[]{:S(2)}, u32[]{:S(2)}) collective-permute-start(bf16[2,128,768]{2,1,0:T(8,128)(2,1)} %get-tuple-element.108), channel_id=1, source_target_pairs={{0,2},{1,3},{2,0},{3,1},{4,6},{5,7},{6,4},{7,5},{8,10},{9,11},{10,... | collective-permute-start | bytes 1179656 | tf_op jit(solution)/shard_map/ppermute | solution.py:172
  17.1 13.6 %collective-permute-start.9 = (bf16[2,128,768]{2,1,0:T(8,128)(2,1)}, bf16[2,128,768]{2,1,0:T(8,128)(2,1)S(1)}, u32[]{:S(2)}, u32[]{:S(2)}) collective-permute-start(bf16[2,128,768]{2,1,0:T(8,128)(2,1)} %get-tuple-element.109), channel_id=1, source_target_pairs={{0,4},{1,5},{2,6},{3,7},{4,0},{5,1},{6,2},{7,3},{8,12},{9,13},{10,... | collective-permute-start | bytes 1179656 | tf_op jit(solution)/shard_map/ppermute | solution.py:172
  18.5 19.6 %collective-permute-start.4 = (bf16[96,2432]{1,0:T(8,128)(2,1)S(1)}, bf16[96,2432]{1,0:T(8,128)(2,1)S(1)}, u32[]{:S(2)}, u32[]{:S(2)}) collective-permute-start(bf16[96,2432]{1,0:T(8,128)(2,1)S(1)} %join_qkv.1.refs_4_.refs_8_.weight), channel_id=1, source_target_pairs={{0,2},{1,5},{2,0},{3,7},{4,6},{5,1},{6,4},{7,3},{8,10},{9,13},{10,... | collective-permute-start | bytes 1400840 | tf_op jit(solution)/shard_map/ppermute | solution.py:178
  20.1 17.2 %collective-permute-start.5 = (bf16[288,384]{1,0:T(8,128)(2,1)}, bf16[288,384]{1,0:T(8,128)(2,1)S(1)}, u32[]{:S(2)}, u32[]{:S(2)}) collective-permute-start(bf16[288,384]{1,0:T(8,128)(2,1)} %get-tuple-element.113.refs_0_), channel_id=1, source_target_pairs={{0,16},{8,24},{16,0},{24,8},{1,17},{9,25},{17,1},{25,9},{2,18},{10... | collective-permute-start | bytes 663560 | tf_op jit(solution)/shard_map/ppermute | solution.py:166
  23.4 25.8 %copy-start.6 = (bf16[2,128,768]{2,1,0:T(8,128)(2,1)}, bf16[2,128,768]{2,1,0:T(8,128)(2,1)S(1)}, u32[]{:S(2)}) copy-start(bf16[2,128,768]{2,1,0:T(8,128)(2,1)S(1)} %collective-permute-done.10.refs_3_.refs_5_) | copy-start | bytes 1179652
  23.4 13.9 %collective-permute-start.6 = (bf16[288,384]{1,0:T(8,128)(2,1)}, bf16[288,384]{1,0:T(8,128)(2,1)S(1)}, u32[]{:S(2)}, u32[]{:S(2)}) collective-permute-start(bf16[288,384]{1,0:T(8,128)(2,1)} %get-tuple-element.113.refs_0_), channel_id=1, source_target_pairs={{0,24},{8,16},{16,8},{24,0},{1,25},{9,17},{17,9},{25,1},{2,26},{10... | collective-permute-start | bytes 663560 | tf_op jit(solution)/shard_map/ppermute | solution.py:166
  30.2 25.0 %copy-start.8 = (bf16[2,128,768]{2,1,0:T(8,128)(2,1)}, bf16[2,128,768]{2,1,0:T(8,128)(2,1)S(1)}, u32[]{:S(2)}) copy-start(bf16[2,128,768]{2,1,0:T(8,128)(2,1)S(1)} %collective-permute-done.8.refs_1_.refs_3_) | copy-start | bytes 1179652
  30.6 12.0 %collective-permute-start.11 = (bf16[96,2432]{1,0:T(8,128)(2,1)S(1)}, bf16[96,2432]{1,0:T(8,128)(2,1)S(1)}, u32[]{:S(2)}, u32[]{:S(2)}) collective-permute-start(bf16[96,2432]{1,0:T(8,128)(2,1)S(1)} %join_qkv.1.refs_4_.refs_8_.weight), channel_id=1, source_target_pairs={{0,4},{1,3},{2,6},{3,1},{4,0},{5,7},{6,2},{7,5},{8,12},{9,11},{10,... | collective-permute-start | bytes 1400840 | tf_op jit(solution)/shard_map/ppermute | solution.py:179
  38.0 9.4 %collective-permute-start.14 = (bf16[96,2432]{1,0:T(8,128)(2,1)S(1)}, bf16[96,2432]{1,0:T(8,128)(2,1)S(1)}, u32[]{:S(2)}, u32[]{:S(2)}) collective-permute-start(bf16[96,2432]{1,0:T(8,128)(2,1)S(1)} %collective-permute-done.4.refs_5_.refs_9_), channel_id=1, source_target_pairs={{0,4},{1,3},{2,6},{3,1},{4,0},{5,7},{6,2},{7,5},{8,12},{9,11},{10,... | collective-permute-start | bytes 1400840 | tf_op jit(solution)/shard_map/ppermute | solution.py:187
  38.1 9.3 %collective-permute-start.13 = (bf16[288,384]{1,0:T(8,128)(2,1)S(1)}, bf16[288,384]{1,0:T(8,128)(2,1)S(1)}, u32[]{:S(2)}, u32[]{:S(2)}) collective-permute-start(bf16[288,384]{1,0:T(8,128)(2,1)S(1)} %copy-done.27), channel_id=1, source_target_pairs={{0,8},{8,0},{16,24},{24,16},{1,9},{9,1},{17,25},{25,17},{2,10},{10... | collective-permute-start | bytes 663560 | tf_op jit(solution)/shard_map/ppermute | solution.py:166
  42.1 5.4 %collective-permute-start.3 = (bf16[96,2432]{1,0:T(8,128)(2,1)S(1)}, bf16[96,2432]{1,0:T(8,128)(2,1)S(1)}, u32[]{:S(2)}, u32[]{:S(2)}) collective-permute-start(bf16[96,2432]{1,0:T(8,128)(2,1)S(1)} %join_qkv.1.refs_4_.refs_8_.weight), channel_id=1, source_target_pairs={{0,1},{1,0},{2,3},{3,2},{4,5},{5,4},{6,7},{7,6},{8,9},{9,8},{10,11... | collective-permute-start | bytes 1400840 | tf_op jit(solution)/shard_map/ppermute | solution.py:159
  42.1 5.4 %collective-permute-start.7 = (bf16[96,2432]{1,0:T(8,128)(2,1)S(1)}, bf16[96,2432]{1,0:T(8,128)(2,1)S(1)}, u32[]{:S(2)}, u32[]{:S(2)}) collective-permute-start(bf16[96,2432]{1,0:T(8,128)(2,1)S(1)} %collective-permute-done.4.refs_5_.refs_9_), channel_id=1, source_target_pairs={{0,1},{1,0},{2,3},{3,2},{4,5},{5,4},{6,7},{7,6},{8,9},{9,8},{10,11... | collective-permute-start | bytes 1400840 | tf_op jit(solution)/shard_map/ppermute | solution.py:159
  42.6 4.9 %collective-permute-start.12 = (bf16[96,2432]{1,0:T(8,128)(2,1)S(1)}, bf16[96,2432]{1,0:T(8,128)(2,1)S(1)}, u32[]{:S(2)}, u32[]{:S(2)}) collective-permute-start(bf16[96,2432]{1,0:T(8,128)(2,1)S(1)} %collective-permute-done.11.refs_6_.refs_10_), channel_id=1, source_target_pairs={{0,1},{1,0},{2,3},{3,2},{4,5},{5,4},{6,7},{7,6},{8,9},{9,8},{10,11... | collective-permute-start | bytes 1400840 | tf_op jit(solution)/shard_map/ppermute | solution.py:159
  47.4 1.8 collective-permute-start.15
  48.4 17.6 %collective-permute-start.17 = (bf16[528,768]{1,0:T(8,128)(2,1)S(1)}, bf16[528,768]{1,0:T(8,128)(2,1)S(1)}, u32[]{:S(2)}, u32[]{:S(2)}) collective-permute-start(bf16[528,768]{1,0:T(8,128)(2,1)S(1)} %join_rest.1.refs_6_.weight), channel_id=1, source_target_pairs={{0,2},{1,5},{2,0},{3,7},{4,6},{5,1},{6,4},{7,3},{8,10},{9,13},{10,... | collective-permute-start | bytes 2433032 | tf_op jit(solution)/shard_map/ppermute | solution.py:178
  55.8 2.3 %collective-permute-start.16 = (bf16[2,512,384]{2,1,0:T(8,128)(2,1)S(1)}, bf16[2,512,384]{2,1,0:T(8,128)(2,1)S(1)}, u32[]{:S(2)}, u32[]{:S(2)}) collective-permute-start(bf16[2,512,384]{2,1,0:T(8,128)(2,1)S(1)} %get-tuple-element.119.refs_0_), channel_id=1, source_target_pairs={{0,1},{1,0},{2,3},{3,2},{4,5},{5,4},{6,7},{7,6},{8,9},{9,8},{10,11... | collective-permute-start | bytes 2359304 | tf_op jit(solution)/shard_map/ppermute | solution.py:1234
  56.0 12.9 %collective-permute-start.18 = (bf16[528,768]{1,0:T(8,128)(2,1)S(1)}, bf16[528,768]{1,0:T(8,128)(2,1)S(1)}, u32[]{:S(2)}, u32[]{:S(2)}) collective-permute-start(bf16[528,768]{1,0:T(8,128)(2,1)S(1)} %join_rest.1.refs_6_.weight), channel_id=1, source_target_pairs={{0,4},{1,3},{2,6},{3,1},{4,0},{5,7},{6,2},{7,5},{8,12},{9,11},{10,... | collective-permute-start | bytes 2433032 | tf_op jit(solution)/shard_map/ppermute | solution.py:179
  65.9 12.3 %collective-permute-start.20 = (bf16[528,768]{1,0:T(8,128)(2,1)S(1)}, bf16[528,768]{1,0:T(8,128)(2,1)S(1)}, u32[]{:S(2)}, u32[]{:S(2)}) collective-permute-start(bf16[528,768]{1,0:T(8,128)(2,1)S(1)} %collective-permute-done.17.refs_7_), channel_id=1, source_target_pairs={{0,4},{1,3},{2,6},{3,1},{4,0},{5,7},{6,2},{7,5},{8,12},{9,11},{10,... | collective-permute-start | bytes 2433032 | tf_op jit(solution)/shard_map/ppermute | solution.py:187
  67.0 2.3 %collective-permute-start.19 = (bf16[2,512,384]{2,1,0:T(8,128)(2,1)S(1)}, bf16[2,512,384]{2,1,0:T(8,128)(2,1)S(1)}, u32[]{:S(2)}, u32[]{:S(2)}) collective-permute-start(bf16[2,512,384]{2,1,0:T(8,128)(2,1)S(1)} %get-tuple-element.122.refs_0_), channel_id=1, source_target_pairs={{0,1},{1,0},{2,3},{3,2},{4,5},{5,4},{6,7},{7,6},{8,9},{9,8},{10,11... | collective-permute-start | bytes 2359304 | tf_op jit(solution)/shard_map/ppermute | solution.py:1234
  67.0 11.2 %collective-permute-start.21 = (bf16[528,768]{1,0:T(8,128)(2,1)S(1)}, bf16[528,768]{1,0:T(8,128)(2,1)S(1)}, u32[]{:S(2)}, u32[]{:S(2)}) collective-permute-start(bf16[528,768]{1,0:T(8,128)(2,1)S(1)} %join_rest.1.refs_6_.weight), channel_id=1, source_target_pairs={{0,1},{1,0},{2,3},{3,2},{4,5},{5,4},{6,7},{7,6},{8,9},{9,8},{10,11... | collective-permute-start | bytes 2433032 | tf_op jit(solution)/shard_map/ppermute | solution.py:159
  67.5 10.7 %collective-permute-start.22 = (bf16[528,768]{1,0:T(8,128)(2,1)S(1)}, bf16[528,768]{1,0:T(8,128)(2,1)S(1)}, u32[]{:S(2)}, u32[]{:S(2)}) collective-permute-start(bf16[528,768]{1,0:T(8,128)(2,1)S(1)} %collective-permute-done.17.refs_7_), channel_id=1, source_target_pairs={{0,1},{1,0},{2,3},{3,2},{4,5},{5,4},{6,7},{7,6},{8,9},{9,8},{10,11... | collective-permute-start | bytes 2433032 | tf_op jit(solution)/shard_map/ppermute | solution.py:159
  68.9 9.3 %collective-permute-start.23 = (bf16[528,768]{1,0:T(8,128)(2,1)S(1)}, bf16[528,768]{1,0:T(8,128)(2,1)S(1)}, u32[]{:S(2)}, u32[]{:S(2)}) collective-permute-start(bf16[528,768]{1,0:T(8,128)(2,1)S(1)} %collective-permute-done.18.refs_8_), channel_id=1, source_target_pairs={{0,1},{1,0},{2,3},{3,2},{4,5},{5,4},{6,7},{7,6},{8,9},{9,8},{10,11... | collective-permute-start | bytes 2433032 | tf_op jit(solution)/shard_map/ppermute | solution.py:159
  78.2 2.3 %collective-permute-start.24 = (bf16[528,768]{1,0:T(8,128)(2,1)S(1)}, bf16[528,768]{1,0:T(8,128)(2,1)S(1)}, u32[]{:S(2)}, u32[]{:S(2)}) collective-permute-start(bf16[528,768]{1,0:T(8,128)(2,1)S(1)} %collective-permute-done.20.refs_9_), channel_id=1, source_target_pairs={{0,1},{1,0},{2,3},{3,2},{4,5},{5,4},{6,7},{7,6},{8,9},{9,8},{10,11... | collective-permute-start | bytes 2433032 | tf_op jit(solution)/shard_map/ppermute | solution.py:159
  100.8 5.7 %collective-permute-start.26 = (bf16[2,528,768]{2,1,0:T(8,128)(2,1)}, bf16[2,528,768]{2,1,0:T(8,128)(2,1)S(1)}, u32[]{:S(2)}, u32[]{:S(2)}) collective-permute-start(bf16[2,528,768]{2,1,0:T(8,128)(2,1)} %get-tuple-element.136), channel_id=1, source_target_pairs={{0,1},{1,0},{2,3},{3,2},{4,5},{5,4},{6,7},{7,6},{8,9},{9,8},{10,11... | collective-permute-start | bytes 4866056 | tf_op jit(solution)/shard_map/ppermute | solution.py:159
  101.0 7.1 %collective-permute-start.25 = (bf16[2,528,768]{2,1,0:T(8,128)(2,1)}, bf16[2,528,768]{2,1,0:T(8,128)(2,1)S(1)}, u32[]{:S(2)}, u32[]{:S(2)}) collective-permute-start(bf16[2,528,768]{2,1,0:T(8,128)(2,1)} %get-tuple-element.133), channel_id=1, source_target_pairs={{0,1},{1,0},{2,3},{3,2},{4,5},{5,4},{6,7},{7,6},{8,9},{9,8},{10,11... | collective-permute-start | bytes 4866056 | tf_op jit(solution)/shard_map/ppermute | solution.py:159
  107.0 22.3 %collective-permute-start.28 = (bf16[2,528,768]{2,1,0:T(8,128)(2,1)S(1)}, bf16[2,528,768]{2,1,0:T(8,128)(2,1)S(1)}, u32[]{:S(2)}, u32[]{:S(2)}) collective-permute-start(bf16[2,528,768]{2,1,0:T(8,128)(2,1)S(1)} %add_convert_fusion), channel_id=1, source_target_pairs={{0,4},{1,3},{2,6},{3,1},{4,0},{5,7},{6,2},{7,5},{8,12},{9,11},{10,... | collective-permute-start | bytes 4866056 | tf_op jit(solution)/shard_map/ppermute | solution.py:202
  108.1 9.0 %collective-permute-start.27 = (bf16[2,512,128]{2,1,0:T(8,128)(2,1)S(1)}, bf16[2,512,128]{2,1,0:T(8,128)(2,1)S(1)}, u32[]{:S(2)}, u32[]{:S(2)}) collective-permute-start(bf16[2,512,128]{2,1,0:T(8,128)(2,1)S(1)} %get-tuple-element.139), channel_id=1, source_target_pairs={{0,1},{1,0},{2,3},{3,2},{4,5},{5,4},{6,7},{7,6},{8,9},{9,8},{10,11... | collective-permute-start | bytes 786440 | tf_op jit(solution)/shard_map/ppermute | solution.py:1274
  128.7 3.1 %collective-permute-start.30 = (bf16[2,512,384]{2,1,0:T(8,128)(2,1)S(1)}, bf16[2,512,384]{2,1,0:T(8,128)(2,1)S(1)}, u32[]{:S(2)}, u32[]{:S(2)}) collective-permute-start(bf16[2,512,384]{2,1,0:T(8,128)(2,1)S(1)} %get-tuple-element.151), channel_id=1, source_target_pairs={{0,1},{1,0},{2,3},{3,2},{4,5},{5,4},{6,7},{7,6},{8,9},{9,8},{10,11... | collective-permute-start | bytes 2359304 | tf_op jit(solution)/shard_map/ppermute | solution.py:1274
  128.7 3.0 %collective-permute-start.29 = (bf16[2,512,256]{2,1,0:T(8,128)(2,1)S(1)}, bf16[2,512,256]{2,1,0:T(8,128)(2,1)S(1)}, u32[]{:S(2)}, u32[]{:S(2)}) collective-permute-start(bf16[2,512,256]{2,1,0:T(8,128)(2,1)S(1)} %get-tuple-element.149), channel_id=1, source_target_pairs={{0,1},{1,0},{2,3},{3,2},{4,5},{5,4},{6,7},{7,6},{8,9},{9,8},{10,11... | collective-permute-start | bytes 1572872 | tf_op jit(solution)/shard_map/ppermute | solution.py:1274
  129.6 12.3 %collective-permute-start.31 = (bf16[1,528,768]{2,1,0:T(8,128)(2,1)S(1)}, bf16[1,528,768]{2,1,0:T(8,128)(2,1)S(1)}, u32[]{:S(2)}, u32[]{:S(2)}) collective-permute-start(bf16[1,528,768]{2,1,0:T(8,128)(2,1)S(1)} %get-tuple-element.196), channel_id=1, source_target_pairs={{0,2},{1,5},{2,0},{3,7},{4,6},{5,1},{6,4},{7,3},{8,10},{9,13},{10,... | collective-permute-start | bytes 2433032 | tf_op jit(solution)/shard_map/ppermute | solution.py:202
  137.9 4.3 %collective-permute-start.32 = (bf16[2,96,2304]{2,1,0:T(8,128)(2,1)S(1)}, bf16[2,96,2304]{2,1,0:T(8,128)(2,1)S(1)}, u32[]{:S(2)}, u32[]{:S(2)}) collective-permute-start(bf16[2,96,2304]{2,1,0:T(8,128)(2,1)S(1)} %get-tuple-element.156), channel_id=1, source_target_pairs={{0,1},{1,0},{2,3},{3,2},{4,5},{5,4},{6,7},{7,6},{8,9},{9,8},{10,11... | collective-permute-start | bytes 2654216 | tf_op jit(solution)/shard_map/ppermute | solution.py:159
  138.1 11.1 %collective-permute-start.33 = (bf16[2,96,2304]{2,1,0:T(8,128)(2,1)S(1)}, bf16[2,96,2304]{2,1,0:T(8,128)(2,1)S(1)}, u32[]{:S(2)}, u32[]{:S(2)}) collective-permute-start(bf16[2,96,2304]{2,1,0:T(8,128)(2,1)S(1)} %get-tuple-element.158), channel_id=1, source_target_pairs={{0,1},{1,0},{2,3},{3,2},{4,5},{5,4},{6,7},{7,6},{8,9},{9,8},{10,11... | collective-permute-start | bytes 2654216 | tf_op jit(solution)/shard_map/ppermute | solution.py:159
  142.4 17.1 %collective-permute-start.36 = (bf16[2,96,2304]{2,1,0:T(8,128)(2,1)S(1)}, bf16[2,96,2304]{2,1,0:T(8,128)(2,1)S(1)}, u32[]{:S(2)}, u32[]{:S(2)}) collective-permute-start(bf16[2,96,2304]{2,1,0:T(8,128)(2,1)S(1)} %add_convert_fusion.3), channel_id=1, source_target_pairs={{0,4},{1,3},{2,6},{3,1},{4,0},{5,7},{6,2},{7,5},{8,12},{9,11},{10,... | collective-permute-start | bytes 2654216 | tf_op jit(solution)/shard_map/ppermute | solution.py:202
  144.5 12.5 %collective-permute-start.34 = (bf16[288,384]{1,0:T(8,128)(2,1)S(1)}, bf16[288,384]{1,0:T(8,128)(2,1)S(1)}, u32[]{:S(2)}, u32[]{:S(2)}) collective-permute-start(bf16[288,384]{1,0:T(8,128)(2,1)S(1)} %get-tuple-element.161), channel_id=1, source_target_pairs={{0,8},{8,0},{16,24},{24,16},{1,9},{9,1},{17,25},{25,17},{2,10},{10... | collective-permute-start | bytes 663560 | tf_op jit(solution)/shard_map/ppermute | solution.py:1105
  148.0 11.5 %collective-permute-start.35 = (bf16[288,384]{1,0:T(8,128)(2,1)S(1)}, bf16[288,384]{1,0:T(8,128)(2,1)S(1)}, u32[]{:S(2)}, u32[]{:S(2)}) collective-permute-start(bf16[288,384]{1,0:T(8,128)(2,1)S(1)} %get-tuple-element.162), channel_id=1, source_target_pairs={{0,16},{8,24},{16,0},{24,8},{1,17},{9,25},{17,1},{25,9},{2,18},{10... | collective-permute-start | bytes 663560 | tf_op jit(solution)/shard_map/ppermute | solution.py:1105
  159.7 10.9 %collective-permute-start.38 = (bf16[1,96,2304]{2,1,0:T(8,128)(2,1)S(1)}, bf16[1,96,2304]{2,1,0:T(8,128)(2,1)S(1)}, u32[]{:S(2)}, u32[]{:S(2)}) collective-permute-start(bf16[1,96,2304]{2,1,0:T(8,128)(2,1)S(1)} %get-tuple-element.199), channel_id=1, source_target_pairs={{0,2},{1,5},{2,0},{3,7},{4,6},{5,1},{6,4},{7,3},{8,10},{9,13},{10,... | collective-permute-start | bytes 1327112 | tf_op jit(solution)/shard_map/ppermute | solution.py:202
  160.9 7.8 %collective-permute-start.37 = (bf16[288,384]{1,0:T(8,128)(2,1)S(1)}, bf16[288,384]{1,0:T(8,128)(2,1)S(1)}, u32[]{:S(2)}, u32[]{:S(2)}) collective-permute-start(bf16[288,384]{1,0:T(8,128)(2,1)S(1)} %get-tuple-element.163), channel_id=1, source_target_pairs={{0,24},{8,16},{16,8},{24,0},{1,25},{9,17},{17,9},{25,1},{2,26},{10... | collective-permute-start | bytes 663560 | tf_op jit(solution)/shard_map/ppermute | solution.py:1105
  170.8 13.6 %collective-permute-start.41 = (bf16[2,128,768]{2,1,0:T(8,128)(2,1)S(1)}, bf16[2,128,768]{2,1,0:T(8,128)(2,1)S(1)}, u32[]{:S(2)}, u32[]{:S(2)}) collective-permute-start(bf16[2,128,768]{2,1,0:T(8,128)(2,1)S(1)} %get-tuple-element.185), channel_id=1, source_target_pairs={{0,6},{1,7},{2,4},{3,5},{4,2},{5,3},{6,0},{7,1},{8,14},{9,15},{10,... | collective-permute-start | bytes 1179656 | tf_op jit(solution)/shard_map/ppermute | solution.py:172
  176.3 14.3 %collective-permute-start.42 = (bf16[96,640]{1,0:T(8,128)(2,1)S(1)}, bf16[96,640]{1,0:T(8,128)(2,1)S(1)}, u32[]{:S(2)}, u32[]{:S(2)}) collective-permute-start(bf16[96,640]{1,0:T(8,128)(2,1)S(1)} %get-tuple-element.176), channel_id=1, source_target_pairs={{0,8},{8,0},{16,24},{24,16},{1,9},{9,1},{17,25},{25,17},{2,10},{10... | collective-permute-start | bytes 368648 | tf_op jit(solution)/shard_map/ppermute | solution.py:1105
  176.4 14.2 %collective-permute-start.43 = (bf16[96,640]{1,0:T(8,128)(2,1)S(1)}, bf16[96,640]{1,0:T(8,128)(2,1)S(1)}, u32[]{:S(2)}, u32[]{:S(2)}) collective-permute-start(bf16[96,640]{1,0:T(8,128)(2,1)S(1)} %get-tuple-element.177), channel_id=1, source_target_pairs={{0,16},{8,24},{16,0},{24,8},{1,17},{9,25},{17,1},{25,9},{2,18},{10... | collective-permute-start | bytes 368648 | tf_op jit(solution)/shard_map/ppermute | solution.py:1105
  176.5 10.9 %collective-permute-start.40 = (bf16[2,128,768]{2,1,0:T(8,128)(2,1)S(1)}, bf16[2,128,768]{2,1,0:T(8,128)(2,1)S(1)}, u32[]{:S(2)}, u32[]{:S(2)}) collective-permute-start(bf16[2,128,768]{2,1,0:T(8,128)(2,1)S(1)} %get-tuple-element.183), channel_id=1, source_target_pairs={{0,4},{1,5},{2,6},{3,7},{4,0},{5,1},{6,2},{7,3},{8,12},{9,13},{10,... | collective-permute-start | bytes 1179656 | tf_op jit(solution)/shard_map/ppermute | solution.py:172
  177.3 11.5 %collective-permute-start.39 = (bf16[2,128,768]{2,1,0:T(8,128)(2,1)S(1)}, bf16[2,128,768]{2,1,0:T(8,128)(2,1)S(1)}, u32[]{:S(2)}, u32[]{:S(2)}) collective-permute-start(bf16[2,128,768]{2,1,0:T(8,128)(2,1)S(1)} %get-tuple-element.181), channel_id=1, source_target_pairs={{0,2},{1,3},{2,0},{3,1},{4,6},{5,7},{6,4},{7,5},{8,10},{9,11},{10,... | collective-permute-start | bytes 1179656 | tf_op jit(solution)/shard_map/ppermute | solution.py:172
  184.4 6.7 %collective-permute-start.44 = (bf16[96,640]{1,0:T(8,128)(2,1)S(1)}, bf16[96,640]{1,0:T(8,128)(2,1)S(1)}, u32[]{:S(2)}, u32[]{:S(2)}) collective-permute-start(bf16[96,640]{1,0:T(8,128)(2,1)S(1)} %get-tuple-element.178), channel_id=1, source_target_pairs={{0,24},{8,16},{16,8},{24,0},{1,25},{9,17},{17,9},{25,1},{2,26},{10... | collective-permute-start | bytes 368648 | tf_op jit(solution)/shard_map/ppermute | solution.py:1105
  (50 other events, 376.8 us)

commit v3 on v2

--- a/solution.py
+++ b/solution.py
@@ -1298,10 +1298,10 @@
     qkv_low = tie(qkv_low, both[0], *rest_pieces[1:3])
     for step in reversed(range(plan.bits)):
         if step == 0:
-            qkv_low = tie(qkv_low, *rest_pieces[3:])
+            both = [tie(piece, qkv_high) for piece in both]
         qkv_low, qkv_high = reduce_step(plan, step, qkv_low, qkv_high)
-    both = exchange_rows(plan, [tie(piece, qkv_low) for piece in both])
     qkv_cut = cut_qkv(plan, meta, tie(qkv_low, *rest_pieces[1:]), qkv_joined)
+    both = exchange_rows(plan, both[:3] + [tie(piece, *qkv_cut) for piece in both[3:]])
     qkv_pieces = reduce_z(plan, qkv_cut)
     rest_pieces[0] = tie(rest_pieces[0], *qkv_cut)
     out_grad, in_grad, down_grad, mlp_gain_grad = end_rest(plan, rest_pieces)

time: 192 us -> 187 us (0.974)
  waiting for transfers between devices: 42.4 us -> 36.5 us
    ppermute x6, waiting for transfers between devices: 10.1 us -> 4.41 us  [reduce_z(): lax.ppermute(pieces[j], 'row', plan.z_pairs(j))]
    ppermute x6, waiting for transfers between devices: 11.2 us -> 7.94 us  [exchange_rows(): lax.ppermute(pieces[j], 'blk', plan.xor_pairs(2 * j))]
    ppermute x6, starting transfers between devices: 8.72 us -> 11.9 us  [reduce_z(): lax.ppermute(pieces[j], 'row', plan.z_pairs(j))]
    ppermute x4, waiting for transfers between devices: 5.45 us -> 8.4 us  [reduce_step(): moved = lax.ppermute(high, 'blk', plan.step_pairs(step))]
    ppermute x6, starting transfers between devices: 10.3 us -> 7.53 us  [exchange_rows(): lax.ppermute(pieces[j], 'blk', plan.xor_pairs(2 * j))]
  transfers between devices with their start and end apart: 45 -> 45, of which waited for: 22 -> 17; matrix products, arithmetic and copies ran while one was open for 4% -> 4% of each run, Pallas kernels for 33% -> 34%
where the time goes in v3:
time: 187 us; the launch traced here: 186 us
  Pallas kernels  83.8 us (45%)
  starting transfers between devices  48.1 us (26%)
  waiting for transfers between devices  36.5 us (20%)
  local copies, waits for them, and re-layouts  9.79 us (5%)
  other arithmetic  4.64 us (2%)
  between operations  3.38 us (2%)
    pallas_call x3, Pallas kernels, attend_back(): pl.pallas_call(functools.partial(attend_back_kernel, plan, width), grid=(...  23.4 us
    pallas_call x1, Pallas kernels, middle(): pl.pallas_call(functools.partial(middle_kernel, plan), in_specs=[SMEM, VM...  19.4 us
    ppermute x6, starting transfers between devices, gather_z(): pieces.append(lax.ppermute(source, 'row', plan.z_pairs(j)))  15.4 us
    pallas_call x2, Pallas kernels, attend(): pl.pallas_call(functools.partial(attend_kernel, plan, width), grid=(HALF_...  12.9 us
    ppermute x6, starting transfers between devices, reduce_z(): lax.ppermute(pieces[j], 'row', plan.z_pairs(j))  11.9 us
    ppermute x6, waiting for transfers between devices, gather_z(): pieces.append(lax.ppermute(source, 'row', plan.z_pairs(j)))  8.91 us
    ppermute x4, waiting for transfers between devices, reduce_step(): moved = lax.ppermute(high, 'blk', plan.step_pairs(step))  8.4 us
    ppermute x6, waiting for transfers between devices, exchange_rows(): lax.ppermute(pieces[j], 'blk', plan.xor_pairs(2 * j))  7.94 us
  transfers between devices with their start and end apart: 45, of which 17 were waited for; matrix products, arithmetic and copies ran while one was open for 4% of the time, Pallas kernels for 34%

profile of v3, /device:TPU:0, one launch (start us, length us, event | category | flops | bytes accessed | tf_op | source)
XLA Modules:
  0.0 186.2 jit_solution(2714222576226532853)
XLA Ops:
  0.7 4.1 %collective-permute-start.1 = (bf16[96,576]{1,0:T(8,128)(2,1)}, bf16[96,576]{1,0:T(8,128)(2,1)S(1)}, u32[]{:S(2)}, u32[]{:S(2)}) collective-permute-start(bf16[96,576]{1,0:T(8,128)(2,1)} %refs_0_.1), channel_id=1, source_target_pairs={{0,16},{8,24},{16,0},{24,8},{1,17},{9,25},{17,1},{25,9},{2,18},{10... | collective-permute-start | bytes 331784 | tf_op jit(solution)/shard_map/ppermute | solution.py:166
  4.8 1.3 collective-permute-start.2
  6.4 1.2 fusion.3.meta.order
  7.6 2.7 %prepare.1 = (bf16[2,128,768]{2,1,0:T(8,128)(2,1)}, bf16[2,128,768]{2,1,0:T(8,128)(2,1)}, bf16[2,128,768]{2,1,0:T(8,128)(2,1)}, bf16[2,128,768]{2,1,0:T(8,128)(2,1)}, bf16[288,384]{1,0:T(8,128)(2,1)}) custom-call(s32[25]{0:T(128)} %fusion.3.meta.order, bf16[4,128,768]{2,1,0:T(8,128)(2,1)} %tokens.1, bf16[4,128,768]{2,1,0:T(8,128)(2,1)} %cotangent.1, ...), custom_call_target="tpu_custom_call" | custom-call | flops 4000000 | bytes 1024 | tf_op jit(solution)/shard_map/prepare/pallas_call | solution.py:262
  10.2 2.4 %collective-permute-start.10 = (bf16[2,128,768]{2,1,0:T(8,128)(2,1)}, bf16[2,128,768]{2,1,0:T(8,128)(2,1)S(1)}, u32[]{:S(2)}, u32[]{:S(2)}) collective-permute-start(bf16[2,128,768]{2,1,0:T(8,128)(2,1)} %get-tuple-element.110), channel_id=1, source_target_pairs={{0,6},{1,7},{2,4},{3,5},{4,2},{5,3},{6,0},{7,1},{8,14},{9,15},{10,... | collective-permute-start | bytes 1179656 | tf_op jit(solution)/shard_map/ppermute | solution.py:172
  18.5 1.6 collective-permute-start.4
  20.1 2.8 %collective-permute-start.5 = (bf16[288,384]{1,0:T(8,128)(2,1)}, bf16[288,384]{1,0:T(8,128)(2,1)S(1)}, u32[]{:S(2)}, u32[]{:S(2)}) collective-permute-start(bf16[288,384]{1,0:T(8,128)(2,1)} %get-tuple-element.113.refs_0_), channel_id=1, source_target_pairs={{0,16},{8,24},{16,0},{24,8},{1,17},{9,25},{17,1},{25,9},{2,18},{10... | collective-permute-start | bytes 663560 | tf_op jit(solution)/shard_map/ppermute | solution.py:166
  23.4 2.9 %collective-permute-start.6 = (bf16[288,384]{1,0:T(8,128)(2,1)}, bf16[288,384]{1,0:T(8,128)(2,1)S(1)}, u32[]{:S(2)}, u32[]{:S(2)}) collective-permute-start(bf16[288,384]{1,0:T(8,128)(2,1)} %get-tuple-element.113.refs_0_), channel_id=1, source_target_pairs={{0,24},{8,16},{16,8},{24,0},{1,25},{9,17},{17,9},{25,1},{2,26},{10... | collective-permute-start | bytes 663560 | tf_op jit(solution)/shard_map/ppermute | solution.py:166
  26.3 1.0 fusion.2
  27.3 2.8 %collective-permute-done.8.refs_1_.refs_3_ = bf16[2,128,768]{2,1,0:T(8,128)(2,1)S(1)} collective-permute-done((bf16[2,128,768]{2,1,0:T(8,128)(2,1)}, bf16[2,128,768]{2,1,0:T(8,128)(2,1)S(1)}, u32[]{:S(2)}, u32[]{:S(2)}) %collective-permute-start.8) | collective-permute-done | bytes 393248 | tf_op jit(solution)/shard_map/ppermute | solution.py:172
  30.6 1.1 collective-permute-start.11
  32.2 1.1 masks.1
  33.2 4.1 %collective-permute-done.5.refs_2_ = bf16[288,384]{1,0:T(8,128)(2,1)S(1)} collective-permute-done((bf16[288,384]{1,0:T(8,128)(2,1)}, bf16[288,384]{1,0:T(8,128)(2,1)S(1)}, u32[]{:S(2)}, u32[]{:S(2)}) %collective-permute-start.5) | collective-permute-done | bytes 221216 | tf_op jit(solution)/shard_map/ppermute | solution.py:166
  38.1 4.0 %collective-permute-start.13 = (bf16[288,384]{1,0:T(8,128)(2,1)S(1)}, bf16[288,384]{1,0:T(8,128)(2,1)S(1)}, u32[]{:S(2)}, u32[]{:S(2)}) collective-permute-start(bf16[288,384]{1,0:T(8,128)(2,1)S(1)} %copy-done.27), channel_id=1, source_target_pairs={{0,8},{8,0},{16,24},{24,16},{1,9},{9,1},{17,25},{25,17},{2,10},{10... | collective-permute-start | bytes 663560 | tf_op jit(solution)/shard_map/ppermute | solution.py:166
  42.6 4.8 %collective-permute-done.13.refs_1_ = bf16[288,384]{1,0:T(8,128)(2,1)S(1)} collective-permute-done((bf16[288,384]{1,0:T(8,128)(2,1)S(1)}, bf16[288,384]{1,0:T(8,128)(2,1)S(1)}, u32[]{:S(2)}, u32[]{:S(2)}) %collective-permute-start.13) | collective-permute-done | bytes 221216 | tf_op jit(solution)/shard_map/ppermute | solution.py:166
  49.3 5.9 %project.1 = (bf16[512,768]{1,0:T(8,128)(2,1)S(1)}, bf16[2,512,384]{2,1,0:T(8,128)(2,1)S(1)}, bf16[2,512,384]{2,1,0:T(8,128)(2,1)S(1)}, bf16[512,768]{1,0:T(8,128)(2,1)S(1)}, f32[8,768]{1,0:T(8,128)S(1)}) custom-call(s32[25]{0:T(128)S(1)} %copy-done.32, f32[512,128]{1,0:T(8,128)S(1)} %get-tuple-element.203.cos_ref.refs_0_, ...), custom_call_target="tpu_custom_call" | custom-call | flops 7000000 | bytes 1024 | tf_op jit(solution)/shard_map/project/pallas_call | solution.py:500
  56.0 1.3 collective-permute-start.18
  58.1 6.4 %attend.2 = (f32[512,384]{1,0:T(8,128)S(1)}, bf16[512,384]{1,0:T(8,128)(2,1)S(1)}, f32[3,2,512]{2,1,0:T(2,128)S(1)}) custom-call(s32[25]{0:T(128)S(1)} %copy-done.32, bf16[1024,128]{1,0:T(8,128)(2,1)S(1)} %get-tuple-element.105.kmask, bf16[512,128]{1,0:T(8,128)(2,1)S(1)} %get-tuple-element.106.qmask, bf16[512,768]{1,0:T(8,128)(2,1)S(1)} %get-tuple-element.118.q_ref, ...), custom_call_target="tpu_custom_call" | custom-call | flops 9000000 | bytes 1024 | tf_op jit(solution)/shard_map/attend/pallas_call | solution.py:605
  65.9 1.0 collective-permute-start.20
  67.5 1.4 collective-permute-done.18.refs_8_
  69.3 6.4 %attend.3 = (f32[512,384]{1,0:T(8,128)S(1)}, bf16[512,384]{1,0:T(8,128)(2,1)S(1)}, f32[3,2,512]{2,1,0:T(2,128)S(1)}) custom-call(s32[25]{0:T(128)S(1)} %copy-done.32, bf16[1024,128]{1,0:T(8,128)(2,1)S(1)} %get-tuple-element.105.kmask, bf16[512,128]{1,0:T(8,128)(2,1)S(1)} %get-tuple-element.106.qmask, bf16[512,768]{1,0:T(8,128)(2,1)S(1)} %get-tuple-element.118.q_ref, ...), custom_call_target="tpu_custom_call" | custom-call | flops 9000000 | bytes 1024 | tf_op jit(solution)/shard_map/attend/pallas_call | solution.py:605
  78.2 2.3 %collective-permute-done.24.refs_13_ = bf16[528,768]{1,0:T(8,128)(2,1)S(1)} collective-permute-done((bf16[528,768]{1,0:T(8,128)(2,1)S(1)}, bf16[528,768]{1,0:T(8,128)(2,1)S(1)}, u32[]{:S(2)}, u32[]{:S(2)}) %collective-permute-start.24) | collective-permute-done | bytes 811040 | tf_op jit(solution)/shard_map/ppermute | solution.py:159
  81.4 19.4 %middle.1 = (bf16[128,768]{1,0:T(8,128)(2,1)}, bf16[128,768]{1,0:T(8,128)(2,1)}, bf16[128,768]{1,0:T(8,128)(2,1)}, bf16[128,768]{1,0:T(8,128)(2,1)}, bf16[512,76...) custom-call(s32[25]{0:T(128)} %fusion.3.meta.order, ...), custom_call_target="tpu_custom_call" | custom-call | flops 20000000 | bytes 1024 | tf_op jit(solution)/shard_map/middle/pallas_call | solution.py:839
  101.4 1.1 copy-done.2
  102.5 4.0 %attend_back.3 = (bf16[512,128]{1,0:T(8,128)(2,1)S(1)}, bf16[2,512,128]{2,1,0:T(8,128)(2,1)S(1)}, bf16[2,512,128]{2,1,0:T(8,128)(2,1)S(1)}) custom-call(s32[25]{0:T(128)S(1)} %copy-done.33, bf16[1024,128]{1,0:T(8,128)(2,1)S(1)} %get-tuple-element.105.kmask, bf16[512,128]{1,0:T(8,128)(2,1)S(1)} %get-tuple-element.106.qmask, ...), custom_call_target="tpu_custom_call" | custom-call | flops 4000000 | bytes 1024 | tf_op jit(solution)/shard_map/attend_back/pallas_call | solution.py:686
  106.9 1.1 collective-permute-start.28
  109.2 7.8 %attend_back.4 = (bf16[512,256]{1,0:T(8,128)(2,1)S(1)}, bf16[2,512,256]{2,1,0:T(8,128)(2,1)S(1)}, bf16[2,512,256]{2,1,0:T(8,128)(2,1)S(1)}) custom-call(s32[25]{0:T(128)S(1)} %copy-done.33, bf16[1024,128]{1,0:T(8,128)(2,1)S(1)} %get-tuple-element.105.kmask, bf16[512,128]{1,0:T(8,128)(2,1)S(1)} %get-tuple-element.106.qmask, ...), custom_call_target="tpu_custom_call" | custom-call | flops 8000000 | bytes 1024 | tf_op jit(solution)/shard_map/attend_back/pallas_call | solution.py:686
  117.1 11.6 %attend_back.5 = (bf16[512,384]{1,0:T(8,128)(2,1)S(1)}, bf16[2,512,384]{2,1,0:T(8,128)(2,1)S(1)}, bf16[2,512,384]{2,1,0:T(8,128)(2,1)S(1)}) custom-call(s32[25]{0:T(128)S(1)} %copy-done.33, bf16[1024,128]{1,0:T(8,128)(2,1)S(1)} %get-tuple-element.105.kmask, bf16[512,128]{1,0:T(8,128)(2,1)S(1)} %get-tuple-element.106.qmask, ...), custom_call_target="tpu_custom_call" | custom-call | flops 12000000 | bytes 1024 | tf_op jit(solution)/shard_map/attend_back/pallas_call | solution.py:686
  129.6 1.0 collective-permute-start.31
  130.7 1.1 collective-permute-done.29.refs_9_
  131.8 6.1 %back_weight.1 = (bf16[3,512,768]{2,1,0:T(8,128)(2,1)S(1)}, bf16[2,96,2304]{2,1,0:T(8,128)(2,1)S(1)}, bf16[2,96,2304]{2,1,0:T(8,128)(2,1)S(1)}, bf16[2,96,2304]{2,1,0:T(8,128)(2,1)S(1)}, bf16[2,96,2304]{2,1,0:T(8,128)(2,1)S(1)}) custom-call(s32[25]{0:T(128)S(1)} %copy-done.33, f32[512,128]{1,0:T(8,128)S(1)} %get-tuple-element.203.cos_ref.refs_0_, ...), custom_call_target="tpu_custom_call" | custom-call | flops 6000000 | bytes 1024 | tf_op jit(solution)/shard_map/back_weight/pallas_call | solution.py:927
  138.4 3.5 %collective-permute-done.31 = bf16[1,528,768]{2,1,0:T(8,128)(2,1)S(1)} collective-permute-done((bf16[1,528,768]{2,1,0:T(8,128)(2,1)S(1)}, bf16[1,528,768]{2,1,0:T(8,128)(2,1)S(1)}, u32[]{:S(2)}, u32[]{:S(2)}) %collective-permute-start.31) | collective-permute-done | bytes 811040 | tf_op jit(solution)/shard_map/ppermute | solution.py:202
  142.4 1.0 collective-permute-start.36
  144.5 3.4 %collective-permute-start.34 = (bf16[288,384]{1,0:T(8,128)(2,1)S(1)}, bf16[288,384]{1,0:T(8,128)(2,1)S(1)}, u32[]{:S(2)}, u32[]{:S(2)}) collective-permute-start(bf16[288,384]{1,0:T(8,128)(2,1)S(1)} %get-tuple-element.161), channel_id=1, source_target_pairs={{0,8},{8,0},{16,24},{24,16},{1,9},{9,1},{17,25},{25,17},{2,10},{10... | collective-permute-start | bytes 663560 | tf_op jit(solution)/shard_map/ppermute | solution.py:1105
  147.9 1.2 collective-permute-start.35
  149.5 5.6 %back_in.1 = (bf16[2,128,768]{2,1,0:T(8,128)(2,1)S(1)}, bf16[2,128,768]{2,1,0:T(8,128)(2,1)S(1)}, bf16[2,128,768]{2,1,0:T(8,128)(2,1)S(1)}, bf16[2,128,768]{2,1,0:T(8,128)(2,1)S(1)}) custom-call(s32[25]{0:T(128)S(1)} %copy-done.33, bf16[3,512,768]{2,1,0:T(8,128)(2,1)S(1)} %get-tuple-element.153.dp_ref, f32[512,768]{1,0:T(8,128)S(1)} %copy-done.20, ...), custom_call_target="tpu_custom_call" | custom-call | flops 7000000 | bytes 1024 | tf_op jit(solution)/shard_map/back_in/pallas_call | solution.py:976
  155.1 1.9 %collective-permute-done.34.refs_1_ = bf16[288,384]{1,0:T(8,128)(2,1)S(1)} collective-permute-done((bf16[288,384]{1,0:T(8,128)(2,1)S(1)}, bf16[288,384]{1,0:T(8,128)(2,1)S(1)}, u32[]{:S(2)}, u32[]{:S(2)}) %collective-permute-start.34) | collective-permute-done | bytes 221216 | tf_op jit(solution)/shard_map/ppermute | solution.py:1105
  157.0 2.5 %collective-permute-done.35.refs_2_ = bf16[288,384]{1,0:T(8,128)(2,1)S(1)} collective-permute-done((bf16[288,384]{1,0:T(8,128)(2,1)S(1)}, bf16[288,384]{1,0:T(8,128)(2,1)S(1)}, u32[]{:S(2)}, u32[]{:S(2)}) %collective-permute-start.35) | collective-permute-done | bytes 221216 | tf_op jit(solution)/shard_map/ppermute | solution.py:1105
  159.6 1.1 collective-permute-start.37
  160.7 2.6 %collective-permute-start.38 = (bf16[288,384]{1,0:T(8,128)(2,1)S(1)}, bf16[288,384]{1,0:T(8,128)(2,1)S(1)}, u32[]{:S(2)}, u32[]{:S(2)}) collective-permute-start(bf16[288,384]{1,0:T(8,128)(2,1)S(1)} %get-tuple-element.163), channel_id=1, source_target_pairs={{0,24},{8,16},{16,8},{24,0},{1,25},{9,17},{17,9},{25,1},{2,26},{10... | collective-permute-start | bytes 663560 | tf_op jit(solution)/shard_map/ppermute | solution.py:1105
  163.3 1.1 collective-permute-start.40
  164.4 1.1 collective-permute-start.39
  165.5 4.9 %collective-permute-done.37 = bf16[1,96,2304]{2,1,0:T(8,128)(2,1)S(1)} collective-permute-done((bf16[1,96,2304]{2,1,0:T(8,128)(2,1)S(1)}, bf16[1,96,2304]{2,1,0:T(8,128)(2,1)S(1)}, u32[]{:S(2)}, u32[]{:S(2)}) %collective-permute-start.37) | collective-permute-done | bytes 442400 | tf_op jit(solution)/shard_map/ppermute | solution.py:202
  171.5 1.2 collective-permute-start.42
  173.4 1.9 %collective-permute-start.41 = (bf16[2,128,768]{2,1,0:T(8,128)(2,1)S(1)}, bf16[2,128,768]{2,1,0:T(8,128)(2,1)S(1)}, u32[]{:S(2)}, u32[]{:S(2)}) collective-permute-start(bf16[2,128,768]{2,1,0:T(8,128)(2,1)S(1)} %get-tuple-element.185), channel_id=1, source_target_pairs={{0,6},{1,7},{2,4},{3,5},{4,2},{5,3},{6,0},{7,1},{8,14},{9,15},{10,... | collective-permute-start | bytes 1179656 | tf_op jit(solution)/shard_map/ppermute | solution.py:172
  176.2 2.7 %collective-permute-start.44 = (bf16[96,640]{1,0:T(8,128)(2,1)S(1)}, bf16[96,640]{1,0:T(8,128)(2,1)S(1)}, u32[]{:S(2)}, u32[]{:S(2)}) collective-permute-start(bf16[96,640]{1,0:T(8,128)(2,1)S(1)} %get-tuple-element.177), channel_id=1, source_target_pairs={{0,24},{8,16},{16,8},{24,0},{1,25},{9,17},{17,9},{25,1},{2,26},{10... | collective-permute-start | bytes 368648 | tf_op jit(solution)/shard_map/ppermute | solution.py:1105
  179.5 4.1 %collective-permute-done.41.refs_3_ = bf16[2,128,768]{2,1,0:T(8,128)(2,1)S(1)} collective-permute-done((bf16[2,128,768]{2,1,0:T(8,128)(2,1)S(1)}, bf16[2,128,768]{2,1,0:T(8,128)(2,1)S(1)}, u32[]{:S(2)}, u32[]{:S(2)}) %collective-permute-start.41) | collective-permute-done | bytes 393248 | tf_op jit(solution)/shard_map/ppermute | solution.py:172
  183.7 1.8 place_rows.1
  (194 shorter events, 25.3 us)
Async XLA Ops:
  0.7 16.4 %collective-permute-start.1 = (bf16[96,576]{1,0:T(8,128)(2,1)}, bf16[96,576]{1,0:T(8,128)(2,1)S(1)}, u32[]{:S(2)}, u32[]{:S(2)}) collective-permute-start(bf16[96,576]{1,0:T(8,128)(2,1)} %refs_0_.1), channel_id=1, source_target_pairs={{0,16},{8,24},{16,0},{24,8},{1,17},{9,25},{17,1},{25,9},{2,18},{10... | collective-permute-start | bytes 331784 | tf_op jit(solution)/shard_map/ppermute | solution.py:166
  4.8 12.9 %collective-permute-start.2 = (bf16[96,576]{1,0:T(8,128)(2,1)}, bf16[96,576]{1,0:T(8,128)(2,1)S(1)}, u32[]{:S(2)}, u32[]{:S(2)}) collective-permute-start(bf16[96,576]{1,0:T(8,128)(2,1)} %refs_0_.1), channel_id=1, source_target_pairs={{0,24},{8,16},{16,8},{24,0},{1,25},{9,17},{17,9},{25,1},{2,26},{10... | collective-permute-start | bytes 331784 | tf_op jit(solution)/shard_map/ppermute | solution.py:166
  6.1 11.6 %collective-permute-start = (bf16[96,576]{1,0:T(8,128)(2,1)}, bf16[96,576]{1,0:T(8,128)(2,1)S(1)}, u32[]{:S(2)}, u32[]{:S(2)}) collective-permute-start(bf16[96,576]{1,0:T(8,128)(2,1)} %refs_0_.1), channel_id=1, source_target_pairs={{0,8},{8,0},{16,24},{24,16},{1,9},{9,1},{17,25},{25,17},{2,10},{10... | collective-permute-start | bytes 331784 | tf_op jit(solution)/shard_map/ppermute | solution.py:166
  10.2 27.8 %copy-start.27 = (bf16[288,384]{1,0:T(8,128)(2,1)S(1)}, bf16[288,384]{1,0:T(8,128)(2,1)}, u32[]{:S(2)}) copy-start(bf16[288,384]{1,0:T(8,128)(2,1)} %get-tuple-element.113.refs_0_) | copy-start | bytes 663556
  10.2 13.2 %collective-permute-start.10 = (bf16[2,128,768]{2,1,0:T(8,128)(2,1)}, bf16[2,128,768]{2,1,0:T(8,128)(2,1)S(1)}, u32[]{:S(2)}, u32[]{:S(2)}) collective-permute-start(bf16[2,128,768]{2,1,0:T(8,128)(2,1)} %get-tuple-element.110), channel_id=1, source_target_pairs={{0,6},{1,7},{2,4},{3,5},{4,2},{5,3},{6,0},{7,1},{8,14},{9,15},{10,... | collective-permute-start | bytes 1179656 | tf_op jit(solution)/shard_map/ppermute | solution.py:172
  12.7 17.5 %collective-permute-start.8 = (bf16[2,128,768]{2,1,0:T(8,128)(2,1)}, bf16[2,128,768]{2,1,0:T(8,128)(2,1)S(1)}, u32[]{:S(2)}, u32[]{:S(2)}) collective-permute-start(bf16[2,128,768]{2,1,0:T(8,128)(2,1)} %get-tuple-element.108), channel_id=1, source_target_pairs={{0,2},{1,3},{2,0},{3,1},{4,6},{5,7},{6,4},{7,5},{8,10},{9,11},{10,... | collective-permute-start | bytes 1179656 | tf_op jit(solution)/shard_map/ppermute | solution.py:172
  17.1 13.6 %collective-permute-start.9 = (bf16[2,128,768]{2,1,0:T(8,128)(2,1)}, bf16[2,128,768]{2,1,0:T(8,128)(2,1)S(1)}, u32[]{:S(2)}, u32[]{:S(2)}) collective-permute-start(bf16[2,128,768]{2,1,0:T(8,128)(2,1)} %get-tuple-element.109), channel_id=1, source_target_pairs={{0,4},{1,5},{2,6},{3,7},{4,0},{5,1},{6,2},{7,3},{8,12},{9,13},{10,... | collective-permute-start | bytes 1179656 | tf_op jit(solution)/shard_map/ppermute | solution.py:172
  18.5 19.6 %collective-permute-start.4 = (bf16[96,2432]{1,0:T(8,128)(2,1)S(1)}, bf16[96,2432]{1,0:T(8,128)(2,1)S(1)}, u32[]{:S(2)}, u32[]{:S(2)}) collective-permute-start(bf16[96,2432]{1,0:T(8,128)(2,1)S(1)} %join_qkv.1.refs_4_.refs_8_.weight), channel_id=1, source_target_pairs={{0,2},{1,5},{2,0},{3,7},{4,6},{5,1},{6,4},{7,3},{8,10},{9,13},{10,... | collective-permute-start | bytes 1400840 | tf_op jit(solution)/shard_map/ppermute | solution.py:178
  20.1 17.2 %collective-permute-start.5 = (bf16[288,384]{1,0:T(8,128)(2,1)}, bf16[288,384]{1,0:T(8,128)(2,1)S(1)}, u32[]{:S(2)}, u32[]{:S(2)}) collective-permute-start(bf16[288,384]{1,0:T(8,128)(2,1)} %get-tuple-element.113.refs_0_), channel_id=1, source_target_pairs={{0,16},{8,24},{16,0},{24,8},{1,17},{9,25},{17,1},{25,9},{2,18},{10... | collective-permute-start | bytes 663560 | tf_op jit(solution)/shard_map/ppermute | solution.py:166
  23.4 25.8 %copy-start.6 = (bf16[2,128,768]{2,1,0:T(8,128)(2,1)}, bf16[2,128,768]{2,1,0:T(8,128)(2,1)S(1)}, u32[]{:S(2)}) copy-start(bf16[2,128,768]{2,1,0:T(8,128)(2,1)S(1)} %collective-permute-done.10.refs_3_.refs_5_) | copy-start | bytes 1179652
  23.4 13.9 %collective-permute-start.6 = (bf16[288,384]{1,0:T(8,128)(2,1)}, bf16[288,384]{1,0:T(8,128)(2,1)S(1)}, u32[]{:S(2)}, u32[]{:S(2)}) collective-permute-start(bf16[288,384]{1,0:T(8,128)(2,1)} %get-tuple-element.113.refs_0_), channel_id=1, source_target_pairs={{0,24},{8,16},{16,8},{24,0},{1,25},{9,17},{17,9},{25,1},{2,26},{10... | collective-permute-start | bytes 663560 | tf_op jit(solution)/shard_map/ppermute | solution.py:166
  30.2 25.0 %copy-start.8 = (bf16[2,128,768]{2,1,0:T(8,128)(2,1)}, bf16[2,128,768]{2,1,0:T(8,128)(2,1)S(1)}, u32[]{:S(2)}) copy-start(bf16[2,128,768]{2,1,0:T(8,128)(2,1)S(1)} %collective-permute-done.8.refs_1_.refs_3_) | copy-start | bytes 1179652
  30.6 12.0 %collective-permute-start.11 = (bf16[96,2432]{1,0:T(8,128)(2,1)S(1)}, bf16[96,2432]{1,0:T(8,128)(2,1)S(1)}, u32[]{:S(2)}, u32[]{:S(2)}) collective-permute-start(bf16[96,2432]{1,0:T(8,128)(2,1)S(1)} %join_qkv.1.refs_4_.refs_8_.weight), channel_id=1, source_target_pairs={{0,4},{1,3},{2,6},{3,1},{4,0},{5,7},{6,2},{7,5},{8,12},{9,11},{10,... | collective-permute-start | bytes 1400840 | tf_op jit(solution)/shard_map/ppermute | solution.py:179
  38.0 9.4 %collective-permute-start.14 = (bf16[96,2432]{1,0:T(8,128)(2,1)S(1)}, bf16[96,2432]{1,0:T(8,128)(2,1)S(1)}, u32[]{:S(2)}, u32[]{:S(2)}) collective-permute-start(bf16[96,2432]{1,0:T(8,128)(2,1)S(1)} %collective-permute-done.4.refs_5_.refs_9_), channel_id=1, source_target_pairs={{0,4},{1,3},{2,6},{3,1},{4,0},{5,7},{6,2},{7,5},{8,12},{9,11},{10,... | collective-permute-start | bytes 1400840 | tf_op jit(solution)/shard_map/ppermute | solution.py:187
  38.1 9.3 %collective-permute-start.13 = (bf16[288,384]{1,0:T(8,128)(2,1)S(1)}, bf16[288,384]{1,0:T(8,128)(2,1)S(1)}, u32[]{:S(2)}, u32[]{:S(2)}) collective-permute-start(bf16[288,384]{1,0:T(8,128)(2,1)S(1)} %copy-done.27), channel_id=1, source_target_pairs={{0,8},{8,0},{16,24},{24,16},{1,9},{9,1},{17,25},{25,17},{2,10},{10... | collective-permute-start | bytes 663560 | tf_op jit(solution)/shard_map/ppermute | solution.py:166
  42.1 5.4 %collective-permute-start.3 = (bf16[96,2432]{1,0:T(8,128)(2,1)S(1)}, bf16[96,2432]{1,0:T(8,128)(2,1)S(1)}, u32[]{:S(2)}, u32[]{:S(2)}) collective-permute-start(bf16[96,2432]{1,0:T(8,128)(2,1)S(1)} %join_qkv.1.refs_4_.refs_8_.weight), channel_id=1, source_target_pairs={{0,1},{1,0},{2,3},{3,2},{4,5},{5,4},{6,7},{7,6},{8,9},{9,8},{10,11... | collective-permute-start | bytes 1400840 | tf_op jit(solution)/shard_map/ppermute | solution.py:159
  42.1 5.4 %collective-permute-start.7 = (bf16[96,2432]{1,0:T(8,128)(2,1)S(1)}, bf16[96,2432]{1,0:T(8,128)(2,1)S(1)}, u32[]{:S(2)}, u32[]{:S(2)}) collective-permute-start(bf16[96,2432]{1,0:T(8,128)(2,1)S(1)} %collective-permute-done.4.refs_5_.refs_9_), channel_id=1, source_target_pairs={{0,1},{1,0},{2,3},{3,2},{4,5},{5,4},{6,7},{7,6},{8,9},{9,8},{10,11... | collective-permute-start | bytes 1400840 | tf_op jit(solution)/shard_map/ppermute | solution.py:159
  42.6 4.9 %collective-permute-start.12 = (bf16[96,2432]{1,0:T(8,128)(2,1)S(1)}, bf16[96,2432]{1,0:T(8,128)(2,1)S(1)}, u32[]{:S(2)}, u32[]{:S(2)}) collective-permute-start(bf16[96,2432]{1,0:T(8,128)(2,1)S(1)} %collective-permute-done.11.refs_6_.refs_10_), channel_id=1, source_target_pairs={{0,1},{1,0},{2,3},{3,2},{4,5},{5,4},{6,7},{7,6},{8,9},{9,8},{10,11... | collective-permute-start | bytes 1400840 | tf_op jit(solution)/shard_map/ppermute | solution.py:159
  47.4 1.8 collective-permute-start.15
  48.4 17.5 %collective-permute-start.17 = (bf16[528,768]{1,0:T(8,128)(2,1)S(1)}, bf16[528,768]{1,0:T(8,128)(2,1)S(1)}, u32[]{:S(2)}, u32[]{:S(2)}) collective-permute-start(bf16[528,768]{1,0:T(8,128)(2,1)S(1)} %join_rest.1.refs_6_.weight), channel_id=1, source_target_pairs={{0,2},{1,5},{2,0},{3,7},{4,6},{5,1},{6,4},{7,3},{8,10},{9,13},{10,... | collective-permute-start | bytes 2433032 | tf_op jit(solution)/shard_map/ppermute | solution.py:178
  55.8 2.3 %collective-permute-start.16 = (bf16[2,512,384]{2,1,0:T(8,128)(2,1)S(1)}, bf16[2,512,384]{2,1,0:T(8,128)(2,1)S(1)}, u32[]{:S(2)}, u32[]{:S(2)}) collective-permute-start(bf16[2,512,384]{2,1,0:T(8,128)(2,1)S(1)} %get-tuple-element.119.refs_0_), channel_id=1, source_target_pairs={{0,1},{1,0},{2,3},{3,2},{4,5},{5,4},{6,7},{7,6},{8,9},{9,8},{10,11... | collective-permute-start | bytes 2359304 | tf_op jit(solution)/shard_map/ppermute | solution.py:1234
  56.0 12.9 %collective-permute-start.18 = (bf16[528,768]{1,0:T(8,128)(2,1)S(1)}, bf16[528,768]{1,0:T(8,128)(2,1)S(1)}, u32[]{:S(2)}, u32[]{:S(2)}) collective-permute-start(bf16[528,768]{1,0:T(8,128)(2,1)S(1)} %join_rest.1.refs_6_.weight), channel_id=1, source_target_pairs={{0,4},{1,3},{2,6},{3,1},{4,0},{5,7},{6,2},{7,5},{8,12},{9,11},{10,... | collective-permute-start | bytes 2433032 | tf_op jit(solution)/shard_map/ppermute | solution.py:179
  65.9 12.3 %collective-permute-start.20 = (bf16[528,768]{1,0:T(8,128)(2,1)S(1)}, bf16[528,768]{1,0:T(8,128)(2,1)S(1)}, u32[]{:S(2)}, u32[]{:S(2)}) collective-permute-start(bf16[528,768]{1,0:T(8,128)(2,1)S(1)} %collective-permute-done.17.refs_7_), channel_id=1, source_target_pairs={{0,4},{1,3},{2,6},{3,1},{4,0},{5,7},{6,2},{7,5},{8,12},{9,11},{10,... | collective-permute-start | bytes 2433032 | tf_op jit(solution)/shard_map/ppermute | solution.py:187
  67.0 2.3 %collective-permute-start.19 = (bf16[2,512,384]{2,1,0:T(8,128)(2,1)S(1)}, bf16[2,512,384]{2,1,0:T(8,128)(2,1)S(1)}, u32[]{:S(2)}, u32[]{:S(2)}) collective-permute-start(bf16[2,512,384]{2,1,0:T(8,128)(2,1)S(1)} %get-tuple-element.122.refs_0_), channel_id=1, source_target_pairs={{0,1},{1,0},{2,3},{3,2},{4,5},{5,4},{6,7},{7,6},{8,9},{9,8},{10,11... | collective-permute-start | bytes 2359304 | tf_op jit(solution)/shard_map/ppermute | solution.py:1234
  67.0 11.2 %collective-permute-start.21 = (bf16[528,768]{1,0:T(8,128)(2,1)S(1)}, bf16[528,768]{1,0:T(8,128)(2,1)S(1)}, u32[]{:S(2)}, u32[]{:S(2)}) collective-permute-start(bf16[528,768]{1,0:T(8,128)(2,1)S(1)} %join_rest.1.refs_6_.weight), channel_id=1, source_target_pairs={{0,1},{1,0},{2,3},{3,2},{4,5},{5,4},{6,7},{7,6},{8,9},{9,8},{10,11... | collective-permute-start | bytes 2433032 | tf_op jit(solution)/shard_map/ppermute | solution.py:159
  67.5 10.7 %collective-permute-start.22 = (bf16[528,768]{1,0:T(8,128)(2,1)S(1)}, bf16[528,768]{1,0:T(8,128)(2,1)S(1)}, u32[]{:S(2)}, u32[]{:S(2)}) collective-permute-start(bf16[528,768]{1,0:T(8,128)(2,1)S(1)} %collective-permute-done.17.refs_7_), channel_id=1, source_target_pairs={{0,1},{1,0},{2,3},{3,2},{4,5},{5,4},{6,7},{7,6},{8,9},{9,8},{10,11... | collective-permute-start | bytes 2433032 | tf_op jit(solution)/shard_map/ppermute | solution.py:159
  68.9 9.3 %collective-permute-start.23 = (bf16[528,768]{1,0:T(8,128)(2,1)S(1)}, bf16[528,768]{1,0:T(8,128)(2,1)S(1)}, u32[]{:S(2)}, u32[]{:S(2)}) collective-permute-start(bf16[528,768]{1,0:T(8,128)(2,1)S(1)} %collective-permute-done.18.refs_8_), channel_id=1, source_target_pairs={{0,1},{1,0},{2,3},{3,2},{4,5},{5,4},{6,7},{7,6},{8,9},{9,8},{10,11... | collective-permute-start | bytes 2433032 | tf_op jit(solution)/shard_map/ppermute | solution.py:159
  78.2 2.3 %collective-permute-start.24 = (bf16[528,768]{1,0:T(8,128)(2,1)S(1)}, bf16[528,768]{1,0:T(8,128)(2,1)S(1)}, u32[]{:S(2)}, u32[]{:S(2)}) collective-permute-start(bf16[528,768]{1,0:T(8,128)(2,1)S(1)} %collective-permute-done.20.refs_9_), channel_id=1, source_target_pairs={{0,1},{1,0},{2,3},{3,2},{4,5},{5,4},{6,7},{7,6},{8,9},{9,8},{10,11... | collective-permute-start | bytes 2433032 | tf_op jit(solution)/shard_map/ppermute | solution.py:159
  100.8 5.7 %collective-permute-start.26 = (bf16[2,528,768]{2,1,0:T(8,128)(2,1)}, bf16[2,528,768]{2,1,0:T(8,128)(2,1)S(1)}, u32[]{:S(2)}, u32[]{:S(2)}) collective-permute-start(bf16[2,528,768]{2,1,0:T(8,128)(2,1)} %get-tuple-element.136), channel_id=1, source_target_pairs={{0,1},{1,0},{2,3},{3,2},{4,5},{5,4},{6,7},{7,6},{8,9},{9,8},{10,11... | collective-permute-start | bytes 4866056 | tf_op jit(solution)/shard_map/ppermute | solution.py:159
  101.0 7.1 %collective-permute-start.25 = (bf16[2,528,768]{2,1,0:T(8,128)(2,1)}, bf16[2,528,768]{2,1,0:T(8,128)(2,1)S(1)}, u32[]{:S(2)}, u32[]{:S(2)}) collective-permute-start(bf16[2,528,768]{2,1,0:T(8,128)(2,1)} %get-tuple-element.133), channel_id=1, source_target_pairs={{0,1},{1,0},{2,3},{3,2},{4,5},{5,4},{6,7},{7,6},{8,9},{9,8},{10,11... | collective-permute-start | bytes 4866056 | tf_op jit(solution)/shard_map/ppermute | solution.py:159
  106.9 22.3 %collective-permute-start.28 = (bf16[2,528,768]{2,1,0:T(8,128)(2,1)S(1)}, bf16[2,528,768]{2,1,0:T(8,128)(2,1)S(1)}, u32[]{:S(2)}, u32[]{:S(2)}) collective-permute-start(bf16[2,528,768]{2,1,0:T(8,128)(2,1)S(1)} %add_convert_fusion), channel_id=1, source_target_pairs={{0,4},{1,3},{2,6},{3,1},{4,0},{5,7},{6,2},{7,5},{8,12},{9,11},{10,... | collective-permute-start | bytes 4866056 | tf_op jit(solution)/shard_map/ppermute | solution.py:202
  108.1 9.0 %collective-permute-start.27 = (bf16[2,512,128]{2,1,0:T(8,128)(2,1)S(1)}, bf16[2,512,128]{2,1,0:T(8,128)(2,1)S(1)}, u32[]{:S(2)}, u32[]{:S(2)}) collective-permute-start(bf16[2,512,128]{2,1,0:T(8,128)(2,1)S(1)} %get-tuple-element.139), channel_id=1, source_target_pairs={{0,1},{1,0},{2,3},{3,2},{4,5},{5,4},{6,7},{7,6},{8,9},{9,8},{10,11... | collective-permute-start | bytes 786440 | tf_op jit(solution)/shard_map/ppermute | solution.py:1274
  128.6 3.1 %collective-permute-start.30 = (bf16[2,512,384]{2,1,0:T(8,128)(2,1)S(1)}, bf16[2,512,384]{2,1,0:T(8,128)(2,1)S(1)}, u32[]{:S(2)}, u32[]{:S(2)}) collective-permute-start(bf16[2,512,384]{2,1,0:T(8,128)(2,1)S(1)} %get-tuple-element.151), channel_id=1, source_target_pairs={{0,1},{1,0},{2,3},{3,2},{4,5},{5,4},{6,7},{7,6},{8,9},{9,8},{10,11... | collective-permute-start | bytes 2359304 | tf_op jit(solution)/shard_map/ppermute | solution.py:1274
  128.7 3.0 %collective-permute-start.29 = (bf16[2,512,256]{2,1,0:T(8,128)(2,1)S(1)}, bf16[2,512,256]{2,1,0:T(8,128)(2,1)S(1)}, u32[]{:S(2)}, u32[]{:S(2)}) collective-permute-start(bf16[2,512,256]{2,1,0:T(8,128)(2,1)S(1)} %get-tuple-element.149), channel_id=1, source_target_pairs={{0,1},{1,0},{2,3},{3,2},{4,5},{5,4},{6,7},{7,6},{8,9},{9,8},{10,11... | collective-permute-start | bytes 1572872 | tf_op jit(solution)/shard_map/ppermute | solution.py:1274
  129.6 12.3 %collective-permute-start.31 = (bf16[1,528,768]{2,1,0:T(8,128)(2,1)S(1)}, bf16[1,528,768]{2,1,0:T(8,128)(2,1)S(1)}, u32[]{:S(2)}, u32[]{:S(2)}) collective-permute-start(bf16[1,528,768]{2,1,0:T(8,128)(2,1)S(1)} %get-tuple-element.196), channel_id=1, source_target_pairs={{0,2},{1,5},{2,0},{3,7},{4,6},{5,1},{6,4},{7,3},{8,10},{9,13},{10,... | collective-permute-start | bytes 2433032 | tf_op jit(solution)/shard_map/ppermute | solution.py:202
  137.9 4.3 %collective-permute-start.32 = (bf16[2,96,2304]{2,1,0:T(8,128)(2,1)S(1)}, bf16[2,96,2304]{2,1,0:T(8,128)(2,1)S(1)}, u32[]{:S(2)}, u32[]{:S(2)}) collective-permute-start(bf16[2,96,2304]{2,1,0:T(8,128)(2,1)S(1)} %get-tuple-element.156), channel_id=1, source_target_pairs={{0,1},{1,0},{2,3},{3,2},{4,5},{5,4},{6,7},{7,6},{8,9},{9,8},{10,11... | collective-permute-start | bytes 2654216 | tf_op jit(solution)/shard_map/ppermute | solution.py:159
  138.1 11.1 %collective-permute-start.33 = (bf16[2,96,2304]{2,1,0:T(8,128)(2,1)S(1)}, bf16[2,96,2304]{2,1,0:T(8,128)(2,1)S(1)}, u32[]{:S(2)}, u32[]{:S(2)}) collective-permute-start(bf16[2,96,2304]{2,1,0:T(8,128)(2,1)S(1)} %get-tuple-element.158), channel_id=1, source_target_pairs={{0,1},{1,0},{2,3},{3,2},{4,5},{5,4},{6,7},{7,6},{8,9},{9,8},{10,11... | collective-permute-start | bytes 2654216 | tf_op jit(solution)/shard_map/ppermute | solution.py:159
  142.4 17.1 %collective-permute-start.36 = (bf16[2,96,2304]{2,1,0:T(8,128)(2,1)S(1)}, bf16[2,96,2304]{2,1,0:T(8,128)(2,1)S(1)}, u32[]{:S(2)}, u32[]{:S(2)}) collective-permute-start(bf16[2,96,2304]{2,1,0:T(8,128)(2,1)S(1)} %add_convert_fusion.3), channel_id=1, source_target_pairs={{0,4},{1,3},{2,6},{3,1},{4,0},{5,7},{6,2},{7,5},{8,12},{9,11},{10,... | collective-permute-start | bytes 2654216 | tf_op jit(solution)/shard_map/ppermute | solution.py:202
  144.5 12.5 %collective-permute-start.34 = (bf16[288,384]{1,0:T(8,128)(2,1)S(1)}, bf16[288,384]{1,0:T(8,128)(2,1)S(1)}, u32[]{:S(2)}, u32[]{:S(2)}) collective-permute-start(bf16[288,384]{1,0:T(8,128)(2,1)S(1)} %get-tuple-element.161), channel_id=1, source_target_pairs={{0,8},{8,0},{16,24},{24,16},{1,9},{9,1},{17,25},{25,17},{2,10},{10... | collective-permute-start | bytes 663560 | tf_op jit(solution)/shard_map/ppermute | solution.py:1105
  147.9 11.6 %collective-permute-start.35 = (bf16[288,384]{1,0:T(8,128)(2,1)S(1)}, bf16[288,384]{1,0:T(8,128)(2,1)S(1)}, u32[]{:S(2)}, u32[]{:S(2)}) collective-permute-start(bf16[288,384]{1,0:T(8,128)(2,1)S(1)} %get-tuple-element.162), channel_id=1, source_target_pairs={{0,16},{8,24},{16,0},{24,8},{1,17},{9,25},{17,1},{25,9},{2,18},{10... | collective-permute-start | bytes 663560 | tf_op jit(solution)/shard_map/ppermute | solution.py:1105
  159.6 10.8 %collective-permute-start.37 = (bf16[1,96,2304]{2,1,0:T(8,128)(2,1)S(1)}, bf16[1,96,2304]{2,1,0:T(8,128)(2,1)S(1)}, u32[]{:S(2)}, u32[]{:S(2)}) collective-permute-start(bf16[1,96,2304]{2,1,0:T(8,128)(2,1)S(1)} %add_convert_fusion.9), channel_id=1, source_target_pairs={{0,2},{1,5},{2,0},{3,7},{4,6},{5,1},{6,4},{7,3},{8,10},{9,13},{10,... | collective-permute-start | bytes 1327112 | tf_op jit(solution)/shard_map/ppermute | solution.py:202
  160.7 9.8 %collective-permute-start.38 = (bf16[288,384]{1,0:T(8,128)(2,1)S(1)}, bf16[288,384]{1,0:T(8,128)(2,1)S(1)}, u32[]{:S(2)}, u32[]{:S(2)}) collective-permute-start(bf16[288,384]{1,0:T(8,128)(2,1)S(1)} %get-tuple-element.163), channel_id=1, source_target_pairs={{0,24},{8,16},{16,8},{24,0},{1,25},{9,17},{17,9},{25,1},{2,26},{10... | collective-permute-start | bytes 663560 | tf_op jit(solution)/shard_map/ppermute | solution.py:1105
  163.3 12.9 %collective-permute-start.40 = (bf16[2,128,768]{2,1,0:T(8,128)(2,1)S(1)}, bf16[2,128,768]{2,1,0:T(8,128)(2,1)S(1)}, u32[]{:S(2)}, u32[]{:S(2)}) collective-permute-start(bf16[2,128,768]{2,1,0:T(8,128)(2,1)S(1)} %get-tuple-element.182), channel_id=1, source_target_pairs={{0,4},{1,5},{2,6},{3,7},{4,0},{5,1},{6,2},{7,3},{8,12},{9,13},{10,... | collective-permute-start | bytes 1179656 | tf_op jit(solution)/shard_map/ppermute | solution.py:172
  164.4 15.1 %collective-permute-start.39 = (bf16[2,128,768]{2,1,0:T(8,128)(2,1)S(1)}, bf16[2,128,768]{2,1,0:T(8,128)(2,1)S(1)}, u32[]{:S(2)}, u32[]{:S(2)}) collective-permute-start(bf16[2,128,768]{2,1,0:T(8,128)(2,1)S(1)} %get-tuple-element.180), channel_id=1, source_target_pairs={{0,2},{1,3},{2,0},{3,1},{4,6},{5,7},{6,4},{7,5},{8,10},{9,11},{10,... | collective-permute-start | bytes 1179656 | tf_op jit(solution)/shard_map/ppermute | solution.py:172
  171.5 14.0 %collective-permute-start.42 = (bf16[96,640]{1,0:T(8,128)(2,1)S(1)}, bf16[96,640]{1,0:T(8,128)(2,1)S(1)}, u32[]{:S(2)}, u32[]{:S(2)}) collective-permute-start(bf16[96,640]{1,0:T(8,128)(2,1)S(1)} %get-tuple-element.175), channel_id=1, source_target_pairs={{0,8},{8,0},{16,24},{24,16},{1,9},{9,1},{17,25},{25,17},{2,10},{10... | collective-permute-start | bytes 368648 | tf_op jit(solution)/shard_map/ppermute | solution.py:1105
  172.7 12.7 %collective-permute-start.43 = (bf16[96,640]{1,0:T(8,128)(2,1)S(1)}, bf16[96,640]{1,0:T(8,128)(2,1)S(1)}, u32[]{:S(2)}, u32[]{:S(2)}) collective-permute-start(bf16[96,640]{1,0:T(8,128)(2,1)S(1)} %get-tuple-element.176), channel_id=1, source_target_pairs={{0,16},{8,24},{16,0},{24,8},{1,17},{9,25},{17,1},{25,9},{2,18},{10... | collective-permute-start | bytes 368648 | tf_op jit(solution)/shard_map/ppermute | solution.py:1105
  173.4 10.2 %collective-permute-start.41 = (bf16[2,128,768]{2,1,0:T(8,128)(2,1)S(1)}, bf16[2,128,768]{2,1,0:T(8,128)(2,1)S(1)}, u32[]{:S(2)}, u32[]{:S(2)}) collective-permute-start(bf16[2,128,768]{2,1,0:T(8,128)(2,1)S(1)} %get-tuple-element.185), channel_id=1, source_target_pairs={{0,6},{1,7},{2,4},{3,5},{4,2},{5,3},{6,0},{7,1},{8,14},{9,15},{10,... | collective-permute-start | bytes 1179656 | tf_op jit(solution)/shard_map/ppermute | solution.py:172
  176.2 9.2 %collective-permute-start.44 = (bf16[96,640]{1,0:T(8,128)(2,1)S(1)}, bf16[96,640]{1,0:T(8,128)(2,1)S(1)}, u32[]{:S(2)}, u32[]{:S(2)}) collective-permute-start(bf16[96,640]{1,0:T(8,128)(2,1)S(1)} %get-tuple-element.177), channel_id=1, source_target_pairs={{0,24},{8,16},{16,8},{24,0},{1,25},{9,17},{17,9},{25,1},{2,26},{10... | collective-permute-start | bytes 368648 | tf_op jit(solution)/shard_map/ppermute | solution.py:1105
  (50 other events, 376.7 us)

commit v4 on v3

--- a/solution.py
+++ b/solution.py
@@ -32,11 +32,11 @@
     "join_rest": 6,
     "project": 20,
     "masks": 4,
-    "attend": 16,
+    "attend": 12,
     "middle": 56,
-    "attend_back": 16,
+    "attend_back": 12,
     "back_in": 20,
-    "back_weight": 16,
+    "back_weight": 14,
     "cut_qkv": 4,
     "cut_rest": 6,
     "end_rest": 4,
@@ -800,14 +800,11 @@
         for t in range(1, 3):
             grad = grad + dot(dgu_ref[:, D * t : D * (t + 1)], w_in[t, cols, :], NT)
         dh_ref[:, cols] = grad
+        g_in[n] = dot(
+            n_ref[...], dgu_ref[:, pl.ds(pl.multiple_of(n * D, D), D)], TN
+        ).astype(BF16)
     for j in range(rows):
         mover.send(out_ref.at[pl.ds(tok * j, tok)], out_refs[j])
-
-    @pl.loop(0, 3)
-    def _(t):
-        g_in[t] = dot(
-            n_ref[...], dgu_ref[:, pl.ds(pl.multiple_of(t * D, D), D)], TN
-        ).astype(BF16)
 
     for t in range(3):
         for target, block in zip(targets, blocks):

time: 187 us -> 186 us (level)
  no operation moved by 1% of the time
where the time goes in v4:
time: 186 us
  Pallas kernels  83.1 us (45%)
  starting transfers between devices  48.1 us (26%)
  waiting for transfers between devices  36.5 us (20%)
  local copies, waits for them, and re-layouts  9.79 us (5%)
  other arithmetic  4.64 us (2%)
  between operations  3.38 us (2%)
    pallas_call x3, Pallas kernels, attend_back(): pl.pallas_call(functools.partial(attend_back_kernel, plan, width), grid=(...  23.4 us
    pallas_call x1, Pallas kernels, middle(): pl.pallas_call(functools.partial(middle_kernel, plan), in_specs=[SMEM, VM...  18.7 us
    ppermute x6, starting transfers between devices, gather_z(): pieces.append(lax.ppermute(source, 'row', plan.z_pairs(j)))  15.4 us
    pallas_call x2, Pallas kernels, attend(): pl.pallas_call(functools.partial(attend_kernel, plan, width), grid=(HALF_...  12.9 us
    ppermute x6, starting transfers between devices, reduce_z(): lax.ppermute(pieces[j], 'row', plan.z_pairs(j))  11.9 us
    ppermute x6, waiting for transfers between devices, gather_z(): pieces.append(lax.ppermute(source, 'row', plan.z_pairs(j)))  8.91 us
    ppermute x4, waiting for transfers between devices, reduce_step(): moved = lax.ppermute(high, 'blk', plan.step_pairs(step))  8.4 us
    ppermute x6, waiting for transfers between devices, exchange_rows(): lax.ppermute(pieces[j], 'blk', plan.xor_pairs(2 * j))  7.94 us
  transfers between devices with their start and end apart: 45, of which 17 were waited for; matrix products, arithmetic and copies ran while one was open for 4% of the time, Pallas kernels for 34%

profile of v4, /device:TPU:0, one launch (start us, length us, event | category | flops | bytes accessed | tf_op | source)
XLA Modules:
  0.0 185.5 jit_solution(4474702945800368318)
XLA Ops:
  0.7 4.1 %collective-permute-start.1 = (bf16[96,576]{1,0:T(8,128)(2,1)}, bf16[96,576]{1,0:T(8,128)(2,1)S(1)}, u32[]{:S(2)}, u32[]{:S(2)}) collective-permute-start(bf16[96,576]{1,0:T(8,128)(2,1)} %refs_0_.1), channel_id=1, source_target_pairs={{0,16},{8,24},{16,0},{24,8},{1,17},{9,25},{17,1},{25,9},{2,18},{10... | collective-permute-start | bytes 331784 | tf_op jit(solution)/shard_map/ppermute | solution.py:166
  4.8 1.3 collective-permute-start.2
  6.4 1.2 fusion.3.meta.order
  7.6 2.7 %prepare.1 = (bf16[2,128,768]{2,1,0:T(8,128)(2,1)}, bf16[2,128,768]{2,1,0:T(8,128)(2,1)}, bf16[2,128,768]{2,1,0:T(8,128)(2,1)}, bf16[2,128,768]{2,1,0:T(8,128)(2,1)}, bf16[288,384]{1,0:T(8,128)(2,1)}) custom-call(s32[25]{0:T(128)} %fusion.3.meta.order, bf16[4,128,768]{2,1,0:T(8,128)(2,1)} %tokens.1, bf16[4,128,768]{2,1,0:T(8,128)(2,1)} %cotangent.1, ...), custom_call_target="tpu_custom_call" | custom-call | flops 4000000 | bytes 1024 | tf_op jit(solution)/shard_map/prepare/pallas_call | solution.py:262
  10.2 2.4 %collective-permute-start.10 = (bf16[2,128,768]{2,1,0:T(8,128)(2,1)}, bf16[2,128,768]{2,1,0:T(8,128)(2,1)S(1)}, u32[]{:S(2)}, u32[]{:S(2)}) collective-permute-start(bf16[2,128,768]{2,1,0:T(8,128)(2,1)} %get-tuple-element.110), channel_id=1, source_target_pairs={{0,6},{1,7},{2,4},{3,5},{4,2},{5,3},{6,0},{7,1},{8,14},{9,15},{10,... | collective-permute-start | bytes 1179656 | tf_op jit(solution)/shard_map/ppermute | solution.py:172
  18.5 1.6 collective-permute-start.4
  20.1 2.8 %collective-permute-start.5 = (bf16[288,384]{1,0:T(8,128)(2,1)}, bf16[288,384]{1,0:T(8,128)(2,1)S(1)}, u32[]{:S(2)}, u32[]{:S(2)}) collective-permute-start(bf16[288,384]{1,0:T(8,128)(2,1)} %get-tuple-element.113.refs_0_), channel_id=1, source_target_pairs={{0,16},{8,24},{16,0},{24,8},{1,17},{9,25},{17,1},{25,9},{2,18},{10... | collective-permute-start | bytes 663560 | tf_op jit(solution)/shard_map/ppermute | solution.py:166
  23.4 2.9 %collective-permute-start.6 = (bf16[288,384]{1,0:T(8,128)(2,1)}, bf16[288,384]{1,0:T(8,128)(2,1)S(1)}, u32[]{:S(2)}, u32[]{:S(2)}) collective-permute-start(bf16[288,384]{1,0:T(8,128)(2,1)} %get-tuple-element.113.refs_0_), channel_id=1, source_target_pairs={{0,24},{8,16},{16,8},{24,0},{1,25},{9,17},{17,9},{25,1},{2,26},{10... | collective-permute-start | bytes 663560 | tf_op jit(solution)/shard_map/ppermute | solution.py:166
  26.3 1.0 fusion.2
  27.3 2.8 %collective-permute-done.8.refs_1_.refs_3_ = bf16[2,128,768]{2,1,0:T(8,128)(2,1)S(1)} collective-permute-done((bf16[2,128,768]{2,1,0:T(8,128)(2,1)}, bf16[2,128,768]{2,1,0:T(8,128)(2,1)S(1)}, u32[]{:S(2)}, u32[]{:S(2)}) %collective-permute-start.8) | collective-permute-done | bytes 393248 | tf_op jit(solution)/shard_map/ppermute | solution.py:172
  30.6 1.1 collective-permute-start.11
  32.2 1.1 masks.1
  33.2 4.1 %collective-permute-done.5.refs_2_ = bf16[288,384]{1,0:T(8,128)(2,1)S(1)} collective-permute-done((bf16[288,384]{1,0:T(8,128)(2,1)}, bf16[288,384]{1,0:T(8,128)(2,1)S(1)}, u32[]{:S(2)}, u32[]{:S(2)}) %collective-permute-start.5) | collective-permute-done | bytes 221216 | tf_op jit(solution)/shard_map/ppermute | solution.py:166
  38.1 4.0 %collective-permute-start.13 = (bf16[288,384]{1,0:T(8,128)(2,1)S(1)}, bf16[288,384]{1,0:T(8,128)(2,1)S(1)}, u32[]{:S(2)}, u32[]{:S(2)}) collective-permute-start(bf16[288,384]{1,0:T(8,128)(2,1)S(1)} %copy-done.27), channel_id=1, source_target_pairs={{0,8},{8,0},{16,24},{24,16},{1,9},{9,1},{17,25},{25,17},{2,10},{10... | collective-permute-start | bytes 663560 | tf_op jit(solution)/shard_map/ppermute | solution.py:166
  42.6 4.8 %collective-permute-done.13.refs_1_ = bf16[288,384]{1,0:T(8,128)(2,1)S(1)} collective-permute-done((bf16[288,384]{1,0:T(8,128)(2,1)S(1)}, bf16[288,384]{1,0:T(8,128)(2,1)S(1)}, u32[]{:S(2)}, u32[]{:S(2)}) %collective-permute-start.13) | collective-permute-done | bytes 221216 | tf_op jit(solution)/shard_map/ppermute | solution.py:166
  49.3 5.9 %project.1 = (bf16[512,768]{1,0:T(8,128)(2,1)S(1)}, bf16[2,512,384]{2,1,0:T(8,128)(2,1)S(1)}, bf16[2,512,384]{2,1,0:T(8,128)(2,1)S(1)}, bf16[512,768]{1,0:T(8,128)(2,1)S(1)}, f32[8,768]{1,0:T(8,128)S(1)}) custom-call(s32[25]{0:T(128)S(1)} %copy-done.32, f32[512,128]{1,0:T(8,128)S(1)} %get-tuple-element.203.cos_ref.refs_0_, ...), custom_call_target="tpu_custom_call" | custom-call | flops 7000000 | bytes 1024 | tf_op jit(solution)/shard_map/project/pallas_call | solution.py:500
  56.0 1.3 collective-permute-start.18
  58.1 6.4 %attend.2 = (f32[512,384]{1,0:T(8,128)S(1)}, bf16[512,384]{1,0:T(8,128)(2,1)S(1)}, f32[3,2,512]{2,1,0:T(2,128)S(1)}) custom-call(s32[25]{0:T(128)S(1)} %copy-done.32, bf16[1024,128]{1,0:T(8,128)(2,1)S(1)} %get-tuple-element.105.kmask, bf16[512,128]{1,0:T(8,128)(2,1)S(1)} %get-tuple-element.106.qmask, bf16[512,768]{1,0:T(8,128)(2,1)S(1)} %get-tuple-element.118.q_ref, ...), custom_call_target="tpu_custom_call" | custom-call | flops 9000000 | bytes 1024 | tf_op jit(solution)/shard_map/attend/pallas_call | solution.py:605
  65.9 1.0 collective-permute-start.20
  67.5 1.4 collective-permute-done.18.refs_8_
  69.3 6.4 %attend.3 = (f32[512,384]{1,0:T(8,128)S(1)}, bf16[512,384]{1,0:T(8,128)(2,1)S(1)}, f32[3,2,512]{2,1,0:T(2,128)S(1)}) custom-call(s32[25]{0:T(128)S(1)} %copy-done.32, bf16[1024,128]{1,0:T(8,128)(2,1)S(1)} %get-tuple-element.105.kmask, bf16[512,128]{1,0:T(8,128)(2,1)S(1)} %get-tuple-element.106.qmask, bf16[512,768]{1,0:T(8,128)(2,1)S(1)} %get-tuple-element.118.q_ref, ...), custom_call_target="tpu_custom_call" | custom-call | flops 9000000 | bytes 1024 | tf_op jit(solution)/shard_map/attend/pallas_call | solution.py:605
  78.2 2.3 %collective-permute-done.24.refs_13_ = bf16[528,768]{1,0:T(8,128)(2,1)S(1)} collective-permute-done((bf16[528,768]{1,0:T(8,128)(2,1)S(1)}, bf16[528,768]{1,0:T(8,128)(2,1)S(1)}, u32[]{:S(2)}, u32[]{:S(2)}) %collective-permute-start.24) | collective-permute-done | bytes 811040 | tf_op jit(solution)/shard_map/ppermute | solution.py:159
  81.4 18.7 %middle.1 = (bf16[128,768]{1,0:T(8,128)(2,1)}, bf16[128,768]{1,0:T(8,128)(2,1)}, bf16[128,768]{1,0:T(8,128)(2,1)}, bf16[128,768]{1,0:T(8,128)(2,1)}, bf16[512,76...) custom-call(s32[25]{0:T(128)} %fusion.3.meta.order, ...), custom_call_target="tpu_custom_call" | custom-call | flops 20000000 | bytes 1024 | tf_op jit(solution)/shard_map/middle/pallas_call | solution.py:836
  100.7 1.1 copy-done.2
  101.8 4.0 %attend_back.3 = (bf16[512,128]{1,0:T(8,128)(2,1)S(1)}, bf16[2,512,128]{2,1,0:T(8,128)(2,1)S(1)}, bf16[2,512,128]{2,1,0:T(8,128)(2,1)S(1)}) custom-call(s32[25]{0:T(128)S(1)} %copy-done.33, bf16[1024,128]{1,0:T(8,128)(2,1)S(1)} %get-tuple-element.105.kmask, bf16[512,128]{1,0:T(8,128)(2,1)S(1)} %get-tuple-element.106.qmask, ...), custom_call_target="tpu_custom_call" | custom-call | flops 4000000 | bytes 1024 | tf_op jit(solution)/shard_map/attend_back/pallas_call | solution.py:686
  106.2 1.1 collective-permute-start.28
  108.5 7.8 %attend_back.4 = (bf16[512,256]{1,0:T(8,128)(2,1)S(1)}, bf16[2,512,256]{2,1,0:T(8,128)(2,1)S(1)}, bf16[2,512,256]{2,1,0:T(8,128)(2,1)S(1)}) custom-call(s32[25]{0:T(128)S(1)} %copy-done.33, bf16[1024,128]{1,0:T(8,128)(2,1)S(1)} %get-tuple-element.105.kmask, bf16[512,128]{1,0:T(8,128)(2,1)S(1)} %get-tuple-element.106.qmask, ...), custom_call_target="tpu_custom_call" | custom-call | flops 8000000 | bytes 1024 | tf_op jit(solution)/shard_map/attend_back/pallas_call | solution.py:686
  116.3 11.6 %attend_back.5 = (bf16[512,384]{1,0:T(8,128)(2,1)S(1)}, bf16[2,512,384]{2,1,0:T(8,128)(2,1)S(1)}, bf16[2,512,384]{2,1,0:T(8,128)(2,1)S(1)}) custom-call(s32[25]{0:T(128)S(1)} %copy-done.33, bf16[1024,128]{1,0:T(8,128)(2,1)S(1)} %get-tuple-element.105.kmask, bf16[512,128]{1,0:T(8,128)(2,1)S(1)} %get-tuple-element.106.qmask, ...), custom_call_target="tpu_custom_call" | custom-call | flops 12000000 | bytes 1024 | tf_op jit(solution)/shard_map/attend_back/pallas_call | solution.py:686
  128.9 1.0 collective-permute-start.31
  129.9 1.1 collective-permute-done.29.refs_9_
  131.0 6.1 %back_weight.1 = (bf16[3,512,768]{2,1,0:T(8,128)(2,1)S(1)}, bf16[2,96,2304]{2,1,0:T(8,128)(2,1)S(1)}, bf16[2,96,2304]{2,1,0:T(8,128)(2,1)S(1)}, bf16[2,96,2304]{2,1,0:T(8,128)(2,1)S(1)}, bf16[2,96,2304]{2,1,0:T(8,128)(2,1)S(1)}) custom-call(s32[25]{0:T(128)S(1)} %copy-done.33, f32[512,128]{1,0:T(8,128)S(1)} %get-tuple-element.203.cos_ref.refs_0_, ...), custom_call_target="tpu_custom_call" | custom-call | flops 6000000 | bytes 1024 | tf_op jit(solution)/shard_map/back_weight/pallas_call | solution.py:924
  137.7 3.5 %collective-permute-done.31 = bf16[1,528,768]{2,1,0:T(8,128)(2,1)S(1)} collective-permute-done((bf16[1,528,768]{2,1,0:T(8,128)(2,1)S(1)}, bf16[1,528,768]{2,1,0:T(8,128)(2,1)S(1)}, u32[]{:S(2)}, u32[]{:S(2)}) %collective-permute-start.31) | collective-permute-done | bytes 811040 | tf_op jit(solution)/shard_map/ppermute | solution.py:202
  141.7 1.0 collective-permute-start.36
  143.8 3.4 %collective-permute-start.34 = (bf16[288,384]{1,0:T(8,128)(2,1)S(1)}, bf16[288,384]{1,0:T(8,128)(2,1)S(1)}, u32[]{:S(2)}, u32[]{:S(2)}) collective-permute-start(bf16[288,384]{1,0:T(8,128)(2,1)S(1)} %get-tuple-element.161), channel_id=1, source_target_pairs={{0,8},{8,0},{16,24},{24,16},{1,9},{9,1},{17,25},{25,17},{2,10},{10... | collective-permute-start | bytes 663560 | tf_op jit(solution)/shard_map/ppermute | solution.py:1102
  147.2 1.2 collective-permute-start.35
  148.8 5.6 %back_in.1 = (bf16[2,128,768]{2,1,0:T(8,128)(2,1)S(1)}, bf16[2,128,768]{2,1,0:T(8,128)(2,1)S(1)}, bf16[2,128,768]{2,1,0:T(8,128)(2,1)S(1)}, bf16[2,128,768]{2,1,0:T(8,128)(2,1)S(1)}) custom-call(s32[25]{0:T(128)S(1)} %copy-done.33, bf16[3,512,768]{2,1,0:T(8,128)(2,1)S(1)} %get-tuple-element.153.dp_ref, f32[512,768]{1,0:T(8,128)S(1)} %copy-done.20, ...), custom_call_target="tpu_custom_call" | custom-call | flops 7000000 | bytes 1024 | tf_op jit(solution)/shard_map/back_in/pallas_call | solution.py:973
  154.4 1.9 %collective-permute-done.34.refs_1_ = bf16[288,384]{1,0:T(8,128)(2,1)S(1)} collective-permute-done((bf16[288,384]{1,0:T(8,128)(2,1)S(1)}, bf16[288,384]{1,0:T(8,128)(2,1)S(1)}, u32[]{:S(2)}, u32[]{:S(2)}) %collective-permute-start.34) | collective-permute-done | bytes 221216 | tf_op jit(solution)/shard_map/ppermute | solution.py:1102
  156.3 2.5 %collective-permute-done.35.refs_2_ = bf16[288,384]{1,0:T(8,128)(2,1)S(1)} collective-permute-done((bf16[288,384]{1,0:T(8,128)(2,1)S(1)}, bf16[288,384]{1,0:T(8,128)(2,1)S(1)}, u32[]{:S(2)}, u32[]{:S(2)}) %collective-permute-start.35) | collective-permute-done | bytes 221216 | tf_op jit(solution)/shard_map/ppermute | solution.py:1102
  158.9 1.1 collective-permute-start.37
  160.0 2.6 %collective-permute-start.38 = (bf16[288,384]{1,0:T(8,128)(2,1)S(1)}, bf16[288,384]{1,0:T(8,128)(2,1)S(1)}, u32[]{:S(2)}, u32[]{:S(2)}) collective-permute-start(bf16[288,384]{1,0:T(8,128)(2,1)S(1)} %get-tuple-element.163), channel_id=1, source_target_pairs={{0,24},{8,16},{16,8},{24,0},{1,25},{9,17},{17,9},{25,1},{2,26},{10... | collective-permute-start | bytes 663560 | tf_op jit(solution)/shard_map/ppermute | solution.py:1102
  162.6 1.1 collective-permute-start.40
  163.7 1.1 collective-permute-start.39
  164.8 4.9 %collective-permute-done.37 = bf16[1,96,2304]{2,1,0:T(8,128)(2,1)S(1)} collective-permute-done((bf16[1,96,2304]{2,1,0:T(8,128)(2,1)S(1)}, bf16[1,96,2304]{2,1,0:T(8,128)(2,1)S(1)}, u32[]{:S(2)}, u32[]{:S(2)}) %collective-permute-start.37) | collective-permute-done | bytes 442400 | tf_op jit(solution)/shard_map/ppermute | solution.py:202
  170.7 1.2 collective-permute-start.42
  172.7 1.9 %collective-permute-start.41 = (bf16[2,128,768]{2,1,0:T(8,128)(2,1)S(1)}, bf16[2,128,768]{2,1,0:T(8,128)(2,1)S(1)}, u32[]{:S(2)}, u32[]{:S(2)}) collective-permute-start(bf16[2,128,768]{2,1,0:T(8,128)(2,1)S(1)} %get-tuple-element.185), channel_id=1, source_target_pairs={{0,6},{1,7},{2,4},{3,5},{4,2},{5,3},{6,0},{7,1},{8,14},{9,15},{10,... | collective-permute-start | bytes 1179656 | tf_op jit(solution)/shard_map/ppermute | solution.py:172
  175.5 2.7 %collective-permute-start.44 = (bf16[96,640]{1,0:T(8,128)(2,1)S(1)}, bf16[96,640]{1,0:T(8,128)(2,1)S(1)}, u32[]{:S(2)}, u32[]{:S(2)}) collective-permute-start(bf16[96,640]{1,0:T(8,128)(2,1)S(1)} %get-tuple-element.177), channel_id=1, source_target_pairs={{0,24},{8,16},{16,8},{24,0},{1,25},{9,17},{17,9},{25,1},{2,26},{10... | collective-permute-start | bytes 368648 | tf_op jit(solution)/shard_map/ppermute | solution.py:1102
  178.8 4.1 %collective-permute-done.41.refs_3_ = bf16[2,128,768]{2,1,0:T(8,128)(2,1)S(1)} collective-permute-done((bf16[2,128,768]{2,1,0:T(8,128)(2,1)S(1)}, bf16[2,128,768]{2,1,0:T(8,128)(2,1)S(1)}, u32[]{:S(2)}, u32[]{:S(2)}) %collective-permute-start.41) | collective-permute-done | bytes 393248 | tf_op jit(solution)/shard_map/ppermute | solution.py:172
  182.9 1.8 place_rows.1
  (194 shorter events, 25.3 us)
Async XLA Ops:
  0.7 16.4 %collective-permute-start.1 = (bf16[96,576]{1,0:T(8,128)(2,1)}, bf16[96,576]{1,0:T(8,128)(2,1)S(1)}, u32[]{:S(2)}, u32[]{:S(2)}) collective-permute-start(bf16[96,576]{1,0:T(8,128)(2,1)} %refs_0_.1), channel_id=1, source_target_pairs={{0,16},{8,24},{16,0},{24,8},{1,17},{9,25},{17,1},{25,9},{2,18},{10... | collective-permute-start | bytes 331784 | tf_op jit(solution)/shard_map/ppermute | solution.py:166
  4.8 12.9 %collective-permute-start.2 = (bf16[96,576]{1,0:T(8,128)(2,1)}, bf16[96,576]{1,0:T(8,128)(2,1)S(1)}, u32[]{:S(2)}, u32[]{:S(2)}) collective-permute-start(bf16[96,576]{1,0:T(8,128)(2,1)} %refs_0_.1), channel_id=1, source_target_pairs={{0,24},{8,16},{16,8},{24,0},{1,25},{9,17},{17,9},{25,1},{2,26},{10... | collective-permute-start | bytes 331784 | tf_op jit(solution)/shard_map/ppermute | solution.py:166
  6.1 11.6 %collective-permute-start = (bf16[96,576]{1,0:T(8,128)(2,1)}, bf16[96,576]{1,0:T(8,128)(2,1)S(1)}, u32[]{:S(2)}, u32[]{:S(2)}) collective-permute-start(bf16[96,576]{1,0:T(8,128)(2,1)} %refs_0_.1), channel_id=1, source_target_pairs={{0,8},{8,0},{16,24},{24,16},{1,9},{9,1},{17,25},{25,17},{2,10},{10... | collective-permute-start | bytes 331784 | tf_op jit(solution)/shard_map/ppermute | solution.py:166
  10.2 27.8 %copy-start.27 = (bf16[288,384]{1,0:T(8,128)(2,1)S(1)}, bf16[288,384]{1,0:T(8,128)(2,1)}, u32[]{:S(2)}) copy-start(bf16[288,384]{1,0:T(8,128)(2,1)} %get-tuple-element.113.refs_0_) | copy-start | bytes 663556
  10.2 13.2 %collective-permute-start.10 = (bf16[2,128,768]{2,1,0:T(8,128)(2,1)}, bf16[2,128,768]{2,1,0:T(8,128)(2,1)S(1)}, u32[]{:S(2)}, u32[]{:S(2)}) collective-permute-start(bf16[2,128,768]{2,1,0:T(8,128)(2,1)} %get-tuple-element.110), channel_id=1, source_target_pairs={{0,6},{1,7},{2,4},{3,5},{4,2},{5,3},{6,0},{7,1},{8,14},{9,15},{10,... | collective-permute-start | bytes 1179656 | tf_op jit(solution)/shard_map/ppermute | solution.py:172
  12.7 17.5 %collective-permute-start.8 = (bf16[2,128,768]{2,1,0:T(8,128)(2,1)}, bf16[2,128,768]{2,1,0:T(8,128)(2,1)S(1)}, u32[]{:S(2)}, u32[]{:S(2)}) collective-permute-start(bf16[2,128,768]{2,1,0:T(8,128)(2,1)} %get-tuple-element.108), channel_id=1, source_target_pairs={{0,2},{1,3},{2,0},{3,1},{4,6},{5,7},{6,4},{7,5},{8,10},{9,11},{10,... | collective-permute-start | bytes 1179656 | tf_op jit(solution)/shard_map/ppermute | solution.py:172
  17.1 13.6 %collective-permute-start.9 = (bf16[2,128,768]{2,1,0:T(8,128)(2,1)}, bf16[2,128,768]{2,1,0:T(8,128)(2,1)S(1)}, u32[]{:S(2)}, u32[]{:S(2)}) collective-permute-start(bf16[2,128,768]{2,1,0:T(8,128)(2,1)} %get-tuple-element.109), channel_id=1, source_target_pairs={{0,4},{1,5},{2,6},{3,7},{4,0},{5,1},{6,2},{7,3},{8,12},{9,13},{10,... | collective-permute-start | bytes 1179656 | tf_op jit(solution)/shard_map/ppermute | solution.py:172
  18.5 19.6 %collective-permute-start.4 = (bf16[96,2432]{1,0:T(8,128)(2,1)S(1)}, bf16[96,2432]{1,0:T(8,128)(2,1)S(1)}, u32[]{:S(2)}, u32[]{:S(2)}) collective-permute-start(bf16[96,2432]{1,0:T(8,128)(2,1)S(1)} %join_qkv.1.refs_4_.refs_8_.weight), channel_id=1, source_target_pairs={{0,2},{1,5},{2,0},{3,7},{4,6},{5,1},{6,4},{7,3},{8,10},{9,13},{10,... | collective-permute-start | bytes 1400840 | tf_op jit(solution)/shard_map/ppermute | solution.py:178
  20.1 17.2 %collective-permute-start.5 = (bf16[288,384]{1,0:T(8,128)(2,1)}, bf16[288,384]{1,0:T(8,128)(2,1)S(1)}, u32[]{:S(2)}, u32[]{:S(2)}) collective-permute-start(bf16[288,384]{1,0:T(8,128)(2,1)} %get-tuple-element.113.refs_0_), channel_id=1, source_target_pairs={{0,16},{8,24},{16,0},{24,8},{1,17},{9,25},{17,1},{25,9},{2,18},{10... | collective-permute-start | bytes 663560 | tf_op jit(solution)/shard_map/ppermute | solution.py:166
  23.4 25.8 %copy-start.6 = (bf16[2,128,768]{2,1,0:T(8,128)(2,1)}, bf16[2,128,768]{2,1,0:T(8,128)(2,1)S(1)}, u32[]{:S(2)}) copy-start(bf16[2,128,768]{2,1,0:T(8,128)(2,1)S(1)} %collective-permute-done.10.refs_3_.refs_5_) | copy-start | bytes 1179652
  23.4 13.9 %collective-permute-start.6 = (bf16[288,384]{1,0:T(8,128)(2,1)}, bf16[288,384]{1,0:T(8,128)(2,1)S(1)}, u32[]{:S(2)}, u32[]{:S(2)}) collective-permute-start(bf16[288,384]{1,0:T(8,128)(2,1)} %get-tuple-element.113.refs_0_), channel_id=1, source_target_pairs={{0,24},{8,16},{16,8},{24,0},{1,25},{9,17},{17,9},{25,1},{2,26},{10... | collective-permute-start | bytes 663560 | tf_op jit(solution)/shard_map/ppermute | solution.py:166
  30.2 25.0 %copy-start.8 = (bf16[2,128,768]{2,1,0:T(8,128)(2,1)}, bf16[2,128,768]{2,1,0:T(8,128)(2,1)S(1)}, u32[]{:S(2)}) copy-start(bf16[2,128,768]{2,1,0:T(8,128)(2,1)S(1)} %collective-permute-done.8.refs_1_.refs_3_) | copy-start | bytes 1179652
  30.6 12.0 %collective-permute-start.11 = (bf16[96,2432]{1,0:T(8,128)(2,1)S(1)}, bf16[96,2432]{1,0:T(8,128)(2,1)S(1)}, u32[]{:S(2)}, u32[]{:S(2)}) collective-permute-start(bf16[96,2432]{1,0:T(8,128)(2,1)S(1)} %join_qkv.1.refs_4_.refs_8_.weight), channel_id=1, source_target_pairs={{0,4},{1,3},{2,6},{3,1},{4,0},{5,7},{6,2},{7,5},{8,12},{9,11},{10,... | collective-permute-start | bytes 1400840 | tf_op jit(solution)/shard_map/ppermute | solution.py:179
  38.0 9.4 %collective-permute-start.14 = (bf16[96,2432]{1,0:T(8,128)(2,1)S(1)}, bf16[96,2432]{1,0:T(8,128)(2,1)S(1)}, u32[]{:S(2)}, u32[]{:S(2)}) collective-permute-start(bf16[96,2432]{1,0:T(8,128)(2,1)S(1)} %collective-permute-done.4.refs_5_.refs_9_), channel_id=1, source_target_pairs={{0,4},{1,3},{2,6},{3,1},{4,0},{5,7},{6,2},{7,5},{8,12},{9,11},{10,... | collective-permute-start | bytes 1400840 | tf_op jit(solution)/shard_map/ppermute | solution.py:187
  38.1 9.3 %collective-permute-start.13 = (bf16[288,384]{1,0:T(8,128)(2,1)S(1)}, bf16[288,384]{1,0:T(8,128)(2,1)S(1)}, u32[]{:S(2)}, u32[]{:S(2)}) collective-permute-start(bf16[288,384]{1,0:T(8,128)(2,1)S(1)} %copy-done.27), channel_id=1, source_target_pairs={{0,8},{8,0},{16,24},{24,16},{1,9},{9,1},{17,25},{25,17},{2,10},{10... | collective-permute-start | bytes 663560 | tf_op jit(solution)/shard_map/ppermute | solution.py:166
  42.1 5.4 %collective-permute-start.3 = (bf16[96,2432]{1,0:T(8,128)(2,1)S(1)}, bf16[96,2432]{1,0:T(8,128)(2,1)S(1)}, u32[]{:S(2)}, u32[]{:S(2)}) collective-permute-start(bf16[96,2432]{1,0:T(8,128)(2,1)S(1)} %join_qkv.1.refs_4_.refs_8_.weight), channel_id=1, source_target_pairs={{0,1},{1,0},{2,3},{3,2},{4,5},{5,4},{6,7},{7,6},{8,9},{9,8},{10,11... | collective-permute-start | bytes 1400840 | tf_op jit(solution)/shard_map/ppermute | solution.py:159
  42.1 5.4 %collective-permute-start.7 = (bf16[96,2432]{1,0:T(8,128)(2,1)S(1)}, bf16[96,2432]{1,0:T(8,128)(2,1)S(1)}, u32[]{:S(2)}, u32[]{:S(2)}) collective-permute-start(bf16[96,2432]{1,0:T(8,128)(2,1)S(1)} %collective-permute-done.4.refs_5_.refs_9_), channel_id=1, source_target_pairs={{0,1},{1,0},{2,3},{3,2},{4,5},{5,4},{6,7},{7,6},{8,9},{9,8},{10,11... | collective-permute-start | bytes 1400840 | tf_op jit(solution)/shard_map/ppermute | solution.py:159
  42.6 4.9 %collective-permute-start.12 = (bf16[96,2432]{1,0:T(8,128)(2,1)S(1)}, bf16[96,2432]{1,0:T(8,128)(2,1)S(1)}, u32[]{:S(2)}, u32[]{:S(2)}) collective-permute-start(bf16[96,2432]{1,0:T(8,128)(2,1)S(1)} %collective-permute-done.11.refs_6_.refs_10_), channel_id=1, source_target_pairs={{0,1},{1,0},{2,3},{3,2},{4,5},{5,4},{6,7},{7,6},{8,9},{9,8},{10,11... | collective-permute-start | bytes 1400840 | tf_op jit(solution)/shard_map/ppermute | solution.py:159
  47.4 1.8 collective-permute-start.15
  48.4 17.5 %collective-permute-start.17 = (bf16[528,768]{1,0:T(8,128)(2,1)S(1)}, bf16[528,768]{1,0:T(8,128)(2,1)S(1)}, u32[]{:S(2)}, u32[]{:S(2)}) collective-permute-start(bf16[528,768]{1,0:T(8,128)(2,1)S(1)} %join_rest.1.refs_6_.weight), channel_id=1, source_target_pairs={{0,2},{1,5},{2,0},{3,7},{4,6},{5,1},{6,4},{7,3},{8,10},{9,13},{10,... | collective-permute-start | bytes 2433032 | tf_op jit(solution)/shard_map/ppermute | solution.py:178
  55.8 2.3 %collective-permute-start.16 = (bf16[2,512,384]{2,1,0:T(8,128)(2,1)S(1)}, bf16[2,512,384]{2,1,0:T(8,128)(2,1)S(1)}, u32[]{:S(2)}, u32[]{:S(2)}) collective-permute-start(bf16[2,512,384]{2,1,0:T(8,128)(2,1)S(1)} %get-tuple-element.119.refs_0_), channel_id=1, source_target_pairs={{0,1},{1,0},{2,3},{3,2},{4,5},{5,4},{6,7},{7,6},{8,9},{9,8},{10,11... | collective-permute-start | bytes 2359304 | tf_op jit(solution)/shard_map/ppermute | solution.py:1231
  56.0 12.9 %collective-permute-start.18 = (bf16[528,768]{1,0:T(8,128)(2,1)S(1)}, bf16[528,768]{1,0:T(8,128)(2,1)S(1)}, u32[]{:S(2)}, u32[]{:S(2)}) collective-permute-start(bf16[528,768]{1,0:T(8,128)(2,1)S(1)} %join_rest.1.refs_6_.weight), channel_id=1, source_target_pairs={{0,4},{1,3},{2,6},{3,1},{4,0},{5,7},{6,2},{7,5},{8,12},{9,11},{10,... | collective-permute-start | bytes 2433032 | tf_op jit(solution)/shard_map/ppermute | solution.py:179
  65.9 12.3 %collective-permute-start.20 = (bf16[528,768]{1,0:T(8,128)(2,1)S(1)}, bf16[528,768]{1,0:T(8,128)(2,1)S(1)}, u32[]{:S(2)}, u32[]{:S(2)}) collective-permute-start(bf16[528,768]{1,0:T(8,128)(2,1)S(1)} %collective-permute-done.17.refs_7_), channel_id=1, source_target_pairs={{0,4},{1,3},{2,6},{3,1},{4,0},{5,7},{6,2},{7,5},{8,12},{9,11},{10,... | collective-permute-start | bytes 2433032 | tf_op jit(solution)/shard_map/ppermute | solution.py:187
  67.0 2.3 %collective-permute-start.19 = (bf16[2,512,384]{2,1,0:T(8,128)(2,1)S(1)}, bf16[2,512,384]{2,1,0:T(8,128)(2,1)S(1)}, u32[]{:S(2)}, u32[]{:S(2)}) collective-permute-start(bf16[2,512,384]{2,1,0:T(8,128)(2,1)S(1)} %get-tuple-element.122.refs_0_), channel_id=1, source_target_pairs={{0,1},{1,0},{2,3},{3,2},{4,5},{5,4},{6,7},{7,6},{8,9},{9,8},{10,11... | collective-permute-start | bytes 2359304 | tf_op jit(solution)/shard_map/ppermute | solution.py:1231
  67.0 11.2 %collective-permute-start.21 = (bf16[528,768]{1,0:T(8,128)(2,1)S(1)}, bf16[528,768]{1,0:T(8,128)(2,1)S(1)}, u32[]{:S(2)}, u32[]{:S(2)}) collective-permute-start(bf16[528,768]{1,0:T(8,128)(2,1)S(1)} %join_rest.1.refs_6_.weight), channel_id=1, source_target_pairs={{0,1},{1,0},{2,3},{3,2},{4,5},{5,4},{6,7},{7,6},{8,9},{9,8},{10,11... | collective-permute-start | bytes 2433032 | tf_op jit(solution)/shard_map/ppermute | solution.py:159
  67.5 10.7 %collective-permute-start.22 = (bf16[528,768]{1,0:T(8,128)(2,1)S(1)}, bf16[528,768]{1,0:T(8,128)(2,1)S(1)}, u32[]{:S(2)}, u32[]{:S(2)}) collective-permute-start(bf16[528,768]{1,0:T(8,128)(2,1)S(1)} %collective-permute-done.17.refs_7_), channel_id=1, source_target_pairs={{0,1},{1,0},{2,3},{3,2},{4,5},{5,4},{6,7},{7,6},{8,9},{9,8},{10,11... | collective-permute-start | bytes 2433032 | tf_op jit(solution)/shard_map/ppermute | solution.py:159
  68.9 9.3 %collective-permute-start.23 = (bf16[528,768]{1,0:T(8,128)(2,1)S(1)}, bf16[528,768]{1,0:T(8,128)(2,1)S(1)}, u32[]{:S(2)}, u32[]{:S(2)}) collective-permute-start(bf16[528,768]{1,0:T(8,128)(2,1)S(1)} %collective-permute-done.18.refs_8_), channel_id=1, source_target_pairs={{0,1},{1,0},{2,3},{3,2},{4,5},{5,4},{6,7},{7,6},{8,9},{9,8},{10,11... | collective-permute-start | bytes 2433032 | tf_op jit(solution)/shard_map/ppermute | solution.py:159
  78.2 2.3 %collective-permute-start.24 = (bf16[528,768]{1,0:T(8,128)(2,1)S(1)}, bf16[528,768]{1,0:T(8,128)(2,1)S(1)}, u32[]{:S(2)}, u32[]{:S(2)}) collective-permute-start(bf16[528,768]{1,0:T(8,128)(2,1)S(1)} %collective-permute-done.20.refs_9_), channel_id=1, source_target_pairs={{0,1},{1,0},{2,3},{3,2},{4,5},{5,4},{6,7},{7,6},{8,9},{9,8},{10,11... | collective-permute-start | bytes 2433032 | tf_op jit(solution)/shard_map/ppermute | solution.py:159
  100.1 5.7 %collective-permute-start.26 = (bf16[2,528,768]{2,1,0:T(8,128)(2,1)}, bf16[2,528,768]{2,1,0:T(8,128)(2,1)S(1)}, u32[]{:S(2)}, u32[]{:S(2)}) collective-permute-start(bf16[2,528,768]{2,1,0:T(8,128)(2,1)} %get-tuple-element.136), channel_id=1, source_target_pairs={{0,1},{1,0},{2,3},{3,2},{4,5},{5,4},{6,7},{7,6},{8,9},{9,8},{10,11... | collective-permute-start | bytes 4866056 | tf_op jit(solution)/shard_map/ppermute | solution.py:159
  100.3 7.1 %collective-permute-start.25 = (bf16[2,528,768]{2,1,0:T(8,128)(2,1)}, bf16[2,528,768]{2,1,0:T(8,128)(2,1)S(1)}, u32[]{:S(2)}, u32[]{:S(2)}) collective-permute-start(bf16[2,528,768]{2,1,0:T(8,128)(2,1)} %get-tuple-element.133), channel_id=1, source_target_pairs={{0,1},{1,0},{2,3},{3,2},{4,5},{5,4},{6,7},{7,6},{8,9},{9,8},{10,11... | collective-permute-start | bytes 4866056 | tf_op jit(solution)/shard_map/ppermute | solution.py:159
  106.2 22.3 %collective-permute-start.28 = (bf16[2,528,768]{2,1,0:T(8,128)(2,1)S(1)}, bf16[2,528,768]{2,1,0:T(8,128)(2,1)S(1)}, u32[]{:S(2)}, u32[]{:S(2)}) collective-permute-start(bf16[2,528,768]{2,1,0:T(8,128)(2,1)S(1)} %add_convert_fusion), channel_id=1, source_target_pairs={{0,4},{1,3},{2,6},{3,1},{4,0},{5,7},{6,2},{7,5},{8,12},{9,11},{10,... | collective-permute-start | bytes 4866056 | tf_op jit(solution)/shard_map/ppermute | solution.py:202
  107.3 9.0 %collective-permute-start.27 = (bf16[2,512,128]{2,1,0:T(8,128)(2,1)S(1)}, bf16[2,512,128]{2,1,0:T(8,128)(2,1)S(1)}, u32[]{:S(2)}, u32[]{:S(2)}) collective-permute-start(bf16[2,512,128]{2,1,0:T(8,128)(2,1)S(1)} %get-tuple-element.139), channel_id=1, source_target_pairs={{0,1},{1,0},{2,3},{3,2},{4,5},{5,4},{6,7},{7,6},{8,9},{9,8},{10,11... | collective-permute-start | bytes 786440 | tf_op jit(solution)/shard_map/ppermute | solution.py:1271
  127.9 3.1 %collective-permute-start.30 = (bf16[2,512,384]{2,1,0:T(8,128)(2,1)S(1)}, bf16[2,512,384]{2,1,0:T(8,128)(2,1)S(1)}, u32[]{:S(2)}, u32[]{:S(2)}) collective-permute-start(bf16[2,512,384]{2,1,0:T(8,128)(2,1)S(1)} %get-tuple-element.151), channel_id=1, source_target_pairs={{0,1},{1,0},{2,3},{3,2},{4,5},{5,4},{6,7},{7,6},{8,9},{9,8},{10,11... | collective-permute-start | bytes 2359304 | tf_op jit(solution)/shard_map/ppermute | solution.py:1271
  128.0 3.0 %collective-permute-start.29 = (bf16[2,512,256]{2,1,0:T(8,128)(2,1)S(1)}, bf16[2,512,256]{2,1,0:T(8,128)(2,1)S(1)}, u32[]{:S(2)}, u32[]{:S(2)}) collective-permute-start(bf16[2,512,256]{2,1,0:T(8,128)(2,1)S(1)} %get-tuple-element.149), channel_id=1, source_target_pairs={{0,1},{1,0},{2,3},{3,2},{4,5},{5,4},{6,7},{7,6},{8,9},{9,8},{10,11... | collective-permute-start | bytes 1572872 | tf_op jit(solution)/shard_map/ppermute | solution.py:1271
  128.9 12.3 %collective-permute-start.31 = (bf16[1,528,768]{2,1,0:T(8,128)(2,1)S(1)}, bf16[1,528,768]{2,1,0:T(8,128)(2,1)S(1)}, u32[]{:S(2)}, u32[]{:S(2)}) collective-permute-start(bf16[1,528,768]{2,1,0:T(8,128)(2,1)S(1)} %get-tuple-element.196), channel_id=1, source_target_pairs={{0,2},{1,5},{2,0},{3,7},{4,6},{5,1},{6,4},{7,3},{8,10},{9,13},{10,... | collective-permute-start | bytes 2433032 | tf_op jit(solution)/shard_map/ppermute | solution.py:202
  137.2 4.3 %collective-permute-start.32 = (bf16[2,96,2304]{2,1,0:T(8,128)(2,1)S(1)}, bf16[2,96,2304]{2,1,0:T(8,128)(2,1)S(1)}, u32[]{:S(2)}, u32[]{:S(2)}) collective-permute-start(bf16[2,96,2304]{2,1,0:T(8,128)(2,1)S(1)} %get-tuple-element.156), channel_id=1, source_target_pairs={{0,1},{1,0},{2,3},{3,2},{4,5},{5,4},{6,7},{7,6},{8,9},{9,8},{10,11... | collective-permute-start | bytes 2654216 | tf_op jit(solution)/shard_map/ppermute | solution.py:159
  137.4 11.1 %collective-permute-start.33 = (bf16[2,96,2304]{2,1,0:T(8,128)(2,1)S(1)}, bf16[2,96,2304]{2,1,0:T(8,128)(2,1)S(1)}, u32[]{:S(2)}, u32[]{:S(2)}) collective-permute-start(bf16[2,96,2304]{2,1,0:T(8,128)(2,1)S(1)} %get-tuple-element.158), channel_id=1, source_target_pairs={{0,1},{1,0},{2,3},{3,2},{4,5},{5,4},{6,7},{7,6},{8,9},{9,8},{10,11... | collective-permute-start | bytes 2654216 | tf_op jit(solution)/shard_map/ppermute | solution.py:159
  141.7 17.1 %collective-permute-start.36 = (bf16[2,96,2304]{2,1,0:T(8,128)(2,1)S(1)}, bf16[2,96,2304]{2,1,0:T(8,128)(2,1)S(1)}, u32[]{:S(2)}, u32[]{:S(2)}) collective-permute-start(bf16[2,96,2304]{2,1,0:T(8,128)(2,1)S(1)} %add_convert_fusion.3), channel_id=1, source_target_pairs={{0,4},{1,3},{2,6},{3,1},{4,0},{5,7},{6,2},{7,5},{8,12},{9,11},{10,... | collective-permute-start | bytes 2654216 | tf_op jit(solution)/shard_map/ppermute | solution.py:202
  143.8 12.5 %collective-permute-start.34 = (bf16[288,384]{1,0:T(8,128)(2,1)S(1)}, bf16[288,384]{1,0:T(8,128)(2,1)S(1)}, u32[]{:S(2)}, u32[]{:S(2)}) collective-permute-start(bf16[288,384]{1,0:T(8,128)(2,1)S(1)} %get-tuple-element.161), channel_id=1, source_target_pairs={{0,8},{8,0},{16,24},{24,16},{1,9},{9,1},{17,25},{25,17},{2,10},{10... | collective-permute-start | bytes 663560 | tf_op jit(solution)/shard_map/ppermute | solution.py:1102
  147.2 11.6 %collective-permute-start.35 = (bf16[288,384]{1,0:T(8,128)(2,1)S(1)}, bf16[288,384]{1,0:T(8,128)(2,1)S(1)}, u32[]{:S(2)}, u32[]{:S(2)}) collective-permute-start(bf16[288,384]{1,0:T(8,128)(2,1)S(1)} %get-tuple-element.162), channel_id=1, source_target_pairs={{0,16},{8,24},{16,0},{24,8},{1,17},{9,25},{17,1},{25,9},{2,18},{10... | collective-permute-start | bytes 663560 | tf_op jit(solution)/shard_map/ppermute | solution.py:1102
  158.9 10.8 %collective-permute-start.37 = (bf16[1,96,2304]{2,1,0:T(8,128)(2,1)S(1)}, bf16[1,96,2304]{2,1,0:T(8,128)(2,1)S(1)}, u32[]{:S(2)}, u32[]{:S(2)}) collective-permute-start(bf16[1,96,2304]{2,1,0:T(8,128)(2,1)S(1)} %add_convert_fusion.9), channel_id=1, source_target_pairs={{0,2},{1,5},{2,0},{3,7},{4,6},{5,1},{6,4},{7,3},{8,10},{9,13},{10,... | collective-permute-start | bytes 1327112 | tf_op jit(solution)/shard_map/ppermute | solution.py:202
  160.0 9.8 %collective-permute-start.38 = (bf16[288,384]{1,0:T(8,128)(2,1)S(1)}, bf16[288,384]{1,0:T(8,128)(2,1)S(1)}, u32[]{:S(2)}, u32[]{:S(2)}) collective-permute-start(bf16[288,384]{1,0:T(8,128)(2,1)S(1)} %get-tuple-element.163), channel_id=1, source_target_pairs={{0,24},{8,16},{16,8},{24,0},{1,25},{9,17},{17,9},{25,1},{2,26},{10... | collective-permute-start | bytes 663560 | tf_op jit(solution)/shard_map/ppermute | solution.py:1102
  162.6 12.9 %collective-permute-start.40 = (bf16[2,128,768]{2,1,0:T(8,128)(2,1)S(1)}, bf16[2,128,768]{2,1,0:T(8,128)(2,1)S(1)}, u32[]{:S(2)}, u32[]{:S(2)}) collective-permute-start(bf16[2,128,768]{2,1,0:T(8,128)(2,1)S(1)} %get-tuple-element.182), channel_id=1, source_target_pairs={{0,4},{1,5},{2,6},{3,7},{4,0},{5,1},{6,2},{7,3},{8,12},{9,13},{10,... | collective-permute-start | bytes 1179656 | tf_op jit(solution)/shard_map/ppermute | solution.py:172
  163.7 15.1 %collective-permute-start.39 = (bf16[2,128,768]{2,1,0:T(8,128)(2,1)S(1)}, bf16[2,128,768]{2,1,0:T(8,128)(2,1)S(1)}, u32[]{:S(2)}, u32[]{:S(2)}) collective-permute-start(bf16[2,128,768]{2,1,0:T(8,128)(2,1)S(1)} %get-tuple-element.180), channel_id=1, source_target_pairs={{0,2},{1,3},{2,0},{3,1},{4,6},{5,7},{6,4},{7,5},{8,10},{9,11},{10,... | collective-permute-start | bytes 1179656 | tf_op jit(solution)/shard_map/ppermute | solution.py:172
  170.7 14.0 %collective-permute-start.42 = (bf16[96,640]{1,0:T(8,128)(2,1)S(1)}, bf16[96,640]{1,0:T(8,128)(2,1)S(1)}, u32[]{:S(2)}, u32[]{:S(2)}) collective-permute-start(bf16[96,640]{1,0:T(8,128)(2,1)S(1)} %get-tuple-element.175), channel_id=1, source_target_pairs={{0,8},{8,0},{16,24},{24,16},{1,9},{9,1},{17,25},{25,17},{2,10},{10... | collective-permute-start | bytes 368648 | tf_op jit(solution)/shard_map/ppermute | solution.py:1102
  172.0 12.7 %collective-permute-start.43 = (bf16[96,640]{1,0:T(8,128)(2,1)S(1)}, bf16[96,640]{1,0:T(8,128)(2,1)S(1)}, u32[]{:S(2)}, u32[]{:S(2)}) collective-permute-start(bf16[96,640]{1,0:T(8,128)(2,1)S(1)} %get-tuple-element.176), channel_id=1, source_target_pairs={{0,16},{8,24},{16,0},{24,8},{1,17},{9,25},{17,1},{25,9},{2,18},{10... | collective-permute-start | bytes 368648 | tf_op jit(solution)/shard_map/ppermute | solution.py:1102
  172.7 10.2 %collective-permute-start.41 = (bf16[2,128,768]{2,1,0:T(8,128)(2,1)S(1)}, bf16[2,128,768]{2,1,0:T(8,128)(2,1)S(1)}, u32[]{:S(2)}, u32[]{:S(2)}) collective-permute-start(bf16[2,128,768]{2,1,0:T(8,128)(2,1)S(1)} %get-tuple-element.185), channel_id=1, source_target_pairs={{0,6},{1,7},{2,4},{3,5},{4,2},{5,3},{6,0},{7,1},{8,14},{9,15},{10,... | collective-permute-start | bytes 1179656 | tf_op jit(solution)/shard_map/ppermute | solution.py:172
  175.5 9.2 %collective-permute-start.44 = (bf16[96,640]{1,0:T(8,128)(2,1)S(1)}, bf16[96,640]{1,0:T(8,128)(2,1)S(1)}, u32[]{:S(2)}, u32[]{:S(2)}) collective-permute-start(bf16[96,640]{1,0:T(8,128)(2,1)S(1)} %get-tuple-element.177), channel_id=1, source_target_pairs={{0,24},{8,16},{16,8},{24,0},{1,25},{9,17},{17,9},{25,1},{2,26},{10... | collective-permute-start | bytes 368648 | tf_op jit(solution)/shard_map/ppermute | solution.py:1102
  (50 other events, 375.2 us)
